TPU v7x, 1024 devices: a whole 4x8x16 slice. The times are simulated.
1024 devices in a mesh: dp: 128 (over y_lo, x, z), tensor: 8 (over y_hi, core).
Axes of the slice: x: 4, y: 8 (y_hi: 4, y_lo: 2; y = y_hi * 2 + y_lo), z: 16, core: 2. Of those that a mesh axis runs over, the one named last changes fastest.
Arguments:
- attn: bfloat16 [16384, 3072], P('dp', 'tensor'), may hold values from -6 to 6
- weight: bfloat16 [2560, 3072], P(None, 'tensor'), may hold values from -0.109375 to 0.109375
- d_out: bfloat16 [16384, 2560], P(('dp', 'tensor')), may hold values from -24 to 24
Outputs:
- mixed: bfloat16 [16384, 2560], P(('dp', 'tensor'))
- d_attn: bfloat16 [16384, 3072], P('dp', 'tensor')
- w_grad: float32 [2560, 3072], P('dp', 'tensor')
All inputs are finite; a program needn't handle non-finite values. Where the computation divides by a largest or mean magnitude, that divisor is 1e-20 or more.
Results may differ from a plain program's by a relative error of at most 0.035.
The roundings to bfloat16 on the way count: a program that leaves them out, or rounds other values in their place, can miss the bound.
Values may be sent and summed in bfloat16 or wider, within the bound.
No kernel may reach another device: no remote copies, remote signals or barrier semaphores. Data moves between devices by JAX's collectives and lax.ppermute only.
A program may use at most 32 MiB of HBM per device.

v0:
```python
import jax
import jax.numpy as jnp
from jax import lax
from jax.sharding import PartitionSpec as P

BLK = 128


code_offset = 6.0


def hadamard(size):
    rows = lax.broadcasted_iota(jnp.int32, (size, size), 0)
    cols = lax.broadcasted_iota(jnp.int32, (size, size), 1)
    common = jnp.bitwise_and(rows, cols)
    parity = jnp.zeros((size, size), jnp.int32)
    for place in range(size.bit_length() - 1):
        parity = parity + jnp.bitwise_and(jnp.right_shift(common, place), 1)
    signs = (1 - 2 * (parity % 2)).astype(jnp.float32)
    return signs / jnp.sqrt(jnp.float32(size))


def rotate(field, table):
    count = field.shape[0]
    blocks = field.reshape(count, -1, BLK)
    turned = jnp.einsum("rkb,bc->rkc", blocks, table, precision=lax.Precision.HIGHEST)
    return turned.reshape(count, -1)


def body(attn, weight, d_out):
    table = hadamard(BLK)
    count = attn.shape[0]
    features = weight.shape[0]
    partial_value = lax.dot_general(
        attn, weight, (((1,), (1,)), ((), ())), preferred_element_type=jnp.float32
    )
    blocks = rotate(partial_value, table).reshape(count, -1, BLK)
    scale = (jnp.max(jnp.abs(blocks), axis=2) + 1e-06).astype(jnp.bfloat16)
    coded = (blocks / scale.astype(jnp.float32)[:, :, None] + code_offset).astype(jnp.bfloat16)
    kept = lax.optimization_barrier(coded)
    values = (
        (kept.astype(jnp.float32) - code_offset) * scale.astype(jnp.float32)[:, :, None]
    ).reshape(count, features)
    total = lax.psum_scatter(
        values.astype(jnp.bfloat16), "tensor", scatter_dimension=0, tiled=True
    ).astype(jnp.float32)
    mixed = rotate(total, table).astype(jnp.bfloat16)
    full_grad = lax.all_gather(d_out, "tensor", axis=0, tiled=True)
    d_attn = jnp.dot(full_grad, weight, preferred_element_type=jnp.float32).astype(jnp.bfloat16)
    w_grad = lax.psum_scatter(
        lax.dot_general(
            full_grad, attn, (((0,), (0,)), ((), ())), preferred_element_type=jnp.float32
        ),
        "dp",
        scatter_dimension=0,
        tiled=True,
    )
    return (mixed, d_attn, w_grad)


def solution(mesh):
    in_specs = (P("dp", "tensor"), P(None, "tensor"), P(("dp", "tensor"), None))
    out_specs = (P(("dp", "tensor"), None), P("dp", "tensor"), P("dp", "tensor"))
    return jax.shard_map(body, mesh=mesh, in_specs=in_specs, out_specs=out_specs, check_vma=False)
```

profile of v0, /device:TPU:40, one launch (start us, length us, event | category | flops | bytes accessed | tf_op | source)
XLA Modules:
  0.0 1258.7 jit_solution(8813563517174217373)
XLA Ops:
  8.0 0.0 copy-start
  8.0 0.0 reduce-scatter.2.cloned.1.call-start
  8.1 1.5 copy-done
  9.5 1.6 fusion.42
  11.1 1.4 abs_reduce_fusion
  12.5 0.2 add_convert_fusion
  12.7 0.2 multiply_convert_fusion
  12.9 0.0 copy-start.2
  12.9 0.0 copy-start.1
  12.9 1.1 copy.16
  14.1 0.0 reduce-scatter.2.cloned.1.call-update
  14.1 0.0 all-reduce.3.cloned.1.call-start
  14.2 0.0 copy-done.2
  14.2 15.1 %all_gather.3 = bf16[128,2560]{1,0:T(8,128)(2,1)S(1)} all-gather(bf16[16,2560]{1,0:T(8,128)(2,1)S(1)} %copy-done.2), channel_id=1, replica_groups=mesh['dp'=128,'tensor'=8] {'tensor'}, dimensions={0}, use_global_device_ids=true | all-gather | bytes 737280 | tf_op jit(solution)/shard_map/all_gather | solution.py:48
  29.3 2.6 fusion.43
  31.9 0.0 all-reduce.3.cloned.1.call-update
  31.9 1.3 dynamic-slice
  33.9 1.2 convolution_convert_fusion
  35.0 30.3 %reduce-scatter.2.cloned.1.call-done = bf16[16,2560]{1,0:T(8,128)(2,1)} async-done(((bf16[128,2560]{1,0:T(8,128)(2,1)}), bf16[16,2560]{1,0:T(8,128)(2,1)}) %reduce-scatter.2.cloned.1.call-update) | async-done | bytes 81936 | tf_op jit(solution)/shard_map/reduce_scatter | solution.py:44
  65.3 1.0 reshape.22
  66.3 0.3 convolution_convert_fusion.1
  66.6 0.6 copy.23
  67.3 1182.6 %all-reduce.3.cloned.1.call-done = f32[2560,384]{1,0:T(8,128)} async-done(((f32[2560,384]{1,0:T(8,128)}), f32[2560,384]{1,0:T(8,128)}) %all-reduce.3.cloned.1.call-update) | async-done | bytes 3932176
  1249.8 1.4 constant_dynamic-slice_fusion
  (2 shorter events, 0.0 us)
Async XLA Ops:
  8.0 1.6 copy-start
  8.0 57.3 %reduce-scatter.2.cloned.1.call-start = ((), (), s32[]{:S(2)}) async-start(), calls=%async_computation.1 | async-start | bytes 737280 | tf_op jit(solution)/shard_map/reduce_scatter | solution.py:44
  12.9 1.2 copy-start.2
  12.9 16.4 %copy-start.1 = (bf16[128,384]{1,0:T(8,128)(2,1)S(1)}, bf16[128,384]{1,0:T(8,128)(2,1)}, u32[]{:S(2)}) copy-start(bf16[128,384]{1,0:T(8,128)(2,1)} %param.3) | copy-start | bytes 294916
  14.1 1235.7 %all-reduce.3.cloned.1.call-start = ((), (), s32[]{:S(2)}) async-start(), calls=%async_computation.2 | async-start | bytes 7864320
Sparse Core Ops, SparseCore 0:
  14.2 51.0 reduce-scatter.1
Sparse Core Ops, SparseCore 1:
  32.0 1217.8 all-reduce.2
where the time goes:
time: 1260 us
  waiting for transfers between devices  1210 us (96%)
  between operations  16.2 us (1%)
  blocking collectives  15.1 us (1%)
    unnamed x3, waiting for transfers between devices  1180 us
    reduce_scatter x1, waiting for transfers between devices, body(): lax.psum_scatter(values.astype(jnp.bfloat16), 'tensor', scatter_dimension...  30.3 us
  transfers between devices with their start and end apart: 2, of which 2 were waited for; matrix products, arithmetic and copies ran while one was open for 1% of the time, Pallas kernels for 0%

commit v1 on v0

--- a/solution.py
+++ b/solution.py
@@ -1,10 +1,13 @@
 import jax
 import jax.numpy as jnp
 from jax import lax
+from jax.sharding import Mesh
 from jax.sharding import PartitionSpec as P
 
 BLK = 128
-
+TENSOR = ("yh", "core")
+NEAR = ("yl", "x")
+FAR = "z"
 
 code_offset = 6.0
 
@@ -30,7 +33,7 @@
 def body(attn, weight, d_out):
     table = hadamard(BLK)
     count = attn.shape[0]
-    features = weight.shape[0]
+    features, width = weight.shape
     partial_value = lax.dot_general(
         attn, weight, (((1,), (1,)), ((), ())), preferred_element_type=jnp.float32
     )
@@ -42,23 +45,28 @@
         (kept.astype(jnp.float32) - code_offset) * scale.astype(jnp.float32)[:, :, None]
     ).reshape(count, features)
     total = lax.psum_scatter(
-        values.astype(jnp.bfloat16), "tensor", scatter_dimension=0, tiled=True
+        values.astype(jnp.bfloat16), TENSOR, scatter_dimension=0, tiled=True
     ).astype(jnp.float32)
     mixed = rotate(total, table).astype(jnp.bfloat16)
-    full_grad = lax.all_gather(d_out, "tensor", axis=0, tiled=True)
+
+    full_grad = lax.all_gather(d_out, TENSOR, axis=0, tiled=True)
     d_attn = jnp.dot(full_grad, weight, preferred_element_type=jnp.float32).astype(jnp.bfloat16)
-    w_grad = lax.psum_scatter(
-        lax.dot_general(
-            full_grad, attn, (((0,), (0,)), ((), ())), preferred_element_type=jnp.float32
-        ),
-        "dp",
-        scatter_dimension=0,
-        tiled=True,
-    )
+
+    term = lax.dot_general(
+        full_grad, attn, (((0,), (0,)), ((), ())), preferred_element_type=jnp.float32
+    ).astype(jnp.bfloat16)
+    near = lax.axis_size(NEAR)
+    pieces = lax.all_to_all(term.reshape(near, features // near, width), NEAR, 0, 0)
+    plane = jnp.sum(pieces.astype(jnp.float32), axis=0).astype(jnp.bfloat16)
+    far = lax.axis_size(FAR)
+    pieces = lax.all_to_all(plane.reshape(far, features // near // far, width), FAR, 0, 0)
+    w_grad = jnp.sum(pieces.astype(jnp.float32), axis=0)
     return (mixed, d_attn, w_grad)
 
 
 def solution(mesh):
-    in_specs = (P("dp", "tensor"), P(None, "tensor"), P(("dp", "tensor"), None))
-    out_specs = (P(("dp", "tensor"), None), P("dp", "tensor"), P("dp", "tensor"))
-    return jax.shard_map(body, mesh=mesh, in_specs=in_specs, out_specs=out_specs, check_vma=False)
+    fine = Mesh(mesh.devices.reshape(2, 4, 16, 4, 2), ("yl", "x", "z", "yh", "core"))
+    dp = ("yl", "x", "z")
+    in_specs = (P(dp, TENSOR), P(None, TENSOR), P(dp + TENSOR, None))
+    out_specs = (P(dp + TENSOR, None), P(dp, TENSOR), P(dp, TENSOR))
+    return jax.shard_map(body, mesh=fine, in_specs=in_specs, out_specs=out_specs, check_vma=False)

time: 1260 us -> 107 us (0.08)
  the two profiles are of different devices: /device:TPU:40 before, /device:TPU:8 now
where the time goes in v1:
time: 107 us; the launch traced here: 106 us
  waiting for transfers between devices  37.5 us (35%)
  starting transfers between devices  24.7 us (23%)
  blocking collectives  17.3 us (16%)
  between operations  14.1 us (13%)
  matrix products  6.41 us (6%)
  local copies, waits for them, and re-layouts  3.45 us (3%)
  other arithmetic  2.93 us (3%)
    all_to_all x1, waiting for transfers between devices, body(): lax.all_to_all(term.reshape(near, features // near, width), NEAR, 0, 0)  21.4 us
    all_gather x1, blocking collectives, body(): full_grad = lax.all_gather(d_out, TENSOR, axis=0, tiled=True)  17.3 us
    all_to_all x1, starting transfers between devices, body(): lax.all_to_all(term.reshape(near, features // near, width), NEAR, 0, 0)  15.6 us
    all_to_all x1, starting transfers between devices, body(): lax.all_to_all(plane.reshape(far, features // near // far, width), FAR, 0...  9.16 us
    all_to_all x1, waiting for transfers between devices, body(): lax.all_to_all(plane.reshape(far, features // near // far, width), FAR, 0...  8.92 us
    reduce_scatter x1, waiting for transfers between devices, body(): lax.psum_scatter(values.astype(jnp.bfloat16), TENSOR, scatter_dimension=0...  7.21 us
    dot_general x1, matrix products, body(): lax.dot_general(full_grad, attn, (((0,), (0,)), ((), ())), preferred_elem...  2.87 us
  transfers between devices with their start and end apart: 3, of which 3 were waited for; matrix products, arithmetic and copies ran while one was open for 9% of the time, Pallas kernels for 0%

profile of v1, /device:TPU:8, one launch (start us, length us, event | category | flops | bytes accessed | tf_op | source)
XLA Modules:
  0.0 106.4 jit_solution(7051762435038324077)
XLA Ops:
  7.2 0.0 copy-start
  7.2 17.3 %all_gather.3 = bf16[128,2560]{1,0:T(8,128)(2,1)S(1)} all-gather(bf16[16,2560]{1,0:T(8,128)(2,1)} %param.5), channel_id=1, replica_groups=mesh['yl'=2,'x'=4,'z'=16,'yh'=4,'core'=2] {'yh','core'}, dimensions={0}, use_global_device_ids=true | all-gather | bytes 737280 | tf_op jit(solution)/shard_map/all_gather | solution.py:52
  24.5 2.9 %convolution_convert_fusion = bf16[2560,384]{1,0:T(8,128)(2,1)} fusion(bf16[128,2560]{1,0:T(8,128)(2,1)S(1)} %all_gather.3, bf16[128,384]{1,0:T(8,128)(2,1)} %param.3), kind=kOutput, calls=%fused_computation | convolution fusion | flops 252641280 | bytes 2719744 | tf_op jit(solution)/shard_map/dot_general | solution.py:55
  27.3 15.6 %all-to-all-start = ((bf16[8,320,384]{2,1,0:T(8,128)(2,1)}), bf16[8,320,384]{2,1,0:T(8,128)(2,1)}, u32[]{:S(2)}, u32[]{:S(2)}) async-start(bf16[8,320,384]{2,1,0:T(8,128)(2,1)} %bitcast.22), calls=%async_computation.1 | async-start | bytes 3932160 | tf_op jit(solution)/shard_map/all_to_all | solution.py:59
  42.9 0.0 reduce-scatter.2.cloned.1.call-start
  42.9 0.0 copy-done
  42.9 0.0 copy-done.1
  42.9 0.7 fusion.42
  43.6 1.4 %abs_reduce_fusion = (f32[128,20]{0,1:T(8,128)S(1)}, f32[128,20,128]{0,2,1:T(8,128)S(1)}) fusion(f32[128,20,128]{0,2,1:T(8,128)S(1)} %bitcast.23), kind=kOutput, calls=%fused_computation.3 | convolution fusion | flops 504559104 | bytes 2631680 | tf_op jit(solution)/shard_map/rkb,bc->rkc/dot_general | solution.py:29
  45.0 0.2 add_convert_fusion
  45.2 0.2 multiply_convert_fusion
  45.4 1.1 %copy.12 = bf16[128,2560]{1,0:T(8,128)(2,1)} copy(bf16[128,2560]{0,1:T(8,128)(2,1)S(1)} %bitcast.24) | data formatting | bytes 1310720 | tf_op jit(solution)/shard_map/convert_element_type | solution.py:48
  46.5 0.0 reduce-scatter.2.cloned.1.call-update
  46.5 21.4 %all-to-all-done = bf16[8,320,384]{2,1,0:T(8,128)(2,1)} async-done(((bf16[8,320,384]{2,1,0:T(8,128)(2,1)}), bf16[8,320,384]{2,1,0:T(8,128)(2,1)}, u32[]{:S(2)}, u32[]{:S(2)}) %all-to-all-start) | async-done | bytes 1966112 | tf_op jit(solution)/shard_map/all_to_all | solution.py:59
  67.9 1.9 %reduce_sum.21 = bf16[320,384]{1,0:T(8,128)(2,1)S(1)} reduce(bf16[8,320,384]{2,1,0:T(8,128)(2,1)} %all-to-all-done, bf16[]{:T(256)} %constant.39.clone.1), dimensions={0}, to_apply=%region_2.3 | reduce | flops 860160 | bytes 2211842 | tf_op jit(solution)/shard_map/reduce_sum | solution.py:60
  69.8 0.8 reshape.30
  70.5 9.2 %all-to-all-start.1 = ((bf16[16,20,384]{2,1,0:T(8,128)(2,1)}), bf16[16,20,384]{2,1,0:T(8,128)(2,1)S(1)}, u32[]{:S(2)}, u32[]{:S(2)}) async-start(bf16[16,20,384]{2,1,0:T(8,128)(2,1)} %reshape.30), calls=%async_computation.2 | async-start | bytes 589824 | tf_op jit(solution)/shard_map/all_to_all | solution.py:62
  79.7 1.2 %convolution_convert_fusion.1 = bf16[128,384]{1,0:T(8,128)(2,1)} fusion(bf16[128,2560]{1,0:T(8,128)(2,1)S(1)} %all_gather.3, bf16[2560,384]{1,0:T(8,128)(2,1)S(1)} %copy-done), kind=kOutput, calls=%fused_computation.4 | convolution fusion | flops 251707392 | bytes 2719744 | tf_op jit(solution)/shard_map/dot_general | solution.py:53
  80.9 7.2 %reduce-scatter.2.cloned.1.call-done = bf16[16,2560]{1,0:T(8,128)(2,1)} async-done(((bf16[128,2560]{1,0:T(8,128)(2,1)}), bf16[16,2560]{1,0:T(8,128)(2,1)}) %reduce-scatter.2.cloned.1.call-update) | async-done | bytes 81936 | tf_op jit(solution)/shard_map/reduce_scatter | solution.py:47
  88.1 1.0 reshape.28
  89.0 0.3 convolution_convert_fusion.2
  89.3 0.6 copy.19
  90.0 8.9 %all-to-all-done.1 = bf16[16,20,384]{2,1,0:T(8,128)(2,1)S(1)} async-done(((bf16[16,20,384]{2,1,0:T(8,128)(2,1)}), bf16[16,20,384]{2,1,0:T(8,128)(2,1)S(1)}, u32[]{:S(2)}, u32[]{:S(2)}) %all-to-all-start.1) | async-done | bytes 245792 | tf_op jit(solution)/shard_map/all_to_all | solution.py:62
  98.9 0.7 convert_reduce_fusion
  (2 shorter events, 0.0 us)
Async XLA Ops:
  7.2 35.7 %copy-start = (bf16[2560,384]{1,0:T(8,128)(2,1)S(1)}, bf16[2560,384]{1,0:T(8,128)(2,1)}, u32[]{:S(2)}) copy-start(bf16[2560,384]{1,0:T(8,128)(2,1)} %param.4) | copy-start | bytes 5898244
  27.3 15.6 %copy-start.1 = (bf16[128,384]{1,0:T(8,128)(2,1)S(1)}, bf16[128,384]{1,0:T(8,128)(2,1)}, u32[]{:S(2)}) copy-start(bf16[128,384]{1,0:T(8,128)(2,1)} %param.3) | copy-start | bytes 294916
  27.3 40.5 %all-to-all-start = ((bf16[8,320,384]{2,1,0:T(8,128)(2,1)}), bf16[8,320,384]{2,1,0:T(8,128)(2,1)}, u32[]{:S(2)}, u32[]{:S(2)}) async-start(bf16[8,320,384]{2,1,0:T(8,128)(2,1)} %bitcast.22), calls=%async_computation.1 | async-start | bytes 3932160 | tf_op jit(solution)/shard_map/all_to_all | solution.py:59
  42.9 45.2 %reduce-scatter.2.cloned.1.call-start = ((), (), s32[]{:S(2)}) async-start(), calls=%async_computation.3 | async-start | bytes 737280 | tf_op jit(solution)/shard_map/reduce_scatter | solution.py:47
  70.5 28.4 %all-to-all-start.1 = ((bf16[16,20,384]{2,1,0:T(8,128)(2,1)}), bf16[16,20,384]{2,1,0:T(8,128)(2,1)S(1)}, u32[]{:S(2)}, u32[]{:S(2)}) async-start(bf16[16,20,384]{2,1,0:T(8,128)(2,1)} %reshape.30), calls=%async_computation.2 | async-start | bytes 589824 | tf_op jit(solution)/shard_map/all_to_all | solution.py:62
Sparse Core Ops, SparseCore 0:
  47.1 40.9 reduce-scatter.1

commit v2 on v1

--- a/solution.py
+++ b/solution.py
@@ -1,3 +1,5 @@
+import functools
+
 import jax
 import jax.numpy as jnp
 from jax import lax
@@ -30,10 +32,8 @@
     return turned.reshape(count, -1)
 
 
-def body(attn, weight, d_out):
-    table = hadamard(BLK)
-    count = attn.shape[0]
-    features, width = weight.shape
+def coded_values(attn, weight, table):
+    count, features = attn.shape[0], weight.shape[0]
     partial_value = lax.dot_general(
         attn, weight, (((1,), (1,)), ((), ())), preferred_element_type=jnp.float32
     )
@@ -41,26 +41,46 @@
     scale = (jnp.max(jnp.abs(blocks), axis=2) + 1e-06).astype(jnp.bfloat16)
     coded = (blocks / scale.astype(jnp.float32)[:, :, None] + code_offset).astype(jnp.bfloat16)
     kept = lax.optimization_barrier(coded)
-    values = (
-        (kept.astype(jnp.float32) - code_offset) * scale.astype(jnp.float32)[:, :, None]
-    ).reshape(count, features)
-    total = lax.psum_scatter(
-        values.astype(jnp.bfloat16), TENSOR, scatter_dimension=0, tiled=True
-    ).astype(jnp.float32)
-    mixed = rotate(total, table).astype(jnp.bfloat16)
+    values = (kept.astype(jnp.float32) - code_offset) * scale.astype(jnp.float32)[:, :, None]
+    return values.reshape(count, features).astype(jnp.bfloat16)
 
+
+def scatter_sum(values):
+    count, features = values.shape
+    tall, cores = lax.axis_size("yh"), lax.axis_size("core")
+    me, mine = lax.axis_index("yh"), lax.axis_index("core")
+    view = values.reshape(tall, cores, count // tall // cores, features)
+    pick = functools.partial(lax.dynamic_index_in_dim, keepdims=False)
+    arrived = lax.ppermute(pick(view, 1 - mine, 1), "core", [(0, 1), (1, 0)])
+    pair = pick(view, mine, 1).astype(jnp.float32) + arrived.astype(jnp.float32)
+    sent = pair.astype(jnp.bfloat16)
+    total = pick(pair, me, 0)
+    for step in range(1, tall):
+        block = pick(sent, lax.rem(me + step, tall), 0)
+        arrived = lax.ppermute(block, "yh", [(i, (i + step) % tall) for i in range(tall)])
+        total = total + arrived.astype(jnp.float32)
+    return total
+
+
+def body(attn, weight, d_out):
+    table = hadamard(BLK)
+    features, width = weight.shape
     full_grad = lax.all_gather(d_out, TENSOR, axis=0, tiled=True)
-    d_attn = jnp.dot(full_grad, weight, preferred_element_type=jnp.float32).astype(jnp.bfloat16)
 
     term = lax.dot_general(
         full_grad, attn, (((0,), (0,)), ((), ())), preferred_element_type=jnp.float32
     ).astype(jnp.bfloat16)
     near = lax.axis_size(NEAR)
     pieces = lax.all_to_all(term.reshape(near, features // near, width), NEAR, 0, 0)
+    pieces, attn, full_grad = lax.optimization_barrier((pieces, attn, full_grad))
     plane = jnp.sum(pieces.astype(jnp.float32), axis=0).astype(jnp.bfloat16)
     far = lax.axis_size(FAR)
     pieces = lax.all_to_all(plane.reshape(far, features // near // far, width), FAR, 0, 0)
     w_grad = jnp.sum(pieces.astype(jnp.float32), axis=0)
+
+    total = scatter_sum(coded_values(attn, weight, table))
+    mixed = rotate(total, table).astype(jnp.bfloat16)
+    d_attn = jnp.dot(full_grad, weight, preferred_element_type=jnp.float32).astype(jnp.bfloat16)
     return (mixed, d_attn, w_grad)
 
 

time: 107 us -> 108 us (level)
  the two profiles are of different devices: /device:TPU:8 before, /device:TPU:1 now
where the time goes in v2:
time: 108 us; the launch traced here: 107 us
  waiting for transfers between devices  30.1 us (28%)
  blocking collectives  29.4 us (27%)
  starting transfers between devices  28.6 us (26%)
  matrix products  6.45 us (6%)
  local copies, waits for them, and re-layouts  5.93 us (5%)
  other arithmetic  5.88 us (5%)
    all_gather x1, blocking collectives, body(): full_grad = lax.all_gather(d_out, TENSOR, axis=0, tiled=True)  29.4 us
    all_to_all x1, waiting for transfers between devices, body(): lax.all_to_all(term.reshape(near, features // near, width), NEAR, 0, 0)  24.8 us
    ppermute x3, starting transfers between devices, scatter_sum(): lax.ppermute(block, 'yh', [(i, (i + step) % tall) for i in range(tall)])  12.6 us
    all_to_all x1, starting transfers between devices, body(): lax.all_to_all(plane.reshape(far, features // near // far, width), FAR, 0...  8.91 us
    ppermute x3, waiting for transfers between devices, scatter_sum(): lax.ppermute(block, 'yh', [(i, (i + step) % tall) for i in range(tall)])  5.27 us
    all_to_all x1, starting transfers between devices, body(): lax.all_to_all(term.reshape(near, features // near, width), NEAR, 0, 0)  4.46 us
    dot_general x1, matrix products, body(): lax.dot_general(full_grad, attn, (((0,), (0,)), ((), ())), preferred_elem...  2.84 us
    convert_element_type x2, local copies, waits for them, and re-layouts, coded_values(): return values.reshape(count, features).astype(jnp.bfloat16)  2.7 us
  transfers between devices with their start and end apart: 6, of which 2 were waited for; matrix products, arithmetic and copies ran while one was open for 6% of the time, Pallas kernels for 0%

profile of v2, /device:TPU:1, one launch (start us, length us, event | category | flops | bytes accessed | tf_op | source)
XLA Modules:
  0.0 107.2 jit_solution(9793514660637781635)
XLA Ops:
  0.6 29.4 %all_gather.3 = bf16[128,2560]{1,0:T(8,128)(2,1)S(1)} all-gather(bf16[16,2560]{1,0:T(8,128)(2,1)} %param.5), channel_id=1, replica_groups=mesh['yl'=2,'x'=4,'z'=16,'yh'=4,'core'=2] {'yh','core'}, dimensions={0}, use_global_device_ids=true | all-gather | bytes 737280 | tf_op jit(solution)/shard_map/all_gather | solution.py:68
  30.0 2.8 %convolution_convert_fusion = bf16[2560,384]{1,0:T(8,128)(2,1)} fusion(bf16[128,2560]{1,0:T(8,128)(2,1)S(1)} %all_gather.3, bf16[128,384]{1,0:T(8,128)(2,1)} %param.3), kind=kOutput, calls=%fused_computation | convolution fusion | flops 252641280 | bytes 2719744 | tf_op jit(solution)/shard_map/dot_general | solution.py:70
  32.9 4.5 %all-to-all-start = ((bf16[8,320,384]{2,1,0:T(8,128)(2,1)}), bf16[8,320,384]{2,1,0:T(8,128)(2,1)}, u32[]{:S(2)}, u32[]{:S(2)}) async-start(bf16[8,320,384]{2,1,0:T(8,128)(2,1)} %bitcast.39), calls=%async_computation | async-start | bytes 3932160 | tf_op jit(solution)/shard_map/all_to_all | solution.py:74
  37.3 24.8 %all-to-all-done = bf16[8,320,384]{2,1,0:T(8,128)(2,1)} async-done(((bf16[8,320,384]{2,1,0:T(8,128)(2,1)}), bf16[8,320,384]{2,1,0:T(8,128)(2,1)}, u32[]{:S(2)}, u32[]{:S(2)}) %all-to-all-start) | async-done | bytes 1966112 | tf_op jit(solution)/shard_map/all_to_all | solution.py:74
  62.2 0.7 fusion.45
  62.9 1.4 %abs_reduce_fusion = (f32[128,20]{0,1:T(8,128)S(1)}, f32[128,20,128]{0,2,1:T(8,128)S(1)}) fusion(f32[128,20,128]{0,2,1:T(8,128)S(1)} %bitcast.40), kind=kOutput, calls=%fused_computation.3 | convolution fusion | flops 504559104 | bytes 2631680 | tf_op jit(solution)/shard_map/rkb,bc->rkc/dot_general | solution.py:31
  64.3 0.2 add_convert_fusion
  64.4 1.0 multiply_convert_fusion
  65.5 1.5 %copy.11 = bf16[128,20,128]{2,1,0:T(8,128)(2,1)S(1)} copy(bf16[128,20,128]{0,2,1:T(8,128)(2,1)} %multiply_convert_fusion) | data formatting | bytes 1310720 | tf_op jit(solution)/shard_map/convert_element_type | solution.py:45
  67.0 1.2 %convert_element_type.78 = bf16[4,2,16,2560]{3,2,1,0:T(8,128)(2,1)} reshape(bf16[128,20,128]{2,1,0:T(8,128)(2,1)S(1)} %copy.11) | data formatting | bytes 1310720 | tf_op jit(solution)/shard_map/convert_element_type | solution.py:45
  68.2 1.7 %dynamic-slice_bitcast_fusion = bf16[4,16,2560]{2,1,0:T(8,128)(2,1)} fusion(bf16[4,2,16,2560]{3,2,1,0:T(8,128)(2,1)} %convert_element_type.78, s32[]{:T(128)S(6)} %select_n.32), kind=kLoop, calls=%fused_computation.8 | loop fusion | bytes 655364 | tf_op jit(solution)/shard_map/jit(dynamic_index_in_dim)/squeeze | solution.py:54
  69.9 2.6 %collective-permute-start = (bf16[4,16,2560]{2,1,0:T(8,128)(2,1)}, bf16[4,16,2560]{2,1,0:T(8,128)(2,1)}, u32[]{:S(2)}, u32[]{:S(2)}) collective-permute-start(bf16[4,16,2560]{2,1,0:T(8,128)(2,1)} %dynamic-slice_bitcast_fusion), channel_id=1, source_target_pairs={{0,1},{1,0},{2,3},{3,2},{4,5},{5,4},{6,7},{7,6},{8,9},{9,8},{10,11... | collective-permute-start | bytes 983048 | tf_op jit(solution)/shard_map/ppermute | solution.py:54
  72.6 2.0 %reduce_sum.21 = bf16[320,384]{1,0:T(8,128)(2,1)S(1)} reduce(bf16[8,320,384]{2,1,0:T(8,128)(2,1)} %all-to-all-done, bf16[]{:T(256)} %constant.75.clone.1), dimensions={0}, to_apply=%region_1.2 | reduce | flops 860160 | bytes 2211842 | tf_op jit(solution)/shard_map/reduce_sum | solution.py:76
  74.6 0.8 reshape.34
  75.3 8.9 %all-to-all-start.1 = ((bf16[16,20,384]{2,1,0:T(8,128)(2,1)}), bf16[16,20,384]{2,1,0:T(8,128)(2,1)}, u32[]{:S(2)}, u32[]{:S(2)}) async-start(bf16[16,20,384]{2,1,0:T(8,128)(2,1)} %reshape.34), calls=%async_computation.1 | async-start | bytes 589824 | tf_op jit(solution)/shard_map/all_to_all | solution.py:78
  84.3 1.1 fusion.44
  85.4 2.6 %collective-permute-start.1 = (bf16[16,2560]{1,0:T(8,128)(2,1)S(1)}, bf16[16,2560]{1,0:T(8,128)(2,1)S(1)}, u32[]{:S(2)}, u32[]{:S(2)}) collective-permute-start(bf16[16,2560]{1,0:T(8,128)(2,1)S(1)} %get-tuple-element.11), channel_id=1, source_target_pairs={{0,2},{2,4},{4,6},{6,0},{1,3},{3,5},{5,7},{7,1},{8,10},{10,12},{12... | collective-permute-start | bytes 245768 | tf_op jit(solution)/shard_map/ppermute | solution.py:60
  88.0 4.8 %collective-permute-start.3 = (bf16[16,2560]{1,0:T(8,128)(2,1)S(1)}, bf16[16,2560]{1,0:T(8,128)(2,1)S(1)}, u32[]{:S(2)}, u32[]{:S(2)}) collective-permute-start(bf16[16,2560]{1,0:T(8,128)(2,1)S(1)} %get-tuple-element.12), channel_id=1, source_target_pairs={{0,6},{2,0},{4,2},{6,4},{1,7},{3,1},{5,3},{7,5},{8,14},{10,8},{12,... | collective-permute-start | bytes 245768 | tf_op jit(solution)/shard_map/ppermute | solution.py:60
  92.8 5.2 %collective-permute-start.2 = (bf16[16,2560]{1,0:T(8,128)(2,1)S(1)}, bf16[16,2560]{1,0:T(8,128)(2,1)S(1)}, u32[]{:S(2)}, u32[]{:S(2)}) collective-permute-start(bf16[16,2560]{1,0:T(8,128)(2,1)S(1)} %get-tuple-element.13), channel_id=1, source_target_pairs={{0,4},{2,6},{4,0},{6,2},{1,5},{3,7},{5,1},{7,3},{8,12},{10,14},{12... | collective-permute-start | bytes 245768 | tf_op jit(solution)/shard_map/ppermute | solution.py:60
  98.0 1.2 %convolution_convert_fusion.1 = bf16[128,384]{1,0:T(8,128)(2,1)} fusion(bf16[128,2560]{1,0:T(8,128)(2,1)S(1)} %all_gather.3, bf16[2560,384]{1,0:T(8,128)(2,1)S(1)} %copy-done), kind=kOutput, calls=%fused_computation.4 | convolution fusion | flops 251707392 | bytes 2719744 | tf_op jit(solution)/shard_map/dot_general | solution.py:83
  99.2 5.3 %collective-permute-done.2 = bf16[16,2560]{1,0:T(8,128)(2,1)S(1)} collective-permute-done((bf16[16,2560]{1,0:T(8,128)(2,1)S(1)}, bf16[16,2560]{1,0:T(8,128)(2,1)S(1)}, u32[]{:S(2)}, u32[]{:S(2)}) %collective-permute-start.2) | collective-permute-done | bytes 81952 | tf_op jit(solution)/shard_map/ppermute | solution.py:60
  104.5 0.4 convolution_convert_fusion.2
  104.9 0.6 copy.18
  105.5 1.6 %convert_reduce_fusion = f32[20,384]{1,0:T(8,128)} fusion(bf16[16,20,384]{2,1,0:T(8,128)(2,1)} %all-to-all-done.1), kind=kLoop, calls=%fused_computation.7 | loop fusion | flops 238080 | bytes 276480 | tf_op jit(solution)/shard_map/reduce_sum | solution.py:79
  (14 shorter events, 0.1 us)
Async XLA Ops:
  0.6 61.6 %copy-start = (bf16[2560,384]{1,0:T(8,128)(2,1)S(1)}, bf16[2560,384]{1,0:T(8,128)(2,1)}, u32[]{:S(2)}) copy-start(bf16[2560,384]{1,0:T(8,128)(2,1)} %param.4) | copy-start | bytes 5898244
  32.9 29.3 %copy-start.2 = (bf16[128,384]{1,0:T(8,128)(2,1)S(1)}, bf16[128,384]{1,0:T(8,128)(2,1)}, u32[]{:S(2)}) copy-start(bf16[128,384]{1,0:T(8,128)(2,1)} %param.3) | copy-start | bytes 294916
  32.9 29.3 %all-to-all-start = ((bf16[8,320,384]{2,1,0:T(8,128)(2,1)}), bf16[8,320,384]{2,1,0:T(8,128)(2,1)}, u32[]{:S(2)}, u32[]{:S(2)}) async-start(bf16[8,320,384]{2,1,0:T(8,128)(2,1)} %bitcast.39), calls=%async_computation | async-start | bytes 3932160 | tf_op jit(solution)/shard_map/all_to_all | solution.py:74
  69.9 14.3 %collective-permute-start = (bf16[4,16,2560]{2,1,0:T(8,128)(2,1)}, bf16[4,16,2560]{2,1,0:T(8,128)(2,1)}, u32[]{:S(2)}, u32[]{:S(2)}) collective-permute-start(bf16[4,16,2560]{2,1,0:T(8,128)(2,1)} %dynamic-slice_bitcast_fusion), channel_id=1, source_target_pairs={{0,1},{1,0},{2,3},{3,2},{4,5},{5,4},{6,7},{7,6},{8,9},{9,8},{10,11... | collective-permute-start | bytes 983048 | tf_op jit(solution)/shard_map/ppermute | solution.py:54
  72.6 11.7 %copy-start.1 = (bf16[4,2,16,2560]{3,2,1,0:T(8,128)(2,1)S(1)}, bf16[4,2,16,2560]{3,2,1,0:T(8,128)(2,1)}, u32[]{:S(2)}) copy-start(bf16[4,2,16,2560]{3,2,1,0:T(8,128)(2,1)} %convert_element_type.78) | copy-start | bytes 1966084
  75.3 30.2 %all-to-all-start.1 = ((bf16[16,20,384]{2,1,0:T(8,128)(2,1)}), bf16[16,20,384]{2,1,0:T(8,128)(2,1)}, u32[]{:S(2)}, u32[]{:S(2)}) async-start(bf16[16,20,384]{2,1,0:T(8,128)(2,1)} %reshape.34), calls=%async_computation.1 | async-start | bytes 589824 | tf_op jit(solution)/shard_map/all_to_all | solution.py:78
  85.4 13.8 %collective-permute-start.1 = (bf16[16,2560]{1,0:T(8,128)(2,1)S(1)}, bf16[16,2560]{1,0:T(8,128)(2,1)S(1)}, u32[]{:S(2)}, u32[]{:S(2)}) collective-permute-start(bf16[16,2560]{1,0:T(8,128)(2,1)S(1)} %get-tuple-element.11), channel_id=1, source_target_pairs={{0,2},{2,4},{4,6},{6,0},{1,3},{3,5},{5,7},{7,1},{8,10},{10,12},{12... | collective-permute-start | bytes 245768 | tf_op jit(solution)/shard_map/ppermute | solution.py:60
  88.0 11.1 %collective-permute-start.3 = (bf16[16,2560]{1,0:T(8,128)(2,1)S(1)}, bf16[16,2560]{1,0:T(8,128)(2,1)S(1)}, u32[]{:S(2)}, u32[]{:S(2)}) collective-permute-start(bf16[16,2560]{1,0:T(8,128)(2,1)S(1)} %get-tuple-element.12), channel_id=1, source_target_pairs={{0,6},{2,0},{4,2},{6,4},{1,7},{3,1},{5,3},{7,5},{8,14},{10,8},{12,... | collective-permute-start | bytes 245768 | tf_op jit(solution)/shard_map/ppermute | solution.py:60
  92.8 11.6 %collective-permute-start.2 = (bf16[16,2560]{1,0:T(8,128)(2,1)S(1)}, bf16[16,2560]{1,0:T(8,128)(2,1)S(1)}, u32[]{:S(2)}, u32[]{:S(2)}) collective-permute-start(bf16[16,2560]{1,0:T(8,128)(2,1)S(1)} %get-tuple-element.13), channel_id=1, source_target_pairs={{0,4},{2,6},{4,0},{6,2},{1,5},{3,7},{5,1},{7,3},{8,12},{10,14},{12... | collective-permute-start | bytes 245768 | tf_op jit(solution)/shard_map/ppermute | solution.py:60

commit v3 on v1

v3 whole, which is shorter than its diff:
```python
import jax
import jax.numpy as jnp
from jax import lax
from jax.experimental import pallas as pl
from jax.experimental.pallas import tpu as pltpu
from jax.sharding import Mesh
from jax.sharding import PartitionSpec as P

BLK = 128
TENSOR = ("yh", "core")
NEAR = ("yl", "x")
FAR = "z"
CHUNKS = 8
WINDOW = 384
VMEM_LIMIT = 40 * 1024 * 1024

code_offset = 6.0
bf16, f32 = jnp.bfloat16, jnp.float32


def call(kernel, outs, scalars, *arrays, flops=0):
    specs = [pl.BlockSpec(memory_space=pltpu.SMEM)] * len(scalars)
    specs += [pl.BlockSpec(memory_space=pltpu.VMEM)] * len(arrays)
    moved = sum(a.size * a.dtype.itemsize for a in tuple(arrays) + tuple(outs))
    return pl.pallas_call(
        kernel,
        out_shape=outs,
        in_specs=specs,
        out_specs=tuple(pl.BlockSpec(memory_space=pltpu.VMEM) for _ in outs),
        compiler_params=pltpu.CompilerParams(vmem_limit_bytes=VMEM_LIMIT),
        cost_estimate=pl.CostEstimate(flops=flops, bytes_accessed=moved, transcendentals=0),
    )(*[jnp.reshape(s, (1,)).astype(jnp.int32) for s in scalars], *arrays)


def signs_table():
    rows = lax.broadcasted_iota(jnp.int32, (BLK, BLK), 0)
    cols = lax.broadcasted_iota(jnp.int32, (BLK, BLK), 1)
    common = jnp.bitwise_and(rows, cols)
    parity = jnp.zeros((BLK, BLK), jnp.int32)
    for place in range(BLK.bit_length() - 1):
        parity = parity + jnp.bitwise_and(jnp.right_shift(common, place), 1)
    return (1 - 2 * jnp.bitwise_and(parity, 1)).astype(f32).astype(bf16)


def rotate(field, table):
    high = field.astype(bf16)
    rest = field - high.astype(f32)
    middle = rest.astype(bf16)
    low = (rest - middle.astype(f32)).astype(bf16)
    turned = jnp.dot(high, table, preferred_element_type=f32)
    turned += jnp.dot(middle, table, preferred_element_type=f32)
    turned += jnp.dot(low, table, preferred_element_type=f32)
    return turned * (BLK**-0.5)


def pack_kernel(attn_ref, d_ref, out_ref):
    count = attn_ref.shape[0]
    for i in range(CHUNKS):
        out_ref[i, :count, :] = attn_ref[...]
        start = i * 320 // BLK * BLK
        out_ref[i, count:, :] = d_ref[:, start : start + WINDOW]


def values_kernel(core_ref, attn_ref, weight_ref, keep_ref, send_ref):
    table = signs_table()
    count, features = attn_ref.shape[0], weight_ref.shape[0]
    tall, rows = keep_ref.shape[0], keep_ref.shape[1]
    first = core_ref[0] == 0
    for j in range(features // BLK):
        cols = slice(j * BLK, (j + 1) * BLK)
        partial_value = lax.dot_general(
            attn_ref[...], weight_ref[cols, :], (((1,), (1,)), ((), ())), preferred_element_type=f32
        )
        turned = rotate(partial_value, table)
        top = jnp.max(jnp.abs(turned), axis=1, keepdims=True) + 1e-06
        scale = top.astype(bf16).astype(f32)
        coded = (turned / scale + code_offset).astype(bf16)
        values = ((coded.astype(f32) - code_offset) * scale).reshape(tall, 2, rows, BLK)
        zero, one = values[:, 0], values[:, 1]
        keep_ref[:, :, cols] = jnp.where(first, zero, one).astype(bf16)
        send_ref[:, :, cols] = jnp.where(first, one, zero).astype(bf16)


def pair_kernel(me_ref, keep_ref, arrived_ref, own_ref, *sent_refs):
    tall = keep_ref.shape[0]
    me = me_ref[0]
    own_ref[...] = keep_ref[me].astype(f32) + arrived_ref[me].astype(f32)
    for step in range(1, tall):
        other = lax.rem(me + step, tall)
        total = keep_ref[other].astype(f32) + arrived_ref[other].astype(f32)
        sent_refs[step - 1][...] = total.astype(bf16)


def mixed_kernel(own_ref, a_ref, b_ref, c_ref, out_ref):
    table = signs_table()
    for j in range(out_ref.shape[1] // BLK):
        cols = slice(j * BLK, (j + 1) * BLK)
        total = own_ref[:, cols] + a_ref[:, cols].astype(f32)
        total += b_ref[:, cols].astype(f32) + c_ref[:, cols].astype(f32)
        out_ref[:, cols] = rotate(total, table).astype(bf16)


def grad_kernel(odd_ref, near_ref, d_ref, out_ref):
    near, group, rows = d_ref.shape[1], d_ref.shape[0], d_ref.shape[2]
    count = group * rows
    left = jnp.concatenate([d_ref[:, p].reshape(count, WINDOW) for p in range(near)], axis=0)
    right = jnp.concatenate([near_ref[p, :count, :] for p in range(near)], axis=0)
    term = lax.dot_general(left, right, (((0,), (0,)), ((), ())), preferred_element_type=f32)
    far, size = out_ref.shape[0], out_ref.shape[1]
    chunk = far * size
    term = jnp.where(odd_ref[0] == 1, term[WINDOW - chunk :, :], term[:chunk, :])
    for z in range(far):
        out_ref[z] = term[z * size : (z + 1) * size, :].astype(bf16)


def total_kernel(pieces_ref, out_ref):
    out_ref[...] = jnp.sum(pieces_ref[...].astype(f32), axis=0)


def shape(dims, dtype):
    return jax.ShapeDtypeStruct(dims, dtype)


def body(attn, weight, d_out):
    count, width = attn.shape
    features = weight.shape[0]
    group, near, far = lax.axis_size(TENSOR), lax.axis_size(NEAR), lax.axis_size(FAR)
    tall = lax.axis_size("yh")
    rows = count // group
    yh, core = lax.axis_index("yh"), lax.axis_index("core")
    odd = lax.rem(lax.axis_index("x"), 2)

    (packed,) = call(pack_kernel, (shape((near, count + rows, width), bf16),), (), attn, d_out)
    packed, attn = lax.optimization_barrier((packed, attn))
    pieces = lax.all_to_all(packed, NEAR, 0, 0)

    half = shape((tall, rows, features), bf16)
    keep, send = call(
        values_kernel, (half, half), (core,), attn, weight, flops=2 * count * features * (width + 3 * BLK)
    )
    arrived = lax.ppermute(send, "core", [(0, 1), (1, 0)])
    one = shape((rows, features), bf16)
    own, *sent = call(pair_kernel, (shape((rows, features), f32), one, one, one), (yh,), keep, arrived)

    pieces, own = lax.optimization_barrier((pieces, own))
    chunk = lax.all_gather(pieces[:, count:, :], TENSOR)
    (plane,) = call(
        grad_kernel,
        (shape((far, features // near // far, width), bf16),),
        (odd,),
        pieces,
        chunk,
        flops=2 * near * count * WINDOW * width,
    )
    plane, d_out, sent = lax.optimization_barrier((plane, d_out, sent))
    terms = lax.all_to_all(plane, FAR, 0, 0)

    blocks = []
    for step in range(1, tall):
        blocks.append(lax.ppermute(sent[step - 1], "yh", [(i, (i + step) % tall) for i in range(tall)]))
    full_grad = lax.all_gather(d_out, TENSOR, axis=0, tiled=True)
    d_attn = jnp.dot(full_grad, weight, preferred_element_type=f32).astype(bf16)
    (mixed,) = call(mixed_kernel, (one,), (), own, *blocks)
    (w_grad,) = call(total_kernel, (shape((features // near // far, width), f32),), (), terms)
    return (mixed, d_attn, w_grad)


def solution(mesh):
    fine = Mesh(mesh.devices.reshape(2, 4, 16, 4, 2), ("yl", "x", "z", "yh", "core"))
    dp = ("yl", "x", "z")
    in_specs = (P(dp, TENSOR), P(None, TENSOR), P(dp + TENSOR, None))
    out_specs = (P(dp + TENSOR, None), P(dp, TENSOR), P(dp, TENSOR))
    return jax.shard_map(body, mesh=fine, in_specs=in_specs, out_specs=out_specs, check_vma=False)
```

time: 107 us -> 93.8 us (0.88)
  the two profiles are of different devices: /device:TPU:8 before, /device:TPU:1 now
where the time goes in v3:
time: 93.8 us; the launch traced here: 93.3 us
  starting transfers between devices  44.1 us (47%)
  blocking collectives  33.6 us (36%)
  Pallas kernels  8.71 us (9%)
  local copies, waits for them, and re-layouts  3.34 us (4%)
  waiting for transfers between devices  1.58 us (2%)
  matrix products  1.16 us (1%)
    all_gather x1, blocking collectives, body(): full_grad = lax.all_gather(d_out, TENSOR, axis=0, tiled=True)  17.7 us
    all_gather x1, blocking collectives, body(): chunk = lax.all_gather(pieces[:, count:, :], TENSOR)  16 us
    ppermute x1, starting transfers between devices, body(): arrived = lax.ppermute(send, 'core', [(0, 1), (1, 0)])  13.8 us
    all_to_all x1, starting transfers between devices, body(): terms = lax.all_to_all(plane, FAR, 0, 0)  12.9 us
    ppermute x3, starting transfers between devices, body(): lax.ppermute(sent[step - 1], 'yh', [(i, (i + step) % tall) for i in range...  11.6 us
    pallas_call x6, Pallas kernels, call(): pl.pallas_call(kernel, out_shape=outs, in_specs=specs, out_specs=tuple((p...  8.71 us
    all_to_all x1, starting transfers between devices, body(): pieces = lax.all_to_all(packed, NEAR, 0, 0)  5.86 us
    unnamed x16, local copies, waits for them, and re-layouts  3.33 us
  transfers between devices with their start and end apart: 6, of which 1 were waited for; matrix products, arithmetic and copies ran while one was open for 1% of the time, Pallas kernels for 7%

profile of v3, /device:TPU:1, one launch (start us, length us, event | category | flops | bytes accessed | tf_op | source)
XLA Modules:
  0.0 93.3 jit_solution(9986724098448692093)
XLA Ops:
  0.6 0.9 copy-done.2
  1.5 0.9 copy-done.4
  2.4 0.1 shard_map.58
  2.5 0.9 copy-done.1
  3.4 5.9 %all-to-all-start = ((bf16[8,144,384]{2,1,0:T(8,128)(2,1)}), bf16[8,144,384]{2,1,0:T(8,128)(2,1)S(1)}, u32[]{:S(2)}, u32[]{:S(2)}) async-start(bf16[8,144,384]{2,1,0:T(8,128)(2,1)} %copy-done.1), calls=%async_computation | async-start | bytes 1769472 | tf_op jit(solution)/shard_map/all_to_all | solution.py:135
  9.3 3.7 %shard_map.59 = (bf16[4,16,2560]{2,1,0:T(8,128)(2,1)S(1)}, bf16[4,16,2560]{2,1,0:T(8,128)(2,1)}) custom-call(s32[1]{0:T(128)} %bitcast.1.core_ref, bf16[128,384]{1,0:T(8,128)(2,1)S(1)} %copy-done.3, bf16[2560,384]{1,0:T(8,128)(2,1)S(1)} %copy-done), custom_call_target="tpu_custom_call" | custom-call | flops 503316480 | bytes 2719744 | tf_op jit(solution)/shard_map/pallas_call | solution.py:25
  13.0 13.8 %collective-permute-start = (bf16[4,16,2560]{2,1,0:T(8,128)(2,1)}, bf16[4,16,2560]{2,1,0:T(8,128)(2,1)}, u32[]{:S(2)}, u32[]{:S(2)}) collective-permute-start(bf16[4,16,2560]{2,1,0:T(8,128)(2,1)} %get-tuple-element.21), channel_id=1, source_target_pairs={{0,1},{1,0},{2,3},{3,2},{4,5},{5,4},{6,7},{7,6},{8,9},{9,8},{10,11... | collective-permute-start | bytes 983048 | tf_op jit(solution)/shard_map/ppermute | solution.py:141
  26.8 1.6 %collective-permute-done.arrived_ref = bf16[4,16,2560]{2,1,0:T(8,128)(2,1)} collective-permute-done((bf16[4,16,2560]{2,1,0:T(8,128)(2,1)}, bf16[4,16,2560]{2,1,0:T(8,128)(2,1)}, u32[]{:S(2)}, u32[]{:S(2)}) %collective-permute-start) | collective-permute-done | bytes 327712 | tf_op jit(solution)/shard_map/ppermute | solution.py:141
  28.3 1.6 %shard_map.60 = (f32[16,2560]{1,0:T(8,128)S(1)}, bf16[16,2560]{1,0:T(8,128)(2,1)}, bf16[16,2560]{1,0:T(8,128)(2,1)S(1)}, bf16[16,2560]{1,0:T(8,128)(2,1)S(1)}) custom-call(s32[1]{0:T(128)} %bitcast.me_ref, bf16[4,16,2560]{2,1,0:T(8,128)(2,1)S(1)} %get-tuple-element.20.keep_ref, bf16[4,16,2560]{2,1,0:T(8,128)(2,1)} %collective-permute-done.arrived_ref), custom_call_target="tpu_custom_call" | custom-call | bytes 1064960 | tf_op jit(solution)/shard_map/pallas_call | solution.py:25
  30.0 0.6 copy-done.6
  30.6 0.0 all-to-all-done.near_ref
  30.6 16.0 %all-gather = bf16[64,16,384]{2,1,0:T(8,128)(2,1)S(1)} all-gather(bf16[8,16,384]{2,1,0:T(8,128)(2,1)S(1)} %slice.3), channel_id=2, replica_groups=mesh['yl'=2,'x'=4,'z'=16,'yh'=4,'core'=2] {'yh','core'}, dimensions={0}, use_global_device_ids=true | all-gather | bytes 884736 | tf_op jit(solution)/shard_map/all_gather | solution.py:146
  46.6 1.3 %shard_map.61 = bf16[16,20,384]{2,1,0:T(8,128)(2,1)} custom-call(s32[1]{0:T(128)} %bitcast.2.odd_ref, bf16[8,144,384]{2,1,0:T(8,128)(2,1)S(1)} %all-to-all-done.near_ref, bf16[8,8,16,384]{3,2,1,0:T(8,128)(2,1)S(1)} %bitcast.6), custom_call_target="tpu_custom_call" | custom-call | flops 301989888 | bytes 1916928 | tf_op jit(solution)/shard_map/pallas_call | solution.py:25
  47.9 12.9 %all-to-all-start.1 = ((bf16[16,20,384]{2,1,0:T(8,128)(2,1)}), bf16[16,20,384]{2,1,0:T(8,128)(2,1)S(1)}, u32[]{:S(2)}, u32[]{:S(2)}) async-start(bf16[16,20,384]{2,1,0:T(8,128)(2,1)} %shard_map.61), calls=%async_computation.1 | async-start | bytes 589824 | tf_op jit(solution)/shard_map/all_to_all | solution.py:156
  60.8 2.9 %collective-permute-start.1 = (bf16[16,2560]{1,0:T(8,128)(2,1)}, bf16[16,2560]{1,0:T(8,128)(2,1)S(1)}, u32[]{:S(2)}, u32[]{:S(2)}) collective-permute-start(bf16[16,2560]{1,0:T(8,128)(2,1)} %get-tuple-element.28), channel_id=1, source_target_pairs={{0,2},{2,4},{4,6},{6,0},{1,3},{3,5},{5,7},{7,1},{8,10},{10,12},{12... | collective-permute-start | bytes 245768 | tf_op jit(solution)/shard_map/ppermute | solution.py:160
  63.7 4.0 %collective-permute-start.2 = (bf16[16,2560]{1,0:T(8,128)(2,1)S(1)}, bf16[16,2560]{1,0:T(8,128)(2,1)S(1)}, u32[]{:S(2)}, u32[]{:S(2)}) collective-permute-start(bf16[16,2560]{1,0:T(8,128)(2,1)S(1)} %copy-done.7), channel_id=1, source_target_pairs={{0,4},{2,6},{4,0},{6,2},{1,5},{3,7},{5,1},{7,3},{8,12},{10,14},{12... | collective-permute-start | bytes 245768 | tf_op jit(solution)/shard_map/ppermute | solution.py:160
  67.7 4.7 %collective-permute-start.3 = (bf16[16,2560]{1,0:T(8,128)(2,1)S(1)}, bf16[16,2560]{1,0:T(8,128)(2,1)S(1)}, u32[]{:S(2)}, u32[]{:S(2)}) collective-permute-start(bf16[16,2560]{1,0:T(8,128)(2,1)S(1)} %get-tuple-element.30), channel_id=1, source_target_pairs={{0,6},{2,0},{4,2},{6,4},{1,7},{3,1},{5,3},{7,5},{8,14},{10,8},{12,... | collective-permute-start | bytes 245768 | tf_op jit(solution)/shard_map/ppermute | solution.py:160
  72.5 17.7 %all_gather.11 = bf16[128,2560]{1,0:T(8,128)(2,1)S(1)} all-gather(bf16[16,2560]{1,0:T(8,128)(2,1)S(1)} %copy-done.5), channel_id=1, replica_groups=mesh['yl'=2,'x'=4,'z'=16,'yh'=4,'core'=2] {'yh','core'}, dimensions={0}, use_global_device_ids=true | all-gather | bytes 737280 | tf_op jit(solution)/shard_map/all_gather | solution.py:161
  90.1 1.2 %convolution_convert_fusion = bf16[128,384]{1,0:T(8,128)(2,1)} fusion(bf16[128,2560]{1,0:T(8,128)(2,1)S(1)} %all_gather.11, bf16[2560,384]{1,0:T(8,128)(2,1)S(1)} %copy-done), kind=kOutput, calls=%fused_computation | convolution fusion | flops 251707392 | bytes 2719744 | tf_op jit(solution)/shard_map/dot_general | solution.py:162
  91.3 0.0 collective-permute-done.1.a_ref
  91.3 0.0 collective-permute-done.2.b_ref
  91.3 0.0 collective-permute-done.3.c_ref
  91.3 1.3 %shard_map.62 = bf16[16,2560]{1,0:T(8,128)(2,1)} custom-call(f32[16,2560]{1,0:T(8,128)S(1)} %get-tuple-element.23.own_ref, bf16[16,2560]{1,0:T(8,128)(2,1)S(1)} %collective-permute-done.1.a_ref, bf16[16,2560]{1,0:T(8,128)(2,1)S(1)} %collective-permute-done.2.b_ref, bf16[16,2560]{1,0:T(8,128)(2,1)S(1)} %collective-permute-done.3.c_ref), custom_call_target="tpu_custom_call" | custom-call | bytes 491520 | tf_op jit(solution)/shard_map/pallas_call | solution.py:25
  92.6 0.7 shard_map.63
  (14 shorter events, 0.0 us)
Async XLA Ops:
  0.6 0.9 copy-start.2
  1.5 0.9 copy-start.4
  2.4 6.9 %copy-start = (bf16[2560,384]{1,0:T(8,128)(2,1)S(1)}, bf16[2560,384]{1,0:T(8,128)(2,1)}, u32[]{:S(2)}) copy-start(bf16[2560,384]{1,0:T(8,128)(2,1)} %weight_ref.1) | copy-start | bytes 5898244
  2.4 6.9 %copy-start.3 = (bf16[128,384]{1,0:T(8,128)(2,1)S(1)}, bf16[128,384]{1,0:T(8,128)(2,1)}, u32[]{:S(2)}) copy-start(bf16[128,384]{1,0:T(8,128)(2,1)} %attn_ref.2) | copy-start | bytes 294916
  2.5 0.9 copy-start.1
  3.4 27.2 %all-to-all-start = ((bf16[8,144,384]{2,1,0:T(8,128)(2,1)}), bf16[8,144,384]{2,1,0:T(8,128)(2,1)S(1)}, u32[]{:S(2)}, u32[]{:S(2)}) async-start(bf16[8,144,384]{2,1,0:T(8,128)(2,1)} %copy-done.1), calls=%async_computation | async-start | bytes 1769472 | tf_op jit(solution)/shard_map/all_to_all | solution.py:135
  13.0 15.3 %collective-permute-start = (bf16[4,16,2560]{2,1,0:T(8,128)(2,1)}, bf16[4,16,2560]{2,1,0:T(8,128)(2,1)}, u32[]{:S(2)}, u32[]{:S(2)}) collective-permute-start(bf16[4,16,2560]{2,1,0:T(8,128)(2,1)} %get-tuple-element.21), channel_id=1, source_target_pairs={{0,1},{1,0},{2,3},{3,2},{4,5},{5,4},{6,7},{7,6},{8,9},{9,8},{10,11... | collective-permute-start | bytes 983048 | tf_op jit(solution)/shard_map/ppermute | solution.py:141
  30.0 0.6 copy-start.6
  30.6 41.9 %copy-start.5 = (bf16[16,2560]{1,0:T(8,128)(2,1)S(1)}, bf16[16,2560]{1,0:T(8,128)(2,1)}, u32[]{:S(2)}) copy-start(bf16[16,2560]{1,0:T(8,128)(2,1)} %d_ref.1) | copy-start | bytes 245764
  30.6 33.1 %copy-start.7 = (bf16[16,2560]{1,0:T(8,128)(2,1)S(1)}, bf16[16,2560]{1,0:T(8,128)(2,1)}, u32[]{:S(2)}) copy-start(bf16[16,2560]{1,0:T(8,128)(2,1)} %copy-done.6) | copy-start | bytes 245764
  47.9 44.7 %all-to-all-start.1 = ((bf16[16,20,384]{2,1,0:T(8,128)(2,1)}), bf16[16,20,384]{2,1,0:T(8,128)(2,1)S(1)}, u32[]{:S(2)}, u32[]{:S(2)}) async-start(bf16[16,20,384]{2,1,0:T(8,128)(2,1)} %shard_map.61), calls=%async_computation.1 | async-start | bytes 589824 | tf_op jit(solution)/shard_map/all_to_all | solution.py:156
  60.8 30.5 %collective-permute-start.1 = (bf16[16,2560]{1,0:T(8,128)(2,1)}, bf16[16,2560]{1,0:T(8,128)(2,1)S(1)}, u32[]{:S(2)}, u32[]{:S(2)}) collective-permute-start(bf16[16,2560]{1,0:T(8,128)(2,1)} %get-tuple-element.28), channel_id=1, source_target_pairs={{0,2},{2,4},{4,6},{6,0},{1,3},{3,5},{5,7},{7,1},{8,10},{10,12},{12... | collective-permute-start | bytes 245768 | tf_op jit(solution)/shard_map/ppermute | solution.py:160
  63.7 27.6 %collective-permute-start.2 = (bf16[16,2560]{1,0:T(8,128)(2,1)S(1)}, bf16[16,2560]{1,0:T(8,128)(2,1)S(1)}, u32[]{:S(2)}, u32[]{:S(2)}) collective-permute-start(bf16[16,2560]{1,0:T(8,128)(2,1)S(1)} %copy-done.7), channel_id=1, source_target_pairs={{0,4},{2,6},{4,0},{6,2},{1,5},{3,7},{5,1},{7,3},{8,12},{10,14},{12... | collective-permute-start | bytes 245768 | tf_op jit(solution)/shard_map/ppermute | solution.py:160
  67.7 23.6 %collective-permute-start.3 = (bf16[16,2560]{1,0:T(8,128)(2,1)S(1)}, bf16[16,2560]{1,0:T(8,128)(2,1)S(1)}, u32[]{:S(2)}, u32[]{:S(2)}) collective-permute-start(bf16[16,2560]{1,0:T(8,128)(2,1)S(1)} %get-tuple-element.30), channel_id=1, source_target_pairs={{0,6},{2,0},{4,2},{6,4},{1,7},{3,1},{5,3},{7,5},{8,14},{10,8},{12,... | collective-permute-start | bytes 245768 | tf_op jit(solution)/shard_map/ppermute | solution.py:160

commit v4 on v3

--- a/solution.py
+++ b/solution.py
@@ -53,12 +53,39 @@
     return turned * (BLK**-0.5)
 
 
-def pack_kernel(attn_ref, d_ref, out_ref):
+def pack_kernel(attn_ref, d_ref, out_ref, sems):
     count = attn_ref.shape[0]
+    copies = []
     for i in range(CHUNKS):
-        out_ref[i, :count, :] = attn_ref[...]
         start = i * 320 // BLK * BLK
-        out_ref[i, count:, :] = d_ref[:, start : start + WINDOW]
+        window = d_ref.at[:, pl.ds(start, WINDOW)]
+        copies.append((attn_ref, out_ref.at[i, pl.ds(0, count), :]))
+        copies.append((window, out_ref.at[i, pl.ds(count, d_ref.shape[0]), :]))
+    copies = [pltpu.make_async_copy(a, b, sems.at[k]) for k, (a, b) in enumerate(copies)]
+    for copy in copies:
+        copy.start()
+    for copy in copies:
+        copy.wait()
+
+
+def pack(attn, d_out):
+    (count, width), rows = attn.shape, d_out.shape[0]
+    out = shape((CHUNKS, count + rows, width), bf16)
+    return pl.pallas_call(
+        pack_kernel,
+        out_shape=out,
+        in_specs=[pl.BlockSpec(memory_space=pltpu.HBM)] * 2,
+        out_specs=pl.BlockSpec(memory_space=pltpu.HBM),
+        scratch_shapes=[pltpu.SemaphoreType.DMA((2 * CHUNKS,))],
+        cost_estimate=pl.CostEstimate(flops=0, bytes_accessed=4 * out.size, transcendentals=0),
+    )(attn, d_out)
+
+
+def rows_kernel(near_ref, d_ref, out_ref):
+    near, rows = near_ref.shape[0], d_ref.shape[0]
+    for p in range(near):
+        out_ref[:, p * WINDOW : (p + 1) * WINDOW] = near_ref[p, near_ref.shape[1] - rows :, :]
+    out_ref[:, near * WINDOW :] = d_ref[...]
 
 
 def values_kernel(core_ref, attn_ref, weight_ref, keep_ref, send_ref):
@@ -101,9 +128,8 @@
 
 
 def grad_kernel(odd_ref, near_ref, d_ref, out_ref):
-    near, group, rows = d_ref.shape[1], d_ref.shape[0], d_ref.shape[2]
-    count = group * rows
-    left = jnp.concatenate([d_ref[:, p].reshape(count, WINDOW) for p in range(near)], axis=0)
+    near, count = near_ref.shape[0], d_ref.shape[0]
+    left = jnp.concatenate([d_ref[:, p * WINDOW : (p + 1) * WINDOW] for p in range(near)], axis=0)
     right = jnp.concatenate([near_ref[p, :count, :] for p in range(near)], axis=0)
     term = lax.dot_general(left, right, (((0,), (0,)), ((), ())), preferred_element_type=f32)
     far, size = out_ref.shape[0], out_ref.shape[1]
@@ -111,6 +137,12 @@
     term = jnp.where(odd_ref[0] == 1, term[WINDOW - chunk :, :], term[:chunk, :])
     for z in range(far):
         out_ref[z] = term[z * size : (z + 1) * size, :].astype(bf16)
+
+
+def d_attn_kernel(d_ref, weight_ref, out_ref):
+    start = d_ref.shape[1] - weight_ref.shape[0]
+    product = jnp.dot(d_ref[:, start:], weight_ref[...], preferred_element_type=f32)
+    out_ref[...] = product.astype(bf16)
 
 
 def total_kernel(pieces_ref, out_ref):
@@ -130,7 +162,7 @@
     yh, core = lax.axis_index("yh"), lax.axis_index("core")
     odd = lax.rem(lax.axis_index("x"), 2)
 
-    (packed,) = call(pack_kernel, (shape((near, count + rows, width), bf16),), (), attn, d_out)
+    packed = pack(attn, d_out)
     packed, attn = lax.optimization_barrier((packed, attn))
     pieces = lax.all_to_all(packed, NEAR, 0, 0)
 
@@ -142,24 +174,26 @@
     one = shape((rows, features), bf16)
     own, *sent = call(pair_kernel, (shape((rows, features), f32), one, one, one), (yh,), keep, arrived)
 
-    pieces, own = lax.optimization_barrier((pieces, own))
-    chunk = lax.all_gather(pieces[:, count:, :], TENSOR)
+    pieces, own, d_out = lax.optimization_barrier((pieces, own, d_out))
+    (lines,) = call(rows_kernel, (shape((rows, near * WINDOW + features), bf16),), (), pieces, d_out)
+    lines = lax.all_gather(lines, TENSOR, axis=0, tiled=True)
     (plane,) = call(
         grad_kernel,
         (shape((far, features // near // far, width), bf16),),
         (odd,),
         pieces,
-        chunk,
+        lines,
         flops=2 * near * count * WINDOW * width,
     )
-    plane, d_out, sent = lax.optimization_barrier((plane, d_out, sent))
+    plane, lines, sent = lax.optimization_barrier((plane, lines, sent))
     terms = lax.all_to_all(plane, FAR, 0, 0)
 
     blocks = []
     for step in range(1, tall):
         blocks.append(lax.ppermute(sent[step - 1], "yh", [(i, (i + step) % tall) for i in range(tall)]))
-    full_grad = lax.all_gather(d_out, TENSOR, axis=0, tiled=True)
-    d_attn = jnp.dot(full_grad, weight, preferred_element_type=f32).astype(bf16)
+    (d_attn,) = call(
+        d_attn_kernel, (shape((count, width), bf16),), (), lines, weight, flops=2 * count * features * width
+    )
     (mixed,) = call(mixed_kernel, (one,), (), own, *blocks)
     (w_grad,) = call(total_kernel, (shape((features // near // far, width), f32),), (), terms)
     return (mixed, d_attn, w_grad)

time: 93.8 us -> 145 us (1.55)
  waiting for transfers between devices: 1.58 us -> 45 us
  blocking collectives: 33.6 us -> 0 us
  Pallas kernels: 8.71 us -> 37.9 us
  between operations: 0.74 us -> 14.2 us
    all_gather x0 -> x1, waiting for transfers between devices: none -> 38.2 us  [body(): lines = lax.all_gather(lines, TENSOR, axis=0, tiled=True)]
    all_gather x2 -> x0, blocking collectives: 33.6 us -> none  [the longest x1 17.7 us: body(): full_grad = lax.all_gather(d_out, TENSOR, axis=0, tiled=True)]
    pallas_call x0 -> x1, Pallas kernels: none -> 28 us  [pack(): pl.pallas_call(pack_kernel, out_shape=out, in_specs=[pl.BlockSpec(memory_...]
    ppermute x3, waiting for transfers between devices: 0.01 us -> 5.29 us  [body(): lax.ppermute(sent[step - 1], 'yh', [(i, (i + step) % tall) for i in range...]
    ppermute x3, starting transfers between devices: 11.6 us -> 10.1 us  [body(): lax.ppermute(sent[step - 1], 'yh', [(i, (i + step) % tall) for i in range...]
    pallas_call x6 -> x7, Pallas kernels: 8.71 us -> 9.89 us  [call(): pl.pallas_call(kernel, out_shape=outs, in_specs=specs, out_specs=tuple((p...]
    unnamed x16 -> x20, local copies, waits for them, and re-layouts: 3.33 us -> 4.01 us
  transfers between devices with their start and end apart: 6 -> 7, of which waited for: 1 -> 3; matrix products, arithmetic and copies ran while one was open for 1% -> 0% of each run, Pallas kernels for 7% -> 5%
where the time goes in v4:
time: 145 us; the launch traced here: 144 us
  waiting for transfers between devices  45 us (31%)
  starting transfers between devices  43 us (30%)
  Pallas kernels  37.9 us (26%)
  between operations  14.2 us (10%)
  local copies, waits for them, and re-layouts  4.01 us (3%)
    all_gather x1, waiting for transfers between devices, body(): lines = lax.all_gather(lines, TENSOR, axis=0, tiled=True)  38.2 us
    pallas_call x1, Pallas kernels, pack(): pl.pallas_call(pack_kernel, out_shape=out, in_specs=[pl.BlockSpec(memory_...  28 us
    ppermute x1, starting transfers between devices, body(): arrived = lax.ppermute(send, 'core', [(0, 1), (1, 0)])  13.7 us
    all_to_all x1, starting transfers between devices, body(): terms = lax.all_to_all(plane, FAR, 0, 0)  13.2 us
    ppermute x3, starting transfers between devices, body(): lax.ppermute(sent[step - 1], 'yh', [(i, (i + step) % tall) for i in range...  10.1 us
    pallas_call x7, Pallas kernels, call(): pl.pallas_call(kernel, out_shape=outs, in_specs=specs, out_specs=tuple((p...  9.89 us
    all_to_all x1, starting transfers between devices, body(): pieces = lax.all_to_all(packed, NEAR, 0, 0)  6.01 us
    ppermute x3, waiting for transfers between devices, body(): lax.ppermute(sent[step - 1], 'yh', [(i, (i + step) % tall) for i in range...  5.29 us
  transfers between devices with their start and end apart: 7, of which 3 were waited for; matrix products, arithmetic and copies ran while one was open for 0% of the time, Pallas kernels for 5%

profile of v4, /device:TPU:1, one launch (start us, length us, event | category | flops | bytes accessed | tf_op | source)
XLA Modules:
  0.0 144.2 jit_solution(16989531708417154616)
XLA Ops:
  7.2 28.0 %shard_map.58 = bf16[8,144,384]{2,1,0:T(8,128)(2,1)} custom-call(bf16[128,384]{1,0:T(8,128)(2,1)} %attn_ref.2, bf16[16,2560]{1,0:T(8,128)(2,1)} %d_ref.2), custom_call_target="tpu_custom_call" | custom-call | bytes 1769472 | tf_op jit(solution)/shard_map/pallas_call | solution.py:74
  35.2 0.0 copy-start.4
  35.3 6.0 %all-to-all-start = ((bf16[8,144,384]{2,1,0:T(8,128)(2,1)}), bf16[8,144,384]{2,1,0:T(8,128)(2,1)S(1)}, u32[]{:S(2)}, u32[]{:S(2)}) async-start(bf16[8,144,384]{2,1,0:T(8,128)(2,1)} %shard_map.58), calls=%async_computation | async-start | bytes 1769472 | tf_op jit(solution)/shard_map/all_to_all | solution.py:167
  41.3 0.0 all-gather.2.cloned.1.call-start
  41.3 3.7 %shard_map.59 = (bf16[4,16,2560]{2,1,0:T(8,128)(2,1)S(1)}, bf16[4,16,2560]{2,1,0:T(8,128)(2,1)}) custom-call(s32[1]{0:T(128)} %bitcast.1.core_ref, bf16[128,384]{1,0:T(8,128)(2,1)S(1)} %copy-done.3, bf16[2560,384]{1,0:T(8,128)(2,1)S(1)} %copy-done), custom_call_target="tpu_custom_call" | custom-call | flops 503316480 | bytes 2719744 | tf_op jit(solution)/shard_map/pallas_call | solution.py:25
  45.0 13.7 %collective-permute-start = (bf16[4,16,2560]{2,1,0:T(8,128)(2,1)}, bf16[4,16,2560]{2,1,0:T(8,128)(2,1)}, u32[]{:S(2)}, u32[]{:S(2)}) collective-permute-start(bf16[4,16,2560]{2,1,0:T(8,128)(2,1)} %get-tuple-element.22), channel_id=1, source_target_pairs={{0,1},{1,0},{2,3},{3,2},{4,5},{5,4},{6,7},{7,6},{8,9},{9,8},{10,11... | collective-permute-start | bytes 983048 | tf_op jit(solution)/shard_map/ppermute | solution.py:173
  58.8 1.6 %collective-permute-done.arrived_ref = bf16[4,16,2560]{2,1,0:T(8,128)(2,1)} collective-permute-done((bf16[4,16,2560]{2,1,0:T(8,128)(2,1)}, bf16[4,16,2560]{2,1,0:T(8,128)(2,1)}, u32[]{:S(2)}, u32[]{:S(2)}) %collective-permute-start) | collective-permute-done | bytes 327712 | tf_op jit(solution)/shard_map/ppermute | solution.py:173
  60.4 1.0 shard_map.60
  61.4 0.6 copy-done.6
  62.1 0.6 copy-done.8
  62.7 0.7 shard_map.61
  63.4 0.0 all-gather.2.cloned.1.call-update
  63.4 38.2 %all-gather.2.cloned.1.call-done.d_ref = bf16[128,5632]{1,0:T(8,128)(2,1)} async-done(((bf16[16,5632]{1,0:T(8,128)(2,1)}), bf16[128,5632]{1,0:T(8,128)(2,1)}) %all-gather.2.cloned.1.call-update) | async-done | bytes 1441808 | tf_op jit(solution)/shard_map/all_gather | solution.py:179
  101.6 1.4 copy-done.1
  102.9 1.3 shard_map.62
  104.3 13.2 %all-to-all-start.1 = ((bf16[16,20,384]{2,1,0:T(8,128)(2,1)}), bf16[16,20,384]{2,1,0:T(8,128)(2,1)S(1)}, u32[]{:S(2)}, u32[]{:S(2)}) async-start(bf16[16,20,384]{2,1,0:T(8,128)(2,1)} %shard_map.62), calls=%async_computation.1 | async-start | bytes 589824 | tf_op jit(solution)/shard_map/all_to_all | solution.py:189
  117.5 2.4 %collective-permute-start.1 = (bf16[16,2560]{1,0:T(8,128)(2,1)S(1)}, bf16[16,2560]{1,0:T(8,128)(2,1)S(1)}, u32[]{:S(2)}, u32[]{:S(2)}) collective-permute-start(bf16[16,2560]{1,0:T(8,128)(2,1)S(1)} %copy-done.9), channel_id=1, source_target_pairs={{0,2},{2,4},{4,6},{6,0},{1,3},{3,5},{5,7},{7,1},{8,10},{10,12},{12... | collective-permute-start | bytes 245768 | tf_op jit(solution)/shard_map/ppermute | solution.py:193
  119.8 5.8 %collective-permute-start.2 = (bf16[16,2560]{1,0:T(8,128)(2,1)S(1)}, bf16[16,2560]{1,0:T(8,128)(2,1)S(1)}, u32[]{:S(2)}, u32[]{:S(2)}) collective-permute-start(bf16[16,2560]{1,0:T(8,128)(2,1)S(1)} %copy-done.7), channel_id=1, source_target_pairs={{0,4},{2,6},{4,0},{6,2},{1,5},{3,7},{5,1},{7,3},{8,12},{10,14},{12... | collective-permute-start | bytes 245768 | tf_op jit(solution)/shard_map/ppermute | solution.py:193
  125.6 1.9 %collective-permute-start.3 = (bf16[16,2560]{1,0:T(8,128)(2,1)}, bf16[16,2560]{1,0:T(8,128)(2,1)S(1)}, u32[]{:S(2)}, u32[]{:S(2)}) collective-permute-start(bf16[16,2560]{1,0:T(8,128)(2,1)} %copy-done.5), channel_id=1, source_target_pairs={{0,6},{2,0},{4,2},{6,4},{1,7},{3,1},{5,3},{7,5},{8,14},{10,8},{12,... | collective-permute-start | bytes 245768 | tf_op jit(solution)/shard_map/ppermute | solution.py:193
  127.6 1.4 copy-done.2
  128.9 1.1 shard_map.64
  130.1 5.3 %collective-permute-done.3.c_ref = bf16[16,2560]{1,0:T(8,128)(2,1)S(1)} collective-permute-done((bf16[16,2560]{1,0:T(8,128)(2,1)}, bf16[16,2560]{1,0:T(8,128)(2,1)S(1)}, u32[]{:S(2)}, u32[]{:S(2)}) %collective-permute-start.3) | collective-permute-done | bytes 81952 | tf_op jit(solution)/shard_map/ppermute | solution.py:193
  135.4 1.3 shard_map.63
  136.7 0.7 shard_map.65
  (19 shorter events, 0.0 us)
Async XLA Ops:
  7.2 34.1 %copy-start.3 = (bf16[128,384]{1,0:T(8,128)(2,1)S(1)}, bf16[128,384]{1,0:T(8,128)(2,1)}, u32[]{:S(2)}) copy-start(bf16[128,384]{1,0:T(8,128)(2,1)} %attn_ref.2) | copy-start | bytes 294916
  7.2 34.1 %copy-start = (bf16[2560,384]{1,0:T(8,128)(2,1)S(1)}, bf16[2560,384]{1,0:T(8,128)(2,1)}, u32[]{:S(2)}) copy-start(bf16[2560,384]{1,0:T(8,128)(2,1)} %weight_ref.3) | copy-start | bytes 5898244
  35.2 27.5 %copy-start.4 = (bf16[16,2560]{1,0:T(8,128)(2,1)S(1)}, bf16[16,2560]{1,0:T(8,128)(2,1)}, u32[]{:S(2)}) copy-start(bf16[16,2560]{1,0:T(8,128)(2,1)} %d_ref.2) | copy-start | bytes 245764
  35.3 27.4 %all-to-all-start = ((bf16[8,144,384]{2,1,0:T(8,128)(2,1)}), bf16[8,144,384]{2,1,0:T(8,128)(2,1)S(1)}, u32[]{:S(2)}, u32[]{:S(2)}) async-start(bf16[8,144,384]{2,1,0:T(8,128)(2,1)} %shard_map.58), calls=%async_computation | async-start | bytes 1769472 | tf_op jit(solution)/shard_map/all_to_all | solution.py:167
  41.3 60.3 %all-gather.2.cloned.1.call-start = ((), (), s32[]{:S(2)}) async-start(), calls=%async_computation.2 | async-start | bytes 1622016 | tf_op jit(solution)/shard_map/all_gather | solution.py:179
  45.0 15.3 %collective-permute-start = (bf16[4,16,2560]{2,1,0:T(8,128)(2,1)}, bf16[4,16,2560]{2,1,0:T(8,128)(2,1)}, u32[]{:S(2)}, u32[]{:S(2)}) collective-permute-start(bf16[4,16,2560]{2,1,0:T(8,128)(2,1)} %get-tuple-element.22), channel_id=1, source_target_pairs={{0,1},{1,0},{2,3},{3,2},{4,5},{5,4},{6,7},{7,6},{8,9},{9,8},{10,11... | collective-permute-start | bytes 983048 | tf_op jit(solution)/shard_map/ppermute | solution.py:173
  61.4 0.6 copy-start.6
  62.1 0.6 copy-start.8
  62.7 41.6 %copy-start.5 = (bf16[16,2560]{1,0:T(8,128)(2,1)}, bf16[16,2560]{1,0:T(8,128)(2,1)S(1)}, u32[]{:S(2)}) copy-start(bf16[16,2560]{1,0:T(8,128)(2,1)S(1)} %get-tuple-element.32) | copy-start | bytes 245764
  63.4 54.1 %copy-start.9 = (bf16[16,2560]{1,0:T(8,128)(2,1)S(1)}, bf16[16,2560]{1,0:T(8,128)(2,1)}, u32[]{:S(2)}) copy-start(bf16[16,2560]{1,0:T(8,128)(2,1)} %copy-done.8) | copy-start | bytes 245764
  63.4 56.5 %copy-start.7 = (bf16[16,2560]{1,0:T(8,128)(2,1)S(1)}, bf16[16,2560]{1,0:T(8,128)(2,1)}, u32[]{:S(2)}) copy-start(bf16[16,2560]{1,0:T(8,128)(2,1)} %copy-done.6) | copy-start | bytes 245764
  101.6 1.4 copy-start.1
  104.3 32.4 %all-to-all-start.1 = ((bf16[16,20,384]{2,1,0:T(8,128)(2,1)}), bf16[16,20,384]{2,1,0:T(8,128)(2,1)S(1)}, u32[]{:S(2)}, u32[]{:S(2)}) async-start(bf16[16,20,384]{2,1,0:T(8,128)(2,1)} %shard_map.62), calls=%async_computation.1 | async-start | bytes 589824 | tf_op jit(solution)/shard_map/all_to_all | solution.py:189
  117.5 12.6 %collective-permute-start.1 = (bf16[16,2560]{1,0:T(8,128)(2,1)S(1)}, bf16[16,2560]{1,0:T(8,128)(2,1)S(1)}, u32[]{:S(2)}, u32[]{:S(2)}) collective-permute-start(bf16[16,2560]{1,0:T(8,128)(2,1)S(1)} %copy-done.9), channel_id=1, source_target_pairs={{0,2},{2,4},{4,6},{6,0},{1,3},{3,5},{5,7},{7,1},{8,10},{10,12},{12... | collective-permute-start | bytes 245768 | tf_op jit(solution)/shard_map/ppermute | solution.py:193
  119.8 10.2 %collective-permute-start.2 = (bf16[16,2560]{1,0:T(8,128)(2,1)S(1)}, bf16[16,2560]{1,0:T(8,128)(2,1)S(1)}, u32[]{:S(2)}, u32[]{:S(2)}) collective-permute-start(bf16[16,2560]{1,0:T(8,128)(2,1)S(1)} %copy-done.7), channel_id=1, source_target_pairs={{0,4},{2,6},{4,0},{6,2},{1,5},{3,7},{5,1},{7,3},{8,12},{10,14},{12... | collective-permute-start | bytes 245768 | tf_op jit(solution)/shard_map/ppermute | solution.py:193
  125.6 9.7 %collective-permute-start.3 = (bf16[16,2560]{1,0:T(8,128)(2,1)}, bf16[16,2560]{1,0:T(8,128)(2,1)S(1)}, u32[]{:S(2)}, u32[]{:S(2)}) collective-permute-start(bf16[16,2560]{1,0:T(8,128)(2,1)} %copy-done.5), channel_id=1, source_target_pairs={{0,6},{2,0},{4,2},{6,4},{1,7},{3,1},{5,3},{7,5},{8,14},{10,8},{12,... | collective-permute-start | bytes 245768 | tf_op jit(solution)/shard_map/ppermute | solution.py:193
  127.6 1.4 copy-start.2
Sparse Core Ops, SparseCore 0:
  63.5 37.9 all-gather.1

commit v5 on v3

--- a/solution.py
+++ b/solution.py
@@ -56,8 +56,8 @@
 def pack_kernel(attn_ref, d_ref, out_ref):
     count = attn_ref.shape[0]
     for i in range(CHUNKS):
+        start = i * 320 // BLK * BLK
         out_ref[i, :count, :] = attn_ref[...]
-        start = i * 320 // BLK * BLK
         out_ref[i, count:, :] = d_ref[:, start : start + WINDOW]
 
 
@@ -100,21 +100,30 @@
         out_ref[:, cols] = rotate(total, table).astype(bf16)
 
 
-def grad_kernel(odd_ref, near_ref, d_ref, out_ref):
-    near, group, rows = d_ref.shape[1], d_ref.shape[0], d_ref.shape[2]
-    count = group * rows
-    left = jnp.concatenate([d_ref[:, p].reshape(count, WINDOW) for p in range(near)], axis=0)
+def grad_kernel(odd_ref, near_ref, out_ref):
+    near, count = near_ref.shape[0], near_ref.shape[1] // 2
+    left = jnp.concatenate([near_ref[p, count:, :] for p in range(near)], axis=0)
     right = jnp.concatenate([near_ref[p, :count, :] for p in range(near)], axis=0)
     term = lax.dot_general(left, right, (((0,), (0,)), ((), ())), preferred_element_type=f32)
-    far, size = out_ref.shape[0], out_ref.shape[1]
+    far, size = out_ref.shape[0], out_ref.shape[1] * BLK // term.shape[1]
     chunk = far * size
     term = jnp.where(odd_ref[0] == 1, term[WINDOW - chunk :, :], term[:chunk, :])
     for z in range(far):
-        out_ref[z] = term[z * size : (z + 1) * size, :].astype(bf16)
+        block = term[z * size : (z + 1) * size, :]
+        parts = [block[:, c : c + BLK] for c in range(0, term.shape[1], BLK)]
+        out_ref[z] = jnp.concatenate(parts, axis=0).astype(bf16)
+
+
+def d_attn_kernel(d_ref, weight_ref, out_ref):
+    product = jnp.dot(d_ref[...], weight_ref[...], preferred_element_type=f32)
+    out_ref[...] = product.astype(bf16)
 
 
 def total_kernel(pieces_ref, out_ref):
-    out_ref[...] = jnp.sum(pieces_ref[...].astype(f32), axis=0)
+    total = jnp.sum(pieces_ref[...].astype(f32), axis=0)
+    size = out_ref.shape[0]
+    for c in range(out_ref.shape[1] // BLK):
+        out_ref[:, c * BLK : (c + 1) * BLK] = total[c * size : (c + 1) * size, :]
 
 
 def shape(dims, dtype):
@@ -130,9 +139,24 @@
     yh, core = lax.axis_index("yh"), lax.axis_index("core")
     odd = lax.rem(lax.axis_index("x"), 2)
 
-    (packed,) = call(pack_kernel, (shape((near, count + rows, width), bf16),), (), attn, d_out)
-    packed, attn = lax.optimization_barrier((packed, attn))
+    full_grad = lax.all_gather(d_out, TENSOR, axis=0, tiled=True)
+    (packed,) = call(pack_kernel, (shape((near, 2 * count, width), bf16),), (), attn, full_grad)
+    packed, attn, full_grad, weight, odd, yh, core = lax.optimization_barrier(
+        (packed, attn, full_grad, weight, odd, yh, core)
+    )
     pieces = lax.all_to_all(packed, NEAR, 0, 0)
+    pieces, attn, full_grad, weight, odd, yh, core = lax.optimization_barrier(
+        (pieces, attn, full_grad, weight, odd, yh, core)
+    )
+    (plane,) = call(
+        grad_kernel,
+        (shape((far, features // near // far * width // BLK, BLK), bf16),),
+        (odd,),
+        pieces,
+        flops=2 * near * count * WINDOW * width,
+    )
+    plane, attn, full_grad, core = lax.optimization_barrier((plane, attn, full_grad, core))
+    terms = lax.all_to_all(plane, FAR, 0, 0)
 
     half = shape((tall, rows, features), bf16)
     keep, send = call(
@@ -141,25 +165,12 @@
     arrived = lax.ppermute(send, "core", [(0, 1), (1, 0)])
     one = shape((rows, features), bf16)
     own, *sent = call(pair_kernel, (shape((rows, features), f32), one, one, one), (yh,), keep, arrived)
-
-    pieces, own = lax.optimization_barrier((pieces, own))
-    chunk = lax.all_gather(pieces[:, count:, :], TENSOR)
-    (plane,) = call(
-        grad_kernel,
-        (shape((far, features // near // far, width), bf16),),
-        (odd,),
-        pieces,
-        chunk,
-        flops=2 * near * count * WINDOW * width,
-    )
-    plane, d_out, sent = lax.optimization_barrier((plane, d_out, sent))
-    terms = lax.all_to_all(plane, FAR, 0, 0)
-
     blocks = []
     for step in range(1, tall):
         blocks.append(lax.ppermute(sent[step - 1], "yh", [(i, (i + step) % tall) for i in range(tall)]))
-    full_grad = lax.all_gather(d_out, TENSOR, axis=0, tiled=True)
-    d_attn = jnp.dot(full_grad, weight, preferred_element_type=f32).astype(bf16)
+    (d_attn,) = call(
+        d_attn_kernel, (shape((count, width), bf16),), (), full_grad, weight, flops=2 * count * features * width
+    )
     (mixed,) = call(mixed_kernel, (one,), (), own, *blocks)
     (w_grad,) = call(total_kernel, (shape((features // near // far, width), f32),), (), terms)
     return (mixed, d_attn, w_grad)

time: 93.8 us -> 93.9 us (level)
  blocking collectives: 33.6 us -> 52 us
  starting transfers between devices: 44.1 us -> 27.1 us
  waiting for transfers between devices: 1.58 us -> 5.15 us
  local copies, waits for them, and re-layouts: 3.34 us -> 0.9 us
  matrix products: 1.16 us -> 0 us
  Pallas kernels: 8.71 us -> 7.6 us
    all_to_all x0 -> x1, blocking collectives: none -> 22.7 us  [body(): pieces = lax.all_to_all(packed, NEAR, 0, 0)]
    all_gather x1 -> x0, blocking collectives: 16 us -> none  [body(): chunk = lax.all_gather(pieces[:, count:, :], TENSOR)]
    all_gather x1, blocking collectives: 17.7 us -> 29.2 us  [body(): full_grad = lax.all_gather(d_out, TENSOR, axis=0, tiled=True)]
    ppermute x1, starting transfers between devices: 13.8 us -> 4.37 us  [body(): arrived = lax.ppermute(send, 'core', [(0, 1), (1, 0)])]
    all_to_all x1 -> x0, starting transfers between devices: 5.86 us -> none  [body(): pieces = lax.all_to_all(packed, NEAR, 0, 0)]
    ppermute x3, waiting for transfers between devices: 0.01 us -> 3.91 us  [body(): lax.ppermute(sent[step - 1], 'yh', [(i, (i + step) % tall) for i in range...]
    all_to_all x1, starting transfers between devices: 12.9 us -> 10 us  [body(): terms = lax.all_to_all(plane, FAR, 0, 0)]
    unnamed x16 -> x6, local copies, waits for them, and re-layouts: 3.33 us -> 0.9 us
  transfers between devices with their start and end apart: 6 -> 5, of which waited for: 1 -> 2; matrix products, arithmetic and copies ran while one was open for 1% -> 0% of each run, Pallas kernels for 7% -> 6%
where the time goes in v5:
time: 93.9 us; the launch traced here: 93.4 us
  blocking collectives  52 us (55%)
  starting transfers between devices  27.1 us (29%)
  Pallas kernels  7.6 us (8%)
  waiting for transfers between devices  5.15 us (5%)
    all_gather x1, blocking collectives, body(): full_grad = lax.all_gather(d_out, TENSOR, axis=0, tiled=True)  29.2 us
    all_to_all x1, blocking collectives, body(): pieces = lax.all_to_all(packed, NEAR, 0, 0)  22.7 us
    ppermute x3, starting transfers between devices, body(): lax.ppermute(sent[step - 1], 'yh', [(i, (i + step) % tall) for i in range...  12.7 us
    all_to_all x1, starting transfers between devices, body(): terms = lax.all_to_all(plane, FAR, 0, 0)  10 us
    pallas_call x7, Pallas kernels, call(): pl.pallas_call(kernel, out_shape=outs, in_specs=specs, out_specs=tuple((p...  7.6 us
    ppermute x1, starting transfers between devices, body(): arrived = lax.ppermute(send, 'core', [(0, 1), (1, 0)])  4.37 us
    ppermute x3, waiting for transfers between devices, body(): lax.ppermute(sent[step - 1], 'yh', [(i, (i + step) % tall) for i in range...  3.91 us
  transfers between devices with their start and end apart: 5, of which 2 were waited for; matrix products, arithmetic and copies ran while one was open for 0% of the time, Pallas kernels for 6%

profile of v5, /device:TPU:1, one launch (start us, length us, event | category | flops | bytes accessed | tf_op | source)
XLA Modules:
  0.0 93.4 jit_solution(9508615326710051850)
XLA Ops:
  0.6 29.2 %all_gather.3.d_ref = bf16[128,2560]{1,0:T(8,128)(2,1)S(1)} all-gather(bf16[16,2560]{1,0:T(8,128)(2,1)} %param.5), channel_id=1, replica_groups=mesh['yl'=2,'x'=4,'z'=16,'yh'=4,'core'=2] {'yh','core'}, dimensions={0}, use_global_device_ids=true | all-gather | bytes 737280 | tf_op jit(solution)/shard_map/all_gather | solution.py:142
  29.9 0.0 copy-start.1
  29.9 0.9 copy-done.1
  30.8 0.1 shard_map.58
  30.9 22.7 %all_to_all.10.near_ref = bf16[8,256,384]{2,1,0:T(8,128)(2,1)S(1)} all-to-all(bf16[8,256,384]{2,1,0:T(8,128)(2,1)S(1)} %shard_map.58), channel_id=1, replica_groups=mesh['yl'=2,'x'=4,'z'=16,'yh'=4,'core'=2] {'yl','x'}, dimensions={0} | all-to-all | bytes 3145728 | tf_op jit(solution)/shard_map/all_to_all | solution.py:147
  53.7 0.0 copy-start
  53.7 1.3 %shard_map.59 = bf16[16,60,128]{2,1,0:T(8,128)(2,1)} custom-call(s32[1]{0:T(128)} %bitcast.1.odd_ref, bf16[8,256,384]{2,1,0:T(8,128)(2,1)S(1)} %all_to_all.10.near_ref), custom_call_target="tpu_custom_call" | custom-call | flops 301989888 | bytes 1818624 | tf_op jit(solution)/shard_map/pallas_call | solution.py:25
  55.0 10.0 %all-to-all-start.1 = ((bf16[16,60,128]{2,1,0:T(8,128)(2,1)}), bf16[16,60,128]{2,1,0:T(8,128)(2,1)S(1)}, u32[]{:S(2)}, u32[]{:S(2)}) async-start(bf16[16,60,128]{2,1,0:T(8,128)(2,1)} %shard_map.59), calls=%async_computation.1 | async-start | bytes 524288 | tf_op jit(solution)/shard_map/all_to_all | solution.py:159
  65.0 0.0 copy-done
  65.0 0.0 copy-done.2
  65.0 3.0 %shard_map.60 = (bf16[4,16,2560]{2,1,0:T(8,128)(2,1)S(1)}, bf16[4,16,2560]{2,1,0:T(8,128)(2,1)S(1)}) custom-call(s32[1]{0:T(128)} %bitcast.2.core_ref, bf16[128,384]{1,0:T(8,128)(2,1)S(1)} %copy-done.2, bf16[2560,384]{1,0:T(8,128)(2,1)S(1)} %copy-done), custom_call_target="tpu_custom_call" | custom-call | flops 503316480 | bytes 2719744 | tf_op jit(solution)/shard_map/pallas_call | solution.py:25
  68.0 4.4 %collective-permute-start = (bf16[4,16,2560]{2,1,0:T(8,128)(2,1)S(1)}, bf16[4,16,2560]{2,1,0:T(8,128)(2,1)S(1)}, u32[]{:S(2)}, u32[]{:S(2)}) collective-permute-start(bf16[4,16,2560]{2,1,0:T(8,128)(2,1)S(1)} %get-tuple-element.44), channel_id=1, source_target_pairs={{0,1},{1,0},{2,3},{3,2},{4,5},{5,4},{6,7},{7,6},{8,9},{9,8},{10,11... | collective-permute-start | bytes 983048 | tf_op jit(solution)/shard_map/ppermute | solution.py:165
  72.4 1.2 %collective-permute-done.arrived_ref = bf16[4,16,2560]{2,1,0:T(8,128)(2,1)S(1)} collective-permute-done((bf16[4,16,2560]{2,1,0:T(8,128)(2,1)S(1)}, bf16[4,16,2560]{2,1,0:T(8,128)(2,1)S(1)}, u32[]{:S(2)}, u32[]{:S(2)}) %collective-permute-start) | collective-permute-done | bytes 327712 | tf_op jit(solution)/shard_map/ppermute | solution.py:165
  73.6 0.1 shard_map.61
  73.7 2.8 %collective-permute-start.1 = (bf16[16,2560]{1,0:T(8,128)(2,1)S(1)}, bf16[16,2560]{1,0:T(8,128)(2,1)S(1)}, u32[]{:S(2)}, u32[]{:S(2)}) collective-permute-start(bf16[16,2560]{1,0:T(8,128)(2,1)S(1)} %get-tuple-element.46), channel_id=1, source_target_pairs={{0,2},{2,4},{4,6},{6,0},{1,3},{3,5},{5,7},{7,1},{8,10},{10,12},{12... | collective-permute-start | bytes 245768 | tf_op jit(solution)/shard_map/ppermute | solution.py:170
  76.4 4.7 %collective-permute-start.2 = (bf16[16,2560]{1,0:T(8,128)(2,1)S(1)}, bf16[16,2560]{1,0:T(8,128)(2,1)S(1)}, u32[]{:S(2)}, u32[]{:S(2)}) collective-permute-start(bf16[16,2560]{1,0:T(8,128)(2,1)S(1)} %get-tuple-element.47), channel_id=1, source_target_pairs={{0,4},{2,6},{4,0},{6,2},{1,5},{3,7},{5,1},{7,3},{8,12},{10,14},{12... | collective-permute-start | bytes 245768 | tf_op jit(solution)/shard_map/ppermute | solution.py:170
  81.2 5.2 %collective-permute-start.3 = (bf16[16,2560]{1,0:T(8,128)(2,1)S(1)}, bf16[16,2560]{1,0:T(8,128)(2,1)S(1)}, u32[]{:S(2)}, u32[]{:S(2)}) collective-permute-start(bf16[16,2560]{1,0:T(8,128)(2,1)S(1)} %get-tuple-element.48), channel_id=1, source_target_pairs={{0,6},{2,0},{4,2},{6,4},{1,7},{3,1},{5,3},{7,5},{8,14},{10,8},{12,... | collective-permute-start | bytes 245768 | tf_op jit(solution)/shard_map/ppermute | solution.py:170
  86.4 1.1 %shard_map.63 = bf16[128,384]{1,0:T(8,128)(2,1)} custom-call(bf16[128,2560]{1,0:T(8,128)(2,1)S(1)} %all_gather.3.d_ref, bf16[2560,384]{1,0:T(8,128)(2,1)S(1)} %copy-done), custom_call_target="tpu_custom_call" | custom-call | flops 251658240 | bytes 2719744 | tf_op jit(solution)/shard_map/pallas_call | solution.py:25
  87.6 0.0 collective-permute-done.1.a_ref
  87.6 0.0 collective-permute-done.2.b_ref
  87.6 3.9 %collective-permute-done.3.c_ref = bf16[16,2560]{1,0:T(8,128)(2,1)S(1)} collective-permute-done((bf16[16,2560]{1,0:T(8,128)(2,1)S(1)}, bf16[16,2560]{1,0:T(8,128)(2,1)S(1)}, u32[]{:S(2)}, u32[]{:S(2)}) %collective-permute-start.3) | collective-permute-done | bytes 81952 | tf_op jit(solution)/shard_map/ppermute | solution.py:170
  91.5 1.3 %shard_map.62 = bf16[16,2560]{1,0:T(8,128)(2,1)} custom-call(f32[16,2560]{1,0:T(8,128)S(1)} %get-tuple-element.45.own_ref, bf16[16,2560]{1,0:T(8,128)(2,1)S(1)} %collective-permute-done.1.a_ref, bf16[16,2560]{1,0:T(8,128)(2,1)S(1)} %collective-permute-done.2.b_ref, bf16[16,2560]{1,0:T(8,128)(2,1)S(1)} %collective-permute-done.3.c_ref), custom_call_target="tpu_custom_call" | custom-call | bytes 491520 | tf_op jit(solution)/shard_map/pallas_call | solution.py:25
  92.8 0.0 all-to-all-done.1.pieces_ref
  92.8 0.7 shard_map.64
  (1 shorter events, 0.0 us)
Async XLA Ops:
  29.9 0.9 copy-start.1
  53.7 11.3 %copy-start = (bf16[2560,384]{1,0:T(8,128)(2,1)S(1)}, bf16[2560,384]{1,0:T(8,128)(2,1)}, u32[]{:S(2)}) copy-start(bf16[2560,384]{1,0:T(8,128)(2,1)} %weight_ref.1) | copy-start | bytes 5898244
  53.7 11.3 %copy-start.2 = (bf16[128,384]{1,0:T(8,128)(2,1)S(1)}, bf16[128,384]{1,0:T(8,128)(2,1)}, u32[]{:S(2)}) copy-start(bf16[128,384]{1,0:T(8,128)(2,1)} %attn_ref.2) | copy-start | bytes 294916
  55.0 37.8 %all-to-all-start.1 = ((bf16[16,60,128]{2,1,0:T(8,128)(2,1)}), bf16[16,60,128]{2,1,0:T(8,128)(2,1)S(1)}, u32[]{:S(2)}, u32[]{:S(2)}) async-start(bf16[16,60,128]{2,1,0:T(8,128)(2,1)} %shard_map.59), calls=%async_computation.1 | async-start | bytes 524288 | tf_op jit(solution)/shard_map/all_to_all | solution.py:159
  68.0 5.6 %collective-permute-start = (bf16[4,16,2560]{2,1,0:T(8,128)(2,1)S(1)}, bf16[4,16,2560]{2,1,0:T(8,128)(2,1)S(1)}, u32[]{:S(2)}, u32[]{:S(2)}) collective-permute-start(bf16[4,16,2560]{2,1,0:T(8,128)(2,1)S(1)} %get-tuple-element.44), channel_id=1, source_target_pairs={{0,1},{1,0},{2,3},{3,2},{4,5},{5,4},{6,7},{7,6},{8,9},{9,8},{10,11... | collective-permute-start | bytes 983048 | tf_op jit(solution)/shard_map/ppermute | solution.py:165
  73.7 13.9 %collective-permute-start.1 = (bf16[16,2560]{1,0:T(8,128)(2,1)S(1)}, bf16[16,2560]{1,0:T(8,128)(2,1)S(1)}, u32[]{:S(2)}, u32[]{:S(2)}) collective-permute-start(bf16[16,2560]{1,0:T(8,128)(2,1)S(1)} %get-tuple-element.46), channel_id=1, source_target_pairs={{0,2},{2,4},{4,6},{6,0},{1,3},{3,5},{5,7},{7,1},{8,10},{10,12},{12... | collective-permute-start | bytes 245768 | tf_op jit(solution)/shard_map/ppermute | solution.py:170
  76.4 11.1 %collective-permute-start.2 = (bf16[16,2560]{1,0:T(8,128)(2,1)S(1)}, bf16[16,2560]{1,0:T(8,128)(2,1)S(1)}, u32[]{:S(2)}, u32[]{:S(2)}) collective-permute-start(bf16[16,2560]{1,0:T(8,128)(2,1)S(1)} %get-tuple-element.47), channel_id=1, source_target_pairs={{0,4},{2,6},{4,0},{6,2},{1,5},{3,7},{5,1},{7,3},{8,12},{10,14},{12... | collective-permute-start | bytes 245768 | tf_op jit(solution)/shard_map/ppermute | solution.py:170
  81.2 10.3 %collective-permute-start.3 = (bf16[16,2560]{1,0:T(8,128)(2,1)S(1)}, bf16[16,2560]{1,0:T(8,128)(2,1)S(1)}, u32[]{:S(2)}, u32[]{:S(2)}) collective-permute-start(bf16[16,2560]{1,0:T(8,128)(2,1)S(1)} %get-tuple-element.48), channel_id=1, source_target_pairs={{0,6},{2,0},{4,2},{6,4},{1,7},{3,1},{5,3},{7,5},{8,14},{10,8},{12,... | collective-permute-start | bytes 245768 | tf_op jit(solution)/shard_map/ppermute | solution.py:170

commit v6 on v3

--- a/solution.py
+++ b/solution.py
@@ -12,7 +12,7 @@
 FAR = "z"
 CHUNKS = 8
 WINDOW = 384
-VMEM_LIMIT = 40 * 1024 * 1024
+VMEM_LIMIT = 16 * 1024 * 1024
 
 code_offset = 6.0
 bf16, f32 = jnp.bfloat16, jnp.float32
@@ -53,12 +53,44 @@
     return turned * (BLK**-0.5)
 
 
-def pack_kernel(attn_ref, d_ref, out_ref):
-    count = attn_ref.shape[0]
+def pack_kernel(attn_ref, d_ref, out_ref, attn_here, d_here, sems):
+    count, rows = attn_here.shape[0], d_here.shape[0]
+    first = pltpu.make_async_copy(attn_ref, attn_here, sems.at[0])
+    second = pltpu.make_async_copy(d_ref, d_here, sems.at[1])
+    first.start()
+    second.start()
+    copies = []
     for i in range(CHUNKS):
-        out_ref[i, :count, :] = attn_ref[...]
-        start = i * 320 // BLK * BLK
-        out_ref[i, count:, :] = d_ref[:, start : start + WINDOW]
+        copies.append((attn_here, out_ref.at[i, pl.ds(0, count), :]))
+    for i in range(CHUNKS):
+        window = d_here.at[:, pl.ds(i * 320 // BLK * BLK, WINDOW)]
+        copies.append((window, out_ref.at[i, pl.ds(count, rows), :]))
+    copies = [pltpu.make_async_copy(a, b, sems.at[2 + k]) for k, (a, b) in enumerate(copies)]
+    first.wait()
+    for copy in copies[:CHUNKS]:
+        copy.start()
+    second.wait()
+    for copy in copies[CHUNKS:]:
+        copy.start()
+    for copy in copies:
+        copy.wait()
+
+
+def pack(attn, d_out):
+    out = shape((CHUNKS, attn.shape[0] + d_out.shape[0], attn.shape[1]), bf16)
+    return pl.pallas_call(
+        pack_kernel,
+        out_shape=out,
+        in_specs=[pl.BlockSpec(memory_space=pltpu.HBM)] * 2,
+        out_specs=pl.BlockSpec(memory_space=pltpu.HBM),
+        scratch_shapes=[
+            pltpu.VMEM(attn.shape, bf16),
+            pltpu.VMEM(d_out.shape, bf16),
+            pltpu.SemaphoreType.DMA((2 + 2 * CHUNKS,)),
+        ],
+        compiler_params=pltpu.CompilerParams(vmem_limit_bytes=VMEM_LIMIT),
+        cost_estimate=pl.CostEstimate(flops=0, bytes_accessed=3 * out.size, transcendentals=0),
+    )(attn, d_out)
 
 
 def values_kernel(core_ref, attn_ref, weight_ref, keep_ref, send_ref):
@@ -81,22 +113,28 @@
         send_ref[:, :, cols] = jnp.where(first, one, zero).astype(bf16)
 
 
-def pair_kernel(me_ref, keep_ref, arrived_ref, own_ref, *sent_refs):
-    tall = keep_ref.shape[0]
+def pair_kernel(me_ref, keep_ref, arrived_ref, d_ref, own_ref, *sent_refs):
+    tall, rows = keep_ref.shape[:2]
     me = me_ref[0]
     own_ref[...] = keep_ref[me].astype(f32) + arrived_ref[me].astype(f32)
     for step in range(1, tall):
         other = lax.rem(me + step, tall)
         total = keep_ref[other].astype(f32) + arrived_ref[other].astype(f32)
-        sent_refs[step - 1][...] = total.astype(bf16)
-
-
-def mixed_kernel(own_ref, a_ref, b_ref, c_ref, out_ref):
+        sent_refs[step - 1][:rows, :] = total.astype(bf16)
+        sent_refs[step - 1][rows:, :] = d_ref[...]
+
+
+def mixed_kernel(me_ref, own_ref, d_ref, a_ref, b_ref, c_ref, out_ref, half_ref):
     table = signs_table()
+    tall, rows = half_ref.shape[:2]
+    me = me_ref[0]
+    half_ref[me] = d_ref[...]
+    for step, ref in ((1, a_ref), (2, b_ref), (3, c_ref)):
+        half_ref[lax.rem(me + tall - step, tall)] = ref[rows:, :]
     for j in range(out_ref.shape[1] // BLK):
         cols = slice(j * BLK, (j + 1) * BLK)
-        total = own_ref[:, cols] + a_ref[:, cols].astype(f32)
-        total += b_ref[:, cols].astype(f32) + c_ref[:, cols].astype(f32)
+        total = own_ref[:, cols] + a_ref[:rows, cols].astype(f32)
+        total += b_ref[:rows, cols].astype(f32) + c_ref[:rows, cols].astype(f32)
         out_ref[:, cols] = rotate(total, table).astype(bf16)
 
 
@@ -106,15 +144,32 @@
     left = jnp.concatenate([d_ref[:, p].reshape(count, WINDOW) for p in range(near)], axis=0)
     right = jnp.concatenate([near_ref[p, :count, :] for p in range(near)], axis=0)
     term = lax.dot_general(left, right, (((0,), (0,)), ((), ())), preferred_element_type=f32)
-    far, size = out_ref.shape[0], out_ref.shape[1]
+    far, size = out_ref.shape[0], out_ref.shape[1] * BLK // term.shape[1]
     chunk = far * size
     term = jnp.where(odd_ref[0] == 1, term[WINDOW - chunk :, :], term[:chunk, :])
     for z in range(far):
-        out_ref[z] = term[z * size : (z + 1) * size, :].astype(bf16)
+        block = term[z * size : (z + 1) * size, :]
+        parts = [block[:, c : c + BLK] for c in range(0, term.shape[1], BLK)]
+        out_ref[z] = jnp.concatenate(parts, axis=0).astype(bf16)
+
+
+def d_attn_kernel(core_ref, half_ref, other_ref, weight_ref, out_ref):
+    tall, _, rows, width = out_ref.shape
+    first = core_ref[0] == 0
+    mine, theirs = half_ref[...], other_ref[...]
+    zero = jnp.where(first, mine, theirs).reshape(tall * rows, -1)
+    one = jnp.where(first, theirs, mine).reshape(tall * rows, -1)
+    both = jnp.concatenate([zero, one], axis=0)
+    product = jnp.dot(both, weight_ref[...], preferred_element_type=f32).astype(bf16)
+    out_ref[:, 0] = product[: tall * rows].reshape(tall, rows, width)
+    out_ref[:, 1] = product[tall * rows :].reshape(tall, rows, width)
 
 
 def total_kernel(pieces_ref, out_ref):
-    out_ref[...] = jnp.sum(pieces_ref[...].astype(f32), axis=0)
+    total = jnp.sum(pieces_ref[...].astype(f32), axis=0)
+    size = out_ref.shape[0]
+    for c in range(out_ref.shape[1] // BLK):
+        out_ref[:, c * BLK : (c + 1) * BLK] = total[c * size : (c + 1) * size, :]
 
 
 def shape(dims, dtype):
@@ -130,7 +185,7 @@
     yh, core = lax.axis_index("yh"), lax.axis_index("core")
     odd = lax.rem(lax.axis_index("x"), 2)
 
-    (packed,) = call(pack_kernel, (shape((near, count + rows, width), bf16),), (), attn, d_out)
+    packed = pack(attn, d_out)
     packed, attn = lax.optimization_barrier((packed, attn))
     pieces = lax.all_to_all(packed, NEAR, 0, 0)
 
@@ -139,28 +194,39 @@
         values_kernel, (half, half), (core,), attn, weight, flops=2 * count * features * (width + 3 * BLK)
     )
     arrived = lax.ppermute(send, "core", [(0, 1), (1, 0)])
-    one = shape((rows, features), bf16)
-    own, *sent = call(pair_kernel, (shape((rows, features), f32), one, one, one), (yh,), keep, arrived)
-
-    pieces, own = lax.optimization_barrier((pieces, own))
+    one, two = shape((rows, features), bf16), shape((2 * rows, features), bf16)
+    own, *sent = call(
+        pair_kernel, (shape((rows, features), f32), two, two, two), (yh,), keep, arrived, d_out
+    )
+    rings = [[(i, (i + step) % tall) for i in range(tall)] for step in range(tall)]
+    first = lax.ppermute(sent[0], "yh", rings[1])
+
+    pieces, first, sent = lax.optimization_barrier((pieces, first, sent))
     chunk = lax.all_gather(pieces[:, count:, :], TENSOR)
     (plane,) = call(
         grad_kernel,
-        (shape((far, features // near // far, width), bf16),),
+        (shape((far, features // near // far * width // BLK, BLK), bf16),),
         (odd,),
         pieces,
         chunk,
         flops=2 * near * count * WINDOW * width,
     )
-    plane, d_out, sent = lax.optimization_barrier((plane, d_out, sent))
+    plane, sent = lax.optimization_barrier((plane, sent))
     terms = lax.all_to_all(plane, FAR, 0, 0)
 
-    blocks = []
-    for step in range(1, tall):
-        blocks.append(lax.ppermute(sent[step - 1], "yh", [(i, (i + step) % tall) for i in range(tall)]))
-    full_grad = lax.all_gather(d_out, TENSOR, axis=0, tiled=True)
-    d_attn = jnp.dot(full_grad, weight, preferred_element_type=f32).astype(bf16)
-    (mixed,) = call(mixed_kernel, (one,), (), own, *blocks)
+    blocks = [first] + [lax.ppermute(sent[step - 1], "yh", rings[step]) for step in range(2, tall)]
+    mixed, mine = call(mixed_kernel, (one, half), (yh,), own, d_out, *blocks)
+    theirs = lax.ppermute(mine, "core", [(0, 1), (1, 0)])
+    (d_attn,) = call(
+        d_attn_kernel,
+        (shape((tall, group // tall, rows, width), bf16),),
+        (core,),
+        mine,
+        theirs,
+        weight,
+        flops=2 * count * features * width,
+    )
+    d_attn = d_attn.reshape(count, width)
     (w_grad,) = call(total_kernel, (shape((features // near // far, width), f32),), (), terms)
     return (mixed, d_attn, w_grad)
 

time: 93.8 us -> 102 us (1.087)
  waiting for transfers between devices: 1.58 us -> 23.1 us
  blocking collectives: 33.6 us -> 17.4 us
  Pallas kernels: 8.71 us -> 11.2 us
  matrix products: 1.16 us -> 0 us
    ppermute x3 -> x4, waiting for transfers between devices: 0.01 us -> 21.6 us  [the longest x2 12.6 us: body(): lax.ppermute(sent[step - 1], 'yh', rings[step])]
    all_gather x1 -> x0, blocking collectives: 17.7 us -> none  [body(): full_grad = lax.all_gather(d_out, TENSOR, axis=0, tiled=True)]
    pallas_call x0 -> x1, Pallas kernels: none -> 1.46 us  [pack(): pl.pallas_call(pack_kernel, out_shape=out, in_specs=[pl.BlockSpec(memory_...]
    all_gather x1, blocking collectives: 16 us -> 17.4 us  [body(): chunk = lax.all_gather(pieces[:, count:, :], TENSOR)]
    dot_general x1 -> x0, matrix products: 1.16 us -> none  [body(): d_attn = jnp.dot(full_grad, weight, preferred_element_type=f32).astype(bf16)]
    pallas_call x6, Pallas kernels: 8.71 us -> 9.78 us  [call(): pl.pallas_call(kernel, out_shape=outs, in_specs=specs, out_specs=tuple((p...]
    unnamed x16 -> x18, local copies, waits for them, and re-layouts: 3.33 us -> 4.05 us
    ppermute x3 -> x4, starting transfers between devices: 11.6 us -> 12 us  [the longest x2 7.6 us: body(): lax.ppermute(sent[step - 1], 'yh', rings[step])]
  transfers between devices with their start and end apart: 6 -> 7, of which waited for: 1 -> 5; matrix products, arithmetic and copies ran while one was open for 1% -> 0% of each run, Pallas kernels for 7% -> 8%
where the time goes in v6:
time: 102 us
  starting transfers between devices  45.1 us (44%)
  waiting for transfers between devices  23.1 us (23%)
  blocking collectives  17.4 us (17%)
  Pallas kernels  11.2 us (11%)
  local copies, waits for them, and re-layouts  4.06 us (4%)
    all_gather x1, blocking collectives, body(): chunk = lax.all_gather(pieces[:, count:, :], TENSOR)  17.4 us
    ppermute x1, starting transfers between devices, body(): arrived = lax.ppermute(send, 'core', [(0, 1), (1, 0)])  13.8 us
    all_to_all x1, starting transfers between devices, body(): terms = lax.all_to_all(plane, FAR, 0, 0)  13.3 us
    ppermute x2, waiting for transfers between devices, body(): lax.ppermute(sent[step - 1], 'yh', rings[step])  12.6 us
    pallas_call x6, Pallas kernels, call(): pl.pallas_call(kernel, out_shape=outs, in_specs=specs, out_specs=tuple((p...  9.78 us
    ppermute x1, waiting for transfers between devices, body(): first = lax.ppermute(sent[0], 'yh', rings[1])  7.74 us
    ppermute x2, starting transfers between devices, body(): lax.ppermute(sent[step - 1], 'yh', rings[step])  7.6 us
    all_to_all x1, starting transfers between devices, body(): pieces = lax.all_to_all(packed, NEAR, 0, 0)  5.99 us
  transfers between devices with their start and end apart: 7, of which 5 were waited for; matrix products, arithmetic and copies ran while one was open for 0% of the time, Pallas kernels for 8%

profile of v6, /device:TPU:1, one launch (start us, length us, event | category | flops | bytes accessed | tf_op | source)
XLA Modules:
  0.0 101.7 jit_solution(17125520428472242335)
XLA Ops:
  0.6 0.9 copy-done.2
  1.5 0.9 copy-done.4
  2.4 1.5 %shard_map.58 = bf16[8,144,384]{2,1,0:T(8,128)(2,1)S(1)} custom-call(bf16[128,384]{1,0:T(8,128)(2,1)S(1)} %copy-done.4, bf16[16,2560]{1,0:T(8,128)(2,1)S(1)} %copy-done.2), custom_call_target="tpu_custom_call" | custom-call | bytes 1327104 | tf_op jit(solution)/shard_map/pallas_call | solution.py:81
  3.9 0.9 copy-done.1
  4.8 6.0 %all-to-all-start = ((bf16[8,144,384]{2,1,0:T(8,128)(2,1)}), bf16[8,144,384]{2,1,0:T(8,128)(2,1)S(1)}, u32[]{:S(2)}, u32[]{:S(2)}) async-start(bf16[8,144,384]{2,1,0:T(8,128)(2,1)} %copy-done.1), calls=%async_computation | async-start | bytes 1769472 | tf_op jit(solution)/shard_map/all_to_all | solution.py:190
  10.8 3.7 %shard_map.59 = (bf16[4,16,2560]{2,1,0:T(8,128)(2,1)S(1)}, bf16[4,16,2560]{2,1,0:T(8,128)(2,1)}) custom-call(s32[1]{0:T(128)} %bitcast.1.core_ref, bf16[128,384]{1,0:T(8,128)(2,1)S(1)} %copy-done.5, bf16[2560,384]{1,0:T(8,128)(2,1)S(1)} %copy-done), custom_call_target="tpu_custom_call" | custom-call | flops 503316480 | bytes 2719744 | tf_op jit(solution)/shard_map/pallas_call | solution.py:25
  14.5 13.8 %collective-permute-start = (bf16[4,16,2560]{2,1,0:T(8,128)(2,1)}, bf16[4,16,2560]{2,1,0:T(8,128)(2,1)}, u32[]{:S(2)}, u32[]{:S(2)}) collective-permute-start(bf16[4,16,2560]{2,1,0:T(8,128)(2,1)} %get-tuple-element.22), channel_id=1, source_target_pairs={{0,1},{1,0},{2,3},{3,2},{4,5},{5,4},{6,7},{7,6},{8,9},{9,8},{10,11... | collective-permute-start | bytes 983048 | tf_op jit(solution)/shard_map/ppermute | solution.py:196
  28.3 1.6 %collective-permute-done.arrived_ref = bf16[4,16,2560]{2,1,0:T(8,128)(2,1)} collective-permute-done((bf16[4,16,2560]{2,1,0:T(8,128)(2,1)}, bf16[4,16,2560]{2,1,0:T(8,128)(2,1)}, u32[]{:S(2)}, u32[]{:S(2)}) %collective-permute-start) | collective-permute-done | bytes 327712 | tf_op jit(solution)/shard_map/ppermute | solution.py:196
  29.8 1.7 %shard_map.60 = (f32[16,2560]{1,0:T(8,128)S(1)}, bf16[32,2560]{1,0:T(8,128)(2,1)}, bf16[32,2560]{1,0:T(8,128)(2,1)S(1)}, bf16[32,2560]{1,0:T(8,128)(2,1)S(1)}) custom-call(s32[1]{0:T(128)} %bitcast.me_ref, bf16[4,16,2560]{2,1,0:T(8,128)(2,1)S(1)} %get-tuple-element.21.keep_ref, bf16[4,16,2560]{2,1,0:T(8,128)(2,1)} %collective-permute-done.arrived_ref, ...), custom_call_target="tpu_custom_call" | custom-call | bytes 1392640 | tf_op jit(solution)/shard_map/pallas_call | solution.py:25
  31.5 0.7 copy-done.6
  32.2 0.7 copy-done.8
  32.9 2.0 %collective-permute-start.1 = (bf16[32,2560]{1,0:T(8,128)(2,1)}, bf16[32,2560]{1,0:T(8,128)(2,1)S(1)}, u32[]{:S(2)}, u32[]{:S(2)}) collective-permute-start(bf16[32,2560]{1,0:T(8,128)(2,1)} %get-tuple-element.25), channel_id=1, source_target_pairs={{0,2},{2,4},{4,6},{6,0},{1,3},{3,5},{5,7},{7,1},{8,10},{10,12},{12... | collective-permute-start | bytes 491528 | tf_op jit(solution)/shard_map/ppermute | solution.py:202
  34.9 7.7 %collective-permute-done.1.a_ref = bf16[32,2560]{1,0:T(8,128)(2,1)S(1)} collective-permute-done((bf16[32,2560]{1,0:T(8,128)(2,1)}, bf16[32,2560]{1,0:T(8,128)(2,1)S(1)}, u32[]{:S(2)}, u32[]{:S(2)}) %collective-permute-start.1) | collective-permute-done | bytes 163872 | tf_op jit(solution)/shard_map/ppermute | solution.py:202
  42.7 17.4 %all-gather = bf16[64,16,384]{2,1,0:T(8,128)(2,1)S(1)} all-gather(bf16[8,16,384]{2,1,0:T(8,128)(2,1)S(1)} %slice.3), channel_id=2, replica_groups=mesh['yl'=2,'x'=4,'z'=16,'yh'=4,'core'=2] {'yh','core'}, dimensions={0}, use_global_device_ids=true | all-gather | bytes 884736 | tf_op jit(solution)/shard_map/all_gather | solution.py:205
  60.1 1.3 %shard_map.61 = bf16[16,60,128]{2,1,0:T(8,128)(2,1)} custom-call(s32[1]{0:T(128)} %bitcast.2.odd_ref, bf16[8,144,384]{2,1,0:T(8,128)(2,1)S(1)} %all-to-all-done.near_ref, bf16[8,8,16,384]{3,2,1,0:T(8,128)(2,1)S(1)} %bitcast.5), custom_call_target="tpu_custom_call" | custom-call | flops 301989888 | bytes 1916928 | tf_op jit(solution)/shard_map/pallas_call | solution.py:25
  61.4 13.3 %all-to-all-start.1 = ((bf16[16,60,128]{2,1,0:T(8,128)(2,1)}), bf16[16,60,128]{2,1,0:T(8,128)(2,1)S(1)}, u32[]{:S(2)}, u32[]{:S(2)}) async-start(bf16[16,60,128]{2,1,0:T(8,128)(2,1)} %shard_map.61), calls=%async_computation.1 | async-start | bytes 524288 | tf_op jit(solution)/shard_map/all_to_all | solution.py:215
  74.7 5.2 %collective-permute-start.2 = (bf16[32,2560]{1,0:T(8,128)(2,1)}, bf16[32,2560]{1,0:T(8,128)(2,1)S(1)}, u32[]{:S(2)}, u32[]{:S(2)}) collective-permute-start(bf16[32,2560]{1,0:T(8,128)(2,1)} %copy-done.8), channel_id=1, source_target_pairs={{0,4},{2,6},{4,0},{6,2},{1,5},{3,7},{5,1},{7,3},{8,12},{10,14},{12... | collective-permute-start | bytes 491528 | tf_op jit(solution)/shard_map/ppermute | solution.py:217
  79.9 2.4 %collective-permute-start.3 = (bf16[32,2560]{1,0:T(8,128)(2,1)S(1)}, bf16[32,2560]{1,0:T(8,128)(2,1)S(1)}, u32[]{:S(2)}, u32[]{:S(2)}) collective-permute-start(bf16[32,2560]{1,0:T(8,128)(2,1)S(1)} %get-tuple-element.33), channel_id=1, source_target_pairs={{0,6},{2,0},{4,2},{6,4},{1,7},{3,1},{5,3},{7,5},{8,14},{10,8},{12,... | collective-permute-start | bytes 491528 | tf_op jit(solution)/shard_map/ppermute | solution.py:217
  82.3 7.8 %collective-permute-done.2.b_ref = bf16[32,2560]{1,0:T(8,128)(2,1)S(1)} collective-permute-done((bf16[32,2560]{1,0:T(8,128)(2,1)}, bf16[32,2560]{1,0:T(8,128)(2,1)S(1)}, u32[]{:S(2)}, u32[]{:S(2)}) %collective-permute-start.2) | collective-permute-done | bytes 163872 | tf_op jit(solution)/shard_map/ppermute | solution.py:217
  90.1 4.8 %collective-permute-done.3.c_ref = bf16[32,2560]{1,0:T(8,128)(2,1)S(1)} collective-permute-done((bf16[32,2560]{1,0:T(8,128)(2,1)S(1)}, bf16[32,2560]{1,0:T(8,128)(2,1)S(1)}, u32[]{:S(2)}, u32[]{:S(2)}) %collective-permute-start.3) | collective-permute-done | bytes 163872 | tf_op jit(solution)/shard_map/ppermute | solution.py:217
  94.9 1.3 %shard_map.62 = (bf16[16,2560]{1,0:T(8,128)(2,1)}, bf16[4,16,2560]{2,1,0:T(8,128)(2,1)S(1)}) custom-call(s32[1]{0:T(128)} %bitcast.me_ref, f32[16,2560]{1,0:T(8,128)S(1)} %copy-done.7, bf16[16,2560]{1,0:T(8,128)(2,1)S(1)} %copy-done.3, bf16[32,2560]{1,0:T(8,128)(2,1)S(1)} %collective-permute-done.1.a_ref, bf16[32,2560]{1,0:T(8,128)(2,1)S(1)} %collective-permute-done.2.b_ref, ...), custom_call_target="tpu_custom_call" | custom-call | bytes 1146880 | tf_op jit(solution)/shard_map/pallas_call | solution.py:25
  96.2 2.4 %collective-permute-start.4 = (bf16[4,16,2560]{2,1,0:T(8,128)(2,1)S(1)}, bf16[4,16,2560]{2,1,0:T(8,128)(2,1)S(1)}, u32[]{:S(2)}, u32[]{:S(2)}) collective-permute-start(bf16[4,16,2560]{2,1,0:T(8,128)(2,1)S(1)} %get-tuple-element.35.half_ref), channel_id=1, source_target_pairs={{0,1},{1,0},{2,3},{3,2},{4,5},{5,4},{6,7},{7,6},{8,9},{9,8},{10,11... | collective-permute-start | bytes 983048 | tf_op jit(solution)/shard_map/ppermute | solution.py:219
  98.6 1.2 %collective-permute-done.4.other_ref = bf16[4,16,2560]{2,1,0:T(8,128)(2,1)S(1)} collective-permute-done((bf16[4,16,2560]{2,1,0:T(8,128)(2,1)S(1)}, bf16[4,16,2560]{2,1,0:T(8,128)(2,1)S(1)}, u32[]{:S(2)}, u32[]{:S(2)}) %collective-permute-start.4) | collective-permute-done | bytes 327712 | tf_op jit(solution)/shard_map/ppermute | solution.py:219
  99.9 1.1 %shard_map.63 = bf16[4,2,16,384]{3,2,1,0:T(8,128)(2,1)} custom-call(s32[1]{0:T(128)} %bitcast.1.core_ref, bf16[4,16,2560]{2,1,0:T(8,128)(2,1)S(1)} %get-tuple-element.35.half_ref, bf16[4,16,2560]{2,1,0:T(8,128)(2,1)S(1)} %collective-permute-done.4.other_ref, bf16[2560,384]{1,0:T(8,128)(2,1)S(1)} %copy-done), custom_call_target="tpu_custom_call" | custom-call | flops 251658240 | bytes 2719744 | tf_op jit(solution)/shard_map/pallas_call | solution.py:25
  (17 shorter events, 0.7 us)
Async XLA Ops:
  0.6 0.9 copy-start.2
  1.5 0.9 copy-start.4
  2.4 8.4 %copy-start = (bf16[2560,384]{1,0:T(8,128)(2,1)S(1)}, bf16[2560,384]{1,0:T(8,128)(2,1)}, u32[]{:S(2)}) copy-start(bf16[2560,384]{1,0:T(8,128)(2,1)} %weight_ref.3) | copy-start | bytes 5898244
  2.4 8.4 %copy-start.5 = (bf16[128,384]{1,0:T(8,128)(2,1)S(1)}, bf16[128,384]{1,0:T(8,128)(2,1)}, u32[]{:S(2)}) copy-start(bf16[128,384]{1,0:T(8,128)(2,1)} %attn_ref.2) | copy-start | bytes 294916
  3.9 0.9 copy-start.1
  4.8 25.0 %copy-start.3 = (bf16[16,2560]{1,0:T(8,128)(2,1)S(1)}, bf16[16,2560]{1,0:T(8,128)(2,1)}, u32[]{:S(2)}) copy-start(bf16[16,2560]{1,0:T(8,128)(2,1)} %d_ref.5) | copy-start | bytes 245764
  4.8 37.9 %all-to-all-start = ((bf16[8,144,384]{2,1,0:T(8,128)(2,1)}), bf16[8,144,384]{2,1,0:T(8,128)(2,1)S(1)}, u32[]{:S(2)}, u32[]{:S(2)}) async-start(bf16[8,144,384]{2,1,0:T(8,128)(2,1)} %copy-done.1), calls=%async_computation | async-start | bytes 1769472 | tf_op jit(solution)/shard_map/all_to_all | solution.py:190
  14.5 15.3 %collective-permute-start = (bf16[4,16,2560]{2,1,0:T(8,128)(2,1)}, bf16[4,16,2560]{2,1,0:T(8,128)(2,1)}, u32[]{:S(2)}, u32[]{:S(2)}) collective-permute-start(bf16[4,16,2560]{2,1,0:T(8,128)(2,1)} %get-tuple-element.22), channel_id=1, source_target_pairs={{0,1},{1,0},{2,3},{3,2},{4,5},{5,4},{6,7},{7,6},{8,9},{9,8},{10,11... | collective-permute-start | bytes 983048 | tf_op jit(solution)/shard_map/ppermute | solution.py:196
  31.5 0.7 copy-start.6
  32.2 0.7 copy-start.8
  32.9 62.1 %copy-start.7 = (f32[16,2560]{1,0:T(8,128)S(1)}, f32[16,2560]{1,0:T(8,128)}, u32[]{:S(2)}) copy-start(f32[16,2560]{1,0:T(8,128)} %copy-done.6) | copy-start | bytes 491524
  32.9 9.8 %collective-permute-start.1 = (bf16[32,2560]{1,0:T(8,128)(2,1)}, bf16[32,2560]{1,0:T(8,128)(2,1)S(1)}, u32[]{:S(2)}, u32[]{:S(2)}) collective-permute-start(bf16[32,2560]{1,0:T(8,128)(2,1)} %get-tuple-element.25), channel_id=1, source_target_pairs={{0,2},{2,4},{4,6},{6,0},{1,3},{3,5},{5,7},{7,1},{8,10},{10,12},{12... | collective-permute-start | bytes 491528 | tf_op jit(solution)/shard_map/ppermute | solution.py:202
  61.4 39.7 %all-to-all-start.1 = ((bf16[16,60,128]{2,1,0:T(8,128)(2,1)}), bf16[16,60,128]{2,1,0:T(8,128)(2,1)S(1)}, u32[]{:S(2)}, u32[]{:S(2)}) async-start(bf16[16,60,128]{2,1,0:T(8,128)(2,1)} %shard_map.61), calls=%async_computation.1 | async-start | bytes 524288 | tf_op jit(solution)/shard_map/all_to_all | solution.py:215
  74.7 15.4 %collective-permute-start.2 = (bf16[32,2560]{1,0:T(8,128)(2,1)}, bf16[32,2560]{1,0:T(8,128)(2,1)S(1)}, u32[]{:S(2)}, u32[]{:S(2)}) collective-permute-start(bf16[32,2560]{1,0:T(8,128)(2,1)} %copy-done.8), channel_id=1, source_target_pairs={{0,4},{2,6},{4,0},{6,2},{1,5},{3,7},{5,1},{7,3},{8,12},{10,14},{12... | collective-permute-start | bytes 491528 | tf_op jit(solution)/shard_map/ppermute | solution.py:217
  79.9 15.0 %collective-permute-start.3 = (bf16[32,2560]{1,0:T(8,128)(2,1)S(1)}, bf16[32,2560]{1,0:T(8,128)(2,1)S(1)}, u32[]{:S(2)}, u32[]{:S(2)}) collective-permute-start(bf16[32,2560]{1,0:T(8,128)(2,1)S(1)} %get-tuple-element.33), channel_id=1, source_target_pairs={{0,6},{2,0},{4,2},{6,4},{1,7},{3,1},{5,3},{7,5},{8,14},{10,8},{12,... | collective-permute-start | bytes 491528 | tf_op jit(solution)/shard_map/ppermute | solution.py:217
  96.2 3.6 %collective-permute-start.4 = (bf16[4,16,2560]{2,1,0:T(8,128)(2,1)S(1)}, bf16[4,16,2560]{2,1,0:T(8,128)(2,1)S(1)}, u32[]{:S(2)}, u32[]{:S(2)}) collective-permute-start(bf16[4,16,2560]{2,1,0:T(8,128)(2,1)S(1)} %get-tuple-element.35.half_ref), channel_id=1, source_target_pairs={{0,1},{1,0},{2,3},{3,2},{4,5},{5,4},{6,7},{7,6},{8,9},{9,8},{10,11... | collective-permute-start | bytes 983048 | tf_op jit(solution)/shard_map/ppermute | solution.py:219

commit v7 on v5

--- a/solution.py
+++ b/solution.py
@@ -12,7 +12,7 @@
 FAR = "z"
 CHUNKS = 8
 WINDOW = 384
-VMEM_LIMIT = 40 * 1024 * 1024
+VMEM_LIMIT = 16 * 1024 * 1024
 
 code_offset = 6.0
 bf16, f32 = jnp.bfloat16, jnp.float32
@@ -141,13 +141,22 @@
 
     full_grad = lax.all_gather(d_out, TENSOR, axis=0, tiled=True)
     (packed,) = call(pack_kernel, (shape((near, 2 * count, width), bf16),), (), attn, full_grad)
-    packed, attn, full_grad, weight, odd, yh, core = lax.optimization_barrier(
-        (packed, attn, full_grad, weight, odd, yh, core)
+    packed, attn = lax.optimization_barrier((packed, attn))
+    pieces = lax.all_to_all(packed, NEAR, 0, 0)
+
+    (d_attn,) = call(
+        d_attn_kernel, (shape((count, width), bf16),), (), full_grad, weight, flops=2 * count * features * width
     )
-    pieces = lax.all_to_all(packed, NEAR, 0, 0)
-    pieces, attn, full_grad, weight, odd, yh, core = lax.optimization_barrier(
-        (pieces, attn, full_grad, weight, odd, yh, core)
+    attn, d_attn = lax.optimization_barrier((attn, d_attn))
+    half = shape((tall, rows, features), bf16)
+    keep, send = call(
+        values_kernel, (half, half), (core,), attn, weight, flops=2 * count * features * (width + 3 * BLK)
     )
+    arrived = lax.ppermute(send, "core", [(0, 1), (1, 0)])
+    one = shape((rows, features), bf16)
+    own, *sent = call(pair_kernel, (shape((rows, features), f32), one, one, one), (yh,), keep, arrived)
+
+    pieces, sent, d_attn = lax.optimization_barrier((pieces, sent, d_attn))
     (plane,) = call(
         grad_kernel,
         (shape((far, features // near // far * width // BLK, BLK), bf16),),
@@ -155,22 +164,12 @@
         pieces,
         flops=2 * near * count * WINDOW * width,
     )
-    plane, attn, full_grad, core = lax.optimization_barrier((plane, attn, full_grad, core))
+    plane, sent = lax.optimization_barrier((plane, sent))
     terms = lax.all_to_all(plane, FAR, 0, 0)
 
-    half = shape((tall, rows, features), bf16)
-    keep, send = call(
-        values_kernel, (half, half), (core,), attn, weight, flops=2 * count * features * (width + 3 * BLK)
-    )
-    arrived = lax.ppermute(send, "core", [(0, 1), (1, 0)])
-    one = shape((rows, features), bf16)
-    own, *sent = call(pair_kernel, (shape((rows, features), f32), one, one, one), (yh,), keep, arrived)
     blocks = []
     for step in range(1, tall):
         blocks.append(lax.ppermute(sent[step - 1], "yh", [(i, (i + step) % tall) for i in range(tall)]))
-    (d_attn,) = call(
-        d_attn_kernel, (shape((count, width), bf16),), (), full_grad, weight, flops=2 * count * features * width
-    )
     (mixed,) = call(mixed_kernel, (one,), (), own, *blocks)
     (w_grad,) = call(total_kernel, (shape((features // near // far, width), f32),), (), terms)
     return (mixed, d_attn, w_grad)

time: 93.9 us -> 88.9 us (0.947)
  blocking collectives: 52 us -> 29.2 us
  waiting for transfers between devices: 5.15 us -> 16.5 us
  local copies, waits for them, and re-layouts: 0.9 us -> 5.67 us
    all_to_all x1 -> x0, blocking collectives: 22.7 us -> none  [body(): pieces = lax.all_to_all(packed, NEAR, 0, 0)]
    all_to_all x0 -> x1, waiting for transfers between devices: none -> 9.13 us  [body(): pieces = lax.all_to_all(packed, NEAR, 0, 0)]
    unnamed x6 -> x16, local copies, waits for them, and re-layouts: 0.9 us -> 5.67 us
    all_to_all x0 -> x1, starting transfers between devices: none -> 3.71 us  [body(): pieces = lax.all_to_all(packed, NEAR, 0, 0)]
    ppermute x1, starting transfers between devices: 4.37 us -> 2.07 us  [body(): arrived = lax.ppermute(send, 'core', [(0, 1), (1, 0)])]
    ppermute x3, waiting for transfers between devices: 3.91 us -> 5.78 us  [body(): lax.ppermute(sent[step - 1], 'yh', [(i, (i + step) % tall) for i in range...]
  transfers between devices with their start and end apart: 5 -> 6, of which waited for: 2 -> 4; matrix products, arithmetic and copies ran while one was open for 0% -> 0% of each run, Pallas kernels for 6% -> 7%
where the time goes in v7:
time: 88.9 us; the launch traced here: 88.4 us
  blocking collectives  29.2 us (33%)
  starting transfers between devices  27.9 us (31%)
  waiting for transfers between devices  16.5 us (19%)
  Pallas kernels  8.3 us (9%)
  local copies, waits for them, and re-layouts  5.67 us (6%)
    all_gather x1, blocking collectives, body(): full_grad = lax.all_gather(d_out, TENSOR, axis=0, tiled=True)  29.2 us
    ppermute x3, starting transfers between devices, body(): lax.ppermute(sent[step - 1], 'yh', [(i, (i + step) % tall) for i in range...  12.7 us
    all_to_all x1, starting transfers between devices, body(): terms = lax.all_to_all(plane, FAR, 0, 0)  9.43 us
    all_to_all x1, waiting for transfers between devices, body(): pieces = lax.all_to_all(packed, NEAR, 0, 0)  9.13 us
    pallas_call x7, Pallas kernels, call(): pl.pallas_call(kernel, out_shape=outs, in_specs=specs, out_specs=tuple((p...  8.3 us
    ppermute x3, waiting for transfers between devices, body(): lax.ppermute(sent[step - 1], 'yh', [(i, (i + step) % tall) for i in range...  5.78 us
    unnamed x16, local copies, waits for them, and re-layouts  5.67 us
    all_to_all x1, starting transfers between devices, body(): pieces = lax.all_to_all(packed, NEAR, 0, 0)  3.71 us
  transfers between devices with their start and end apart: 6, of which 4 were waited for; matrix products, arithmetic and copies ran while one was open for 0% of the time, Pallas kernels for 7%

profile of v7, /device:TPU:1, one launch (start us, length us, event | category | flops | bytes accessed | tf_op | source)
XLA Modules:
  0.0 88.4 jit_solution(9054449288530742018)
XLA Ops:
  0.6 29.2 %all_gather.3.d_ref = bf16[128,2560]{1,0:T(8,128)(2,1)S(1)} all-gather(bf16[16,2560]{1,0:T(8,128)(2,1)} %param.5), channel_id=1, replica_groups=mesh['yl'=2,'x'=4,'z'=16,'yh'=4,'core'=2] {'yh','core'}, dimensions={0}, use_global_device_ids=true | all-gather | bytes 737280 | tf_op jit(solution)/shard_map/all_gather | solution.py:142
  29.9 0.9 %copy-done.4 = bf16[128,384]{1,0:T(8,128)(2,1)S(1)} copy-done((bf16[128,384]{1,0:T(8,128)(2,1)S(1)}, bf16[128,384]{1,0:T(8,128)(2,1)}, u32[]{:S(2)}) %copy-start.4) | copy-done | bytes 98328
  30.8 0.1 shard_map.58
  30.9 1.2 %copy-done.1 = bf16[8,256,384]{2,1,0:T(8,128)(2,1)} copy-done((bf16[8,256,384]{2,1,0:T(8,128)(2,1)}, bf16[8,256,384]{2,1,0:T(8,128)(2,1)S(1)}, u32[]{:S(2)}) %copy-start.1) | copy-done | bytes 1572888
  32.1 0.8 copy-done.2
  32.9 3.7 %all-to-all-start = ((bf16[8,256,384]{2,1,0:T(8,128)(2,1)}), bf16[8,256,384]{2,1,0:T(8,128)(2,1)S(1)}, u32[]{:S(2)}, u32[]{:S(2)}) async-start(bf16[8,256,384]{2,1,0:T(8,128)(2,1)} %copy-done.1), calls=%async_computation | async-start | bytes 3145728 | tf_op jit(solution)/shard_map/all_to_all | solution.py:145
  36.7 1.1 %copy-done.3 = bf16[128,2560]{1,0:T(8,128)(2,1)S(1)} copy-done((bf16[128,2560]{1,0:T(8,128)(2,1)S(1)}, bf16[128,2560]{1,0:T(8,128)(2,1)}, u32[]{:S(2)}) %copy-start.3) | copy-done | bytes 655384
  37.8 1.1 %shard_map.59 = bf16[128,384]{1,0:T(8,128)(2,1)} custom-call(bf16[128,2560]{1,0:T(8,128)(2,1)S(1)} %copy-done.3, bf16[2560,384]{1,0:T(8,128)(2,1)S(1)} %copy-done), custom_call_target="tpu_custom_call" | custom-call | flops 251658240 | bytes 2719744 | tf_op jit(solution)/shard_map/pallas_call | solution.py:25
  38.9 3.7 %shard_map.60 = (bf16[4,16,2560]{2,1,0:T(8,128)(2,1)S(1)}, bf16[4,16,2560]{2,1,0:T(8,128)(2,1)}) custom-call(s32[1]{0:T(128)} %bitcast.1.core_ref, bf16[128,384]{1,0:T(8,128)(2,1)S(1)} %copy-done.5, bf16[2560,384]{1,0:T(8,128)(2,1)S(1)} %copy-done), custom_call_target="tpu_custom_call" | custom-call | flops 503316480 | bytes 2719744 | tf_op jit(solution)/shard_map/pallas_call | solution.py:25
  42.6 0.7 copy-done.6
  43.3 2.1 %collective-permute-start = (bf16[4,16,2560]{2,1,0:T(8,128)(2,1)}, bf16[4,16,2560]{2,1,0:T(8,128)(2,1)S(1)}, u32[]{:S(2)}, u32[]{:S(2)}) collective-permute-start(bf16[4,16,2560]{2,1,0:T(8,128)(2,1)} %get-tuple-element.25), channel_id=1, source_target_pairs={{0,1},{1,0},{2,3},{3,2},{4,5},{5,4},{6,7},{7,6},{8,9},{9,8},{10,11... | collective-permute-start | bytes 983048 | tf_op jit(solution)/shard_map/ppermute | solution.py:155
  45.4 1.6 %collective-permute-done.arrived_ref = bf16[4,16,2560]{2,1,0:T(8,128)(2,1)S(1)} collective-permute-done((bf16[4,16,2560]{2,1,0:T(8,128)(2,1)}, bf16[4,16,2560]{2,1,0:T(8,128)(2,1)S(1)}, u32[]{:S(2)}, u32[]{:S(2)}) %collective-permute-start) | collective-permute-done | bytes 327712 | tf_op jit(solution)/shard_map/ppermute | solution.py:155
  47.0 1.0 %copy-done.7 = bf16[4,16,2560]{2,1,0:T(8,128)(2,1)S(1)} copy-done((bf16[4,16,2560]{2,1,0:T(8,128)(2,1)S(1)}, bf16[4,16,2560]{2,1,0:T(8,128)(2,1)}, u32[]{:S(2)}) %copy-start.7) | copy-done | bytes 327704
  48.0 0.1 shard_map.61
  48.1 9.1 %all-to-all-done.near_ref = bf16[8,256,384]{2,1,0:T(8,128)(2,1)S(1)} async-done(((bf16[8,256,384]{2,1,0:T(8,128)(2,1)}), bf16[8,256,384]{2,1,0:T(8,128)(2,1)S(1)}, u32[]{:S(2)}, u32[]{:S(2)}) %all-to-all-start) | async-done | bytes 1572896 | tf_op jit(solution)/shard_map/all_to_all | solution.py:145
  57.2 1.3 %shard_map.62 = bf16[16,60,128]{2,1,0:T(8,128)(2,1)} custom-call(s32[1]{0:T(128)} %bitcast.2.odd_ref, bf16[8,256,384]{2,1,0:T(8,128)(2,1)S(1)} %all-to-all-done.near_ref), custom_call_target="tpu_custom_call" | custom-call | flops 301989888 | bytes 1818624 | tf_op jit(solution)/shard_map/pallas_call | solution.py:25
  58.5 9.4 %all-to-all-start.1 = ((bf16[16,60,128]{2,1,0:T(8,128)(2,1)}), bf16[16,60,128]{2,1,0:T(8,128)(2,1)S(1)}, u32[]{:S(2)}, u32[]{:S(2)}) async-start(bf16[16,60,128]{2,1,0:T(8,128)(2,1)} %shard_map.62), calls=%async_computation.1 | async-start | bytes 524288 | tf_op jit(solution)/shard_map/all_to_all | solution.py:168
  67.9 2.8 %collective-permute-start.1 = (bf16[16,2560]{1,0:T(8,128)(2,1)S(1)}, bf16[16,2560]{1,0:T(8,128)(2,1)S(1)}, u32[]{:S(2)}, u32[]{:S(2)}) collective-permute-start(bf16[16,2560]{1,0:T(8,128)(2,1)S(1)} %get-tuple-element.36), channel_id=1, source_target_pairs={{0,2},{2,4},{4,6},{6,0},{1,3},{3,5},{5,7},{7,1},{8,10},{10,12},{12... | collective-permute-start | bytes 245768 | tf_op jit(solution)/shard_map/ppermute | solution.py:172
  70.7 4.7 %collective-permute-start.2 = (bf16[16,2560]{1,0:T(8,128)(2,1)S(1)}, bf16[16,2560]{1,0:T(8,128)(2,1)S(1)}, u32[]{:S(2)}, u32[]{:S(2)}) collective-permute-start(bf16[16,2560]{1,0:T(8,128)(2,1)S(1)} %get-tuple-element.37), channel_id=1, source_target_pairs={{0,4},{2,6},{4,0},{6,2},{1,5},{3,7},{5,1},{7,3},{8,12},{10,14},{12... | collective-permute-start | bytes 245768 | tf_op jit(solution)/shard_map/ppermute | solution.py:172
  75.4 5.2 %collective-permute-start.3 = (bf16[16,2560]{1,0:T(8,128)(2,1)S(1)}, bf16[16,2560]{1,0:T(8,128)(2,1)S(1)}, u32[]{:S(2)}, u32[]{:S(2)}) collective-permute-start(bf16[16,2560]{1,0:T(8,128)(2,1)S(1)} %get-tuple-element.38), channel_id=1, source_target_pairs={{0,6},{2,0},{4,2},{6,4},{1,7},{3,1},{5,3},{7,5},{8,14},{10,8},{12,... | collective-permute-start | bytes 245768 | tf_op jit(solution)/shard_map/ppermute | solution.py:172
  80.7 0.4 collective-permute-done.2.b_ref
  81.1 5.4 %collective-permute-done.3.c_ref = bf16[16,2560]{1,0:T(8,128)(2,1)S(1)} collective-permute-done((bf16[16,2560]{1,0:T(8,128)(2,1)S(1)}, bf16[16,2560]{1,0:T(8,128)(2,1)S(1)}, u32[]{:S(2)}, u32[]{:S(2)}) %collective-permute-start.3) | collective-permute-done | bytes 81952 | tf_op jit(solution)/shard_map/ppermute | solution.py:172
  86.5 1.3 %shard_map.63 = bf16[16,2560]{1,0:T(8,128)(2,1)} custom-call(f32[16,2560]{1,0:T(8,128)S(1)} %get-tuple-element.26.own_ref, bf16[16,2560]{1,0:T(8,128)(2,1)S(1)} %collective-permute-done.1.a_ref, bf16[16,2560]{1,0:T(8,128)(2,1)S(1)} %collective-permute-done.2.b_ref, bf16[16,2560]{1,0:T(8,128)(2,1)S(1)} %collective-permute-done.3.c_ref), custom_call_target="tpu_custom_call" | custom-call | bytes 491520 | tf_op jit(solution)/shard_map/pallas_call | solution.py:25
  87.8 0.7 shard_map.64
  (12 shorter events, 0.0 us)
Async XLA Ops:
  29.9 0.9 %copy-start.4 = (bf16[128,384]{1,0:T(8,128)(2,1)S(1)}, bf16[128,384]{1,0:T(8,128)(2,1)}, u32[]{:S(2)}) copy-start(bf16[128,384]{1,0:T(8,128)(2,1)} %attn_ref.2) | copy-start | bytes 294916
  30.9 1.2 %copy-start.1 = (bf16[8,256,384]{2,1,0:T(8,128)(2,1)}, bf16[8,256,384]{2,1,0:T(8,128)(2,1)S(1)}, u32[]{:S(2)}) copy-start(bf16[8,256,384]{2,1,0:T(8,128)(2,1)S(1)} %shard_map.58) | copy-start | bytes 4718596
  32.1 0.8 copy-start.2
  32.9 3.7 %copy-start = (bf16[2560,384]{1,0:T(8,128)(2,1)S(1)}, bf16[2560,384]{1,0:T(8,128)(2,1)}, u32[]{:S(2)}) copy-start(bf16[2560,384]{1,0:T(8,128)(2,1)} %weight_ref.3) | copy-start | bytes 5898244
  32.9 24.3 %all-to-all-start = ((bf16[8,256,384]{2,1,0:T(8,128)(2,1)}), bf16[8,256,384]{2,1,0:T(8,128)(2,1)S(1)}, u32[]{:S(2)}, u32[]{:S(2)}) async-start(bf16[8,256,384]{2,1,0:T(8,128)(2,1)} %copy-done.1), calls=%async_computation | async-start | bytes 3145728 | tf_op jit(solution)/shard_map/all_to_all | solution.py:145
  36.7 1.1 %copy-start.3 = (bf16[128,2560]{1,0:T(8,128)(2,1)S(1)}, bf16[128,2560]{1,0:T(8,128)(2,1)}, u32[]{:S(2)}) copy-start(bf16[128,2560]{1,0:T(8,128)(2,1)} %copy-done.2) | copy-start | bytes 1966084
  37.7 1.2 %copy-start.5 = (bf16[128,384]{1,0:T(8,128)(2,1)S(1)}, bf16[128,384]{1,0:T(8,128)(2,1)}, u32[]{:S(2)}) copy-start(bf16[128,384]{1,0:T(8,128)(2,1)} %attn_ref.2) | copy-start | bytes 294916
  42.6 0.7 copy-start.6
  43.3 3.7 %collective-permute-start = (bf16[4,16,2560]{2,1,0:T(8,128)(2,1)}, bf16[4,16,2560]{2,1,0:T(8,128)(2,1)S(1)}, u32[]{:S(2)}, u32[]{:S(2)}) collective-permute-start(bf16[4,16,2560]{2,1,0:T(8,128)(2,1)} %get-tuple-element.25), channel_id=1, source_target_pairs={{0,1},{1,0},{2,3},{3,2},{4,5},{5,4},{6,7},{7,6},{8,9},{9,8},{10,11... | collective-permute-start | bytes 983048 | tf_op jit(solution)/shard_map/ppermute | solution.py:155
  47.0 1.0 %copy-start.7 = (bf16[4,16,2560]{2,1,0:T(8,128)(2,1)S(1)}, bf16[4,16,2560]{2,1,0:T(8,128)(2,1)}, u32[]{:S(2)}) copy-start(bf16[4,16,2560]{2,1,0:T(8,128)(2,1)} %copy-done.6) | copy-start | bytes 983044
  58.5 29.3 %all-to-all-start.1 = ((bf16[16,60,128]{2,1,0:T(8,128)(2,1)}), bf16[16,60,128]{2,1,0:T(8,128)(2,1)S(1)}, u32[]{:S(2)}, u32[]{:S(2)}) async-start(bf16[16,60,128]{2,1,0:T(8,128)(2,1)} %shard_map.62), calls=%async_computation.1 | async-start | bytes 524288 | tf_op jit(solution)/shard_map/all_to_all | solution.py:168
  67.9 12.7 %collective-permute-start.1 = (bf16[16,2560]{1,0:T(8,128)(2,1)S(1)}, bf16[16,2560]{1,0:T(8,128)(2,1)S(1)}, u32[]{:S(2)}, u32[]{:S(2)}) collective-permute-start(bf16[16,2560]{1,0:T(8,128)(2,1)S(1)} %get-tuple-element.36), channel_id=1, source_target_pairs={{0,2},{2,4},{4,6},{6,0},{1,3},{3,5},{5,7},{7,1},{8,10},{10,12},{12... | collective-permute-start | bytes 245768 | tf_op jit(solution)/shard_map/ppermute | solution.py:172
  70.7 10.4 %collective-permute-start.2 = (bf16[16,2560]{1,0:T(8,128)(2,1)S(1)}, bf16[16,2560]{1,0:T(8,128)(2,1)S(1)}, u32[]{:S(2)}, u32[]{:S(2)}) collective-permute-start(bf16[16,2560]{1,0:T(8,128)(2,1)S(1)} %get-tuple-element.37), channel_id=1, source_target_pairs={{0,4},{2,6},{4,0},{6,2},{1,5},{3,7},{5,1},{7,3},{8,12},{10,14},{12... | collective-permute-start | bytes 245768 | tf_op jit(solution)/shard_map/ppermute | solution.py:172
  75.4 11.0 %collective-permute-start.3 = (bf16[16,2560]{1,0:T(8,128)(2,1)S(1)}, bf16[16,2560]{1,0:T(8,128)(2,1)S(1)}, u32[]{:S(2)}, u32[]{:S(2)}) collective-permute-start(bf16[16,2560]{1,0:T(8,128)(2,1)S(1)} %get-tuple-element.38), channel_id=1, source_target_pairs={{0,6},{2,0},{4,2},{6,4},{1,7},{3,1},{5,3},{7,5},{8,14},{10,8},{12,... | collective-permute-start | bytes 245768 | tf_op jit(solution)/shard_map/ppermute | solution.py:172

commit v8 on v7

--- a/solution.py
+++ b/solution.py
@@ -53,12 +53,43 @@
     return turned * (BLK**-0.5)
 
 
-def pack_kernel(attn_ref, d_ref, out_ref):
-    count = attn_ref.shape[0]
+def pack_kernel(attn_ref, d_ref, out_ref, attn_here, d_here, sems):
+    count = attn_here.shape[0]
+    first = pltpu.make_async_copy(attn_ref, attn_here, sems.at[0])
+    second = pltpu.make_async_copy(d_ref, d_here, sems.at[1])
+    first.start()
+    second.start()
+    copies = []
     for i in range(CHUNKS):
-        start = i * 320 // BLK * BLK
-        out_ref[i, :count, :] = attn_ref[...]
-        out_ref[i, count:, :] = d_ref[:, start : start + WINDOW]
+        copies.append((attn_here, out_ref.at[i, pl.ds(0, count), :]))
+    for i in range(CHUNKS):
+        window = d_here.at[:, pl.ds(i * 320 // BLK * BLK, WINDOW)]
+        copies.append((window, out_ref.at[i, pl.ds(count, count), :]))
+    copies = [pltpu.make_async_copy(a, b, sems.at[2 + k]) for k, (a, b) in enumerate(copies)]
+    first.wait()
+    for copy in copies[:CHUNKS]:
+        copy.start()
+    second.wait()
+    for copy in copies[CHUNKS:]:
+        copy.start()
+    for copy in copies:
+        copy.wait()
+
+
+def pack(attn, full_grad):
+    out = shape((CHUNKS, 2 * attn.shape[0], attn.shape[1]), bf16)
+    return pl.pallas_call(
+        pack_kernel,
+        out_shape=out,
+        in_specs=[pl.BlockSpec(memory_space=pltpu.HBM)] * 2,
+        out_specs=pl.BlockSpec(memory_space=pltpu.HBM),
+        scratch_shapes=[
+            pltpu.VMEM(attn.shape, bf16),
+            pltpu.VMEM(full_grad.shape, bf16),
+            pltpu.SemaphoreType.DMA((2 + 2 * CHUNKS,)),
+        ],
+        cost_estimate=pl.CostEstimate(flops=0, bytes_accessed=3 * out.size, transcendentals=0),
+    )(attn, full_grad)
 
 
 def values_kernel(core_ref, attn_ref, weight_ref, keep_ref, send_ref):
@@ -140,7 +171,7 @@
     odd = lax.rem(lax.axis_index("x"), 2)
 
     full_grad = lax.all_gather(d_out, TENSOR, axis=0, tiled=True)
-    (packed,) = call(pack_kernel, (shape((near, 2 * count, width), bf16),), (), attn, full_grad)
+    packed = pack(attn, full_grad)
     packed, attn = lax.optimization_barrier((packed, attn))
     pieces = lax.all_to_all(packed, NEAR, 0, 0)
 

time: 88.9 us -> 89.2 us (level)
  local copies, waits for them, and re-layouts: 5.67 us -> 2.8 us
  Pallas kernels: 8.3 us -> 10.4 us
  blocking collectives: 29.2 us -> 30.3 us
    unnamed x16 -> x10, local copies, waits for them, and re-layouts: 5.67 us -> 2.8 us
    pallas_call x0 -> x1, Pallas kernels: none -> 2.22 us  [pack(): pl.pallas_call(pack_kernel, out_shape=out, in_specs=[pl.BlockSpec(memory_...]
    all_gather x1, blocking collectives: 29.2 us -> 30.3 us  [body(): full_grad = lax.all_gather(d_out, TENSOR, axis=0, tiled=True)]
    pallas_call x7 -> x6, Pallas kernels: 8.3 us -> 8.19 us  [call(): pl.pallas_call(kernel, out_shape=outs, in_specs=specs, out_specs=tuple((p...]
where the time goes in v8:
time: 89.2 us; the launch traced here: 88.7 us
  blocking collectives  30.3 us (34%)
  starting transfers between devices  27.5 us (31%)
  waiting for transfers between devices  16.9 us (19%)
  Pallas kernels  10.4 us (12%)
  local copies, waits for them, and re-layouts  2.8 us (3%)
    all_gather x1, blocking collectives, body(): full_grad = lax.all_gather(d_out, TENSOR, axis=0, tiled=True)  30.3 us
    ppermute x3, starting transfers between devices, body(): lax.ppermute(sent[step - 1], 'yh', [(i, (i + step) % tall) for i in range...  12.4 us
    all_to_all x1, starting transfers between devices, body(): terms = lax.all_to_all(plane, FAR, 0, 0)  9.34 us
    all_to_all x1, waiting for transfers between devices, body(): pieces = lax.all_to_all(packed, NEAR, 0, 0)  9.1 us
    pallas_call x6, Pallas kernels, call(): pl.pallas_call(kernel, out_shape=outs, in_specs=specs, out_specs=tuple((p...  8.19 us
    ppermute x3, waiting for transfers between devices, body(): lax.ppermute(sent[step - 1], 'yh', [(i, (i + step) % tall) for i in range...  6.13 us
    all_to_all x1, starting transfers between devices, body(): pieces = lax.all_to_all(packed, NEAR, 0, 0)  3.72 us
    unnamed x10, local copies, waits for them, and re-layouts  2.8 us
  transfers between devices with their start and end apart: 6, of which 4 were waited for; matrix products, arithmetic and copies ran while one was open for 0% of the time, Pallas kernels for 7%

profile of v8, /device:TPU:1, one launch (start us, length us, event | category | flops | bytes accessed | tf_op | source)
XLA Modules:
  0.0 88.7 jit_solution(9789537753424422163)
XLA Ops:
  0.6 30.3 %all_gather.3.d_ref = bf16[128,2560]{1,0:T(8,128)(2,1)} all-gather(bf16[16,2560]{1,0:T(8,128)(2,1)} %param.5), channel_id=1, replica_groups=mesh['yl'=2,'x'=4,'z'=16,'yh'=4,'core'=2] {'yh','core'}, dimensions={0}, use_global_device_ids=true | all-gather | bytes 737280 | tf_op jit(solution)/shard_map/all_gather | solution.py:173
  31.0 2.2 %shard_map.58 = bf16[8,256,384]{2,1,0:T(8,128)(2,1)} custom-call(bf16[128,384]{1,0:T(8,128)(2,1)} %attn_ref.2, bf16[128,2560]{1,0:T(8,128)(2,1)} %all_gather.3.d_ref), custom_call_target="tpu_custom_call" | custom-call | bytes 2359296 | tf_op jit(solution)/shard_map/pallas_call | solution.py:81
  33.2 0.0 copy-start
  33.2 3.7 %all-to-all-start = ((bf16[8,256,384]{2,1,0:T(8,128)(2,1)}), bf16[8,256,384]{2,1,0:T(8,128)(2,1)S(1)}, u32[]{:S(2)}, u32[]{:S(2)}) async-start(bf16[8,256,384]{2,1,0:T(8,128)(2,1)} %shard_map.58), calls=%async_computation | async-start | bytes 3145728 | tf_op jit(solution)/shard_map/all_to_all | solution.py:176
  37.0 1.1 %copy-done.1 = bf16[128,2560]{1,0:T(8,128)(2,1)S(1)} copy-done((bf16[128,2560]{1,0:T(8,128)(2,1)S(1)}, bf16[128,2560]{1,0:T(8,128)(2,1)}, u32[]{:S(2)}) %copy-start.1) | copy-done | bytes 655384
  38.0 1.1 %shard_map.59 = bf16[128,384]{1,0:T(8,128)(2,1)} custom-call(bf16[128,2560]{1,0:T(8,128)(2,1)S(1)} %copy-done.1, bf16[2560,384]{1,0:T(8,128)(2,1)S(1)} %copy-done), custom_call_target="tpu_custom_call" | custom-call | flops 251658240 | bytes 2719744 | tf_op jit(solution)/shard_map/pallas_call | solution.py:25
  39.2 3.7 %shard_map.60 = (bf16[4,16,2560]{2,1,0:T(8,128)(2,1)S(1)}, bf16[4,16,2560]{2,1,0:T(8,128)(2,1)}) custom-call(s32[1]{0:T(128)} %bitcast.1.core_ref, bf16[128,384]{1,0:T(8,128)(2,1)S(1)} %copy-done.2, bf16[2560,384]{1,0:T(8,128)(2,1)S(1)} %copy-done), custom_call_target="tpu_custom_call" | custom-call | flops 503316480 | bytes 2719744 | tf_op jit(solution)/shard_map/pallas_call | solution.py:25
  42.9 0.7 copy-done.3
  43.6 2.1 %collective-permute-start = (bf16[4,16,2560]{2,1,0:T(8,128)(2,1)}, bf16[4,16,2560]{2,1,0:T(8,128)(2,1)S(1)}, u32[]{:S(2)}, u32[]{:S(2)}) collective-permute-start(bf16[4,16,2560]{2,1,0:T(8,128)(2,1)} %get-tuple-element.25), channel_id=1, source_target_pairs={{0,1},{1,0},{2,3},{3,2},{4,5},{5,4},{6,7},{7,6},{8,9},{9,8},{10,11... | collective-permute-start | bytes 983048 | tf_op jit(solution)/shard_map/ppermute | solution.py:186
  45.7 1.6 %collective-permute-done.arrived_ref = bf16[4,16,2560]{2,1,0:T(8,128)(2,1)S(1)} collective-permute-done((bf16[4,16,2560]{2,1,0:T(8,128)(2,1)}, bf16[4,16,2560]{2,1,0:T(8,128)(2,1)S(1)}, u32[]{:S(2)}, u32[]{:S(2)}) %collective-permute-start) | collective-permute-done | bytes 327712 | tf_op jit(solution)/shard_map/ppermute | solution.py:186
  47.3 1.0 %copy-done.4 = bf16[4,16,2560]{2,1,0:T(8,128)(2,1)S(1)} copy-done((bf16[4,16,2560]{2,1,0:T(8,128)(2,1)S(1)}, bf16[4,16,2560]{2,1,0:T(8,128)(2,1)}, u32[]{:S(2)}) %copy-start.4) | copy-done | bytes 327704
  48.3 0.1 shard_map.61
  48.4 9.1 %all-to-all-done.near_ref = bf16[8,256,384]{2,1,0:T(8,128)(2,1)S(1)} async-done(((bf16[8,256,384]{2,1,0:T(8,128)(2,1)}), bf16[8,256,384]{2,1,0:T(8,128)(2,1)S(1)}, u32[]{:S(2)}, u32[]{:S(2)}) %all-to-all-start) | async-done | bytes 1572896 | tf_op jit(solution)/shard_map/all_to_all | solution.py:176
  57.5 1.3 %shard_map.62 = bf16[16,60,128]{2,1,0:T(8,128)(2,1)} custom-call(s32[1]{0:T(128)} %bitcast.2.odd_ref, bf16[8,256,384]{2,1,0:T(8,128)(2,1)S(1)} %all-to-all-done.near_ref), custom_call_target="tpu_custom_call" | custom-call | flops 301989888 | bytes 1818624 | tf_op jit(solution)/shard_map/pallas_call | solution.py:25
  58.8 9.3 %all-to-all-start.1 = ((bf16[16,60,128]{2,1,0:T(8,128)(2,1)}), bf16[16,60,128]{2,1,0:T(8,128)(2,1)S(1)}, u32[]{:S(2)}, u32[]{:S(2)}) async-start(bf16[16,60,128]{2,1,0:T(8,128)(2,1)} %shard_map.62), calls=%async_computation.1 | async-start | bytes 524288 | tf_op jit(solution)/shard_map/all_to_all | solution.py:199
  68.1 2.8 %collective-permute-start.1 = (bf16[16,2560]{1,0:T(8,128)(2,1)S(1)}, bf16[16,2560]{1,0:T(8,128)(2,1)S(1)}, u32[]{:S(2)}, u32[]{:S(2)}) collective-permute-start(bf16[16,2560]{1,0:T(8,128)(2,1)S(1)} %get-tuple-element.36), channel_id=1, source_target_pairs={{0,2},{2,4},{4,6},{6,0},{1,3},{3,5},{5,7},{7,1},{8,10},{10,12},{12... | collective-permute-start | bytes 245768 | tf_op jit(solution)/shard_map/ppermute | solution.py:203
  71.0 4.7 %collective-permute-start.2 = (bf16[16,2560]{1,0:T(8,128)(2,1)S(1)}, bf16[16,2560]{1,0:T(8,128)(2,1)S(1)}, u32[]{:S(2)}, u32[]{:S(2)}) collective-permute-start(bf16[16,2560]{1,0:T(8,128)(2,1)S(1)} %get-tuple-element.37), channel_id=1, source_target_pairs={{0,4},{2,6},{4,0},{6,2},{1,5},{3,7},{5,1},{7,3},{8,12},{10,14},{12... | collective-permute-start | bytes 245768 | tf_op jit(solution)/shard_map/ppermute | solution.py:203
  75.7 4.9 %collective-permute-start.3 = (bf16[16,2560]{1,0:T(8,128)(2,1)S(1)}, bf16[16,2560]{1,0:T(8,128)(2,1)S(1)}, u32[]{:S(2)}, u32[]{:S(2)}) collective-permute-start(bf16[16,2560]{1,0:T(8,128)(2,1)S(1)} %get-tuple-element.38), channel_id=1, source_target_pairs={{0,6},{2,0},{4,2},{6,4},{1,7},{3,1},{5,3},{7,5},{8,14},{10,8},{12,... | collective-permute-start | bytes 245768 | tf_op jit(solution)/shard_map/ppermute | solution.py:203
  80.6 0.0 collective-permute-done.1.a_ref
  80.6 0.9 collective-permute-done.2.b_ref
  81.5 5.2 %collective-permute-done.3.c_ref = bf16[16,2560]{1,0:T(8,128)(2,1)S(1)} collective-permute-done((bf16[16,2560]{1,0:T(8,128)(2,1)S(1)}, bf16[16,2560]{1,0:T(8,128)(2,1)S(1)}, u32[]{:S(2)}, u32[]{:S(2)}) %collective-permute-start.3) | collective-permute-done | bytes 81952 | tf_op jit(solution)/shard_map/ppermute | solution.py:203
  86.7 1.3 %shard_map.63 = bf16[16,2560]{1,0:T(8,128)(2,1)} custom-call(f32[16,2560]{1,0:T(8,128)S(1)} %get-tuple-element.26.own_ref, bf16[16,2560]{1,0:T(8,128)(2,1)S(1)} %collective-permute-done.1.a_ref, bf16[16,2560]{1,0:T(8,128)(2,1)S(1)} %collective-permute-done.2.b_ref, bf16[16,2560]{1,0:T(8,128)(2,1)S(1)} %collective-permute-done.3.c_ref), custom_call_target="tpu_custom_call" | custom-call | bytes 491520 | tf_op jit(solution)/shard_map/pallas_call | solution.py:25
  88.0 0.0 all-to-all-done.1.pieces_ref
  88.0 0.7 shard_map.64
  (6 shorter events, 0.0 us)
Async XLA Ops:
  33.2 3.7 %copy-start = (bf16[2560,384]{1,0:T(8,128)(2,1)S(1)}, bf16[2560,384]{1,0:T(8,128)(2,1)}, u32[]{:S(2)}) copy-start(bf16[2560,384]{1,0:T(8,128)(2,1)} %weight_ref.3) | copy-start | bytes 5898244
  33.2 24.3 %all-to-all-start = ((bf16[8,256,384]{2,1,0:T(8,128)(2,1)}), bf16[8,256,384]{2,1,0:T(8,128)(2,1)S(1)}, u32[]{:S(2)}, u32[]{:S(2)}) async-start(bf16[8,256,384]{2,1,0:T(8,128)(2,1)} %shard_map.58), calls=%async_computation | async-start | bytes 3145728 | tf_op jit(solution)/shard_map/all_to_all | solution.py:176
  36.9 1.1 %copy-start.1 = (bf16[128,2560]{1,0:T(8,128)(2,1)S(1)}, bf16[128,2560]{1,0:T(8,128)(2,1)}, u32[]{:S(2)}) copy-start(bf16[128,2560]{1,0:T(8,128)(2,1)} %all_gather.3.d_ref) | copy-start | bytes 1966084
  38.0 1.1 %copy-start.2 = (bf16[128,384]{1,0:T(8,128)(2,1)S(1)}, bf16[128,384]{1,0:T(8,128)(2,1)}, u32[]{:S(2)}) copy-start(bf16[128,384]{1,0:T(8,128)(2,1)} %attn_ref.2) | copy-start | bytes 294916
  42.9 0.7 copy-start.3
  43.6 3.7 %collective-permute-start = (bf16[4,16,2560]{2,1,0:T(8,128)(2,1)}, bf16[4,16,2560]{2,1,0:T(8,128)(2,1)S(1)}, u32[]{:S(2)}, u32[]{:S(2)}) collective-permute-start(bf16[4,16,2560]{2,1,0:T(8,128)(2,1)} %get-tuple-element.25), channel_id=1, source_target_pairs={{0,1},{1,0},{2,3},{3,2},{4,5},{5,4},{6,7},{7,6},{8,9},{9,8},{10,11... | collective-permute-start | bytes 983048 | tf_op jit(solution)/shard_map/ppermute | solution.py:186
  47.3 1.0 %copy-start.4 = (bf16[4,16,2560]{2,1,0:T(8,128)(2,1)S(1)}, bf16[4,16,2560]{2,1,0:T(8,128)(2,1)}, u32[]{:S(2)}) copy-start(bf16[4,16,2560]{2,1,0:T(8,128)(2,1)} %copy-done.3) | copy-start | bytes 983044
  58.8 29.2 %all-to-all-start.1 = ((bf16[16,60,128]{2,1,0:T(8,128)(2,1)}), bf16[16,60,128]{2,1,0:T(8,128)(2,1)S(1)}, u32[]{:S(2)}, u32[]{:S(2)}) async-start(bf16[16,60,128]{2,1,0:T(8,128)(2,1)} %shard_map.62), calls=%async_computation.1 | async-start | bytes 524288 | tf_op jit(solution)/shard_map/all_to_all | solution.py:199
  68.1 12.4 %collective-permute-start.1 = (bf16[16,2560]{1,0:T(8,128)(2,1)S(1)}, bf16[16,2560]{1,0:T(8,128)(2,1)S(1)}, u32[]{:S(2)}, u32[]{:S(2)}) collective-permute-start(bf16[16,2560]{1,0:T(8,128)(2,1)S(1)} %get-tuple-element.36), channel_id=1, source_target_pairs={{0,2},{2,4},{4,6},{6,0},{1,3},{3,5},{5,7},{7,1},{8,10},{10,12},{12... | collective-permute-start | bytes 245768 | tf_op jit(solution)/shard_map/ppermute | solution.py:203
  71.0 10.5 %collective-permute-start.2 = (bf16[16,2560]{1,0:T(8,128)(2,1)S(1)}, bf16[16,2560]{1,0:T(8,128)(2,1)S(1)}, u32[]{:S(2)}, u32[]{:S(2)}) collective-permute-start(bf16[16,2560]{1,0:T(8,128)(2,1)S(1)} %get-tuple-element.37), channel_id=1, source_target_pairs={{0,4},{2,6},{4,0},{6,2},{1,5},{3,7},{5,1},{7,3},{8,12},{10,14},{12... | collective-permute-start | bytes 245768 | tf_op jit(solution)/shard_map/ppermute | solution.py:203
  75.7 11.1 %collective-permute-start.3 = (bf16[16,2560]{1,0:T(8,128)(2,1)S(1)}, bf16[16,2560]{1,0:T(8,128)(2,1)S(1)}, u32[]{:S(2)}, u32[]{:S(2)}) collective-permute-start(bf16[16,2560]{1,0:T(8,128)(2,1)S(1)} %get-tuple-element.38), channel_id=1, source_target_pairs={{0,6},{2,0},{4,2},{6,4},{1,7},{3,1},{5,3},{7,5},{8,14},{10,8},{12,... | collective-permute-start | bytes 245768 | tf_op jit(solution)/shard_map/ppermute | solution.py:203

commit v9 on v8

--- a/solution.py
+++ b/solution.py
@@ -53,42 +53,60 @@
     return turned * (BLK**-0.5)
 
 
-def pack_kernel(attn_ref, d_ref, out_ref, attn_here, d_here, sems):
-    count = attn_here.shape[0]
+def pack_kernel(attn_ref, d_ref, out_ref, grads_ref, attn_here, d_here, stage_a, stage_d, sems):
+    count, width = attn_here.shape
+    half = count // 2
     first = pltpu.make_async_copy(attn_ref, attn_here, sems.at[0])
     second = pltpu.make_async_copy(d_ref, d_here, sems.at[1])
     first.start()
     second.start()
     copies = []
+
+    def send(source, target):
+        copies.append(pltpu.make_async_copy(source, target, sems.at[2 + len(copies)]))
+        copies[-1].start()
+
+    first.wait()
+    for c in range(width // BLK):
+        stage_a[c * count : (c + 1) * count, :] = attn_here[:, c * BLK : (c + 1) * BLK]
     for i in range(CHUNKS):
-        copies.append((attn_here, out_ref.at[i, pl.ds(0, count), :]))
+        send(stage_a, out_ref.at[i, pl.ds(0, stage_a.shape[0]), :])
+    second.wait()
+    send(d_here, grads_ref)
+    low = lax.broadcasted_iota(jnp.int32, (half, BLK), 1) < BLK // 2
     for i in range(CHUNKS):
-        window = d_here.at[:, pl.ds(i * 320 // BLK * BLK, WINDOW)]
-        copies.append((window, out_ref.at[i, pl.ds(count, count), :]))
-    copies = [pltpu.make_async_copy(a, b, sems.at[2 + k]) for k, (a, b) in enumerate(copies)]
-    first.wait()
-    for copy in copies[:CHUNKS]:
-        copy.start()
-    second.wait()
-    for copy in copies[CHUNKS:]:
-        copy.start()
+        pair = i // 2 * 5 * BLK
+        for k in range(2):
+            start = pair + (3 * BLK if i % 2 else 0) + k * BLK
+            stage_d[i, k * count : (k + 1) * count, :] = d_here[:, start : start + BLK]
+        tile = d_here[:, pair + 2 * BLK : pair + 3 * BLK].astype(f32)
+        top, bottom = tile[:half], tile[half:]
+        if i % 2:
+            fold = jnp.where(low, pltpu.roll(top, BLK // 2, 1), bottom)
+        else:
+            fold = jnp.where(low, top, pltpu.roll(bottom, BLK // 2, 1))
+        stage_d[i, 2 * count :, :] = fold.astype(bf16)
+        send(stage_d.at[i], out_ref.at[i, pl.ds(stage_a.shape[0], stage_d.shape[1]), :])
     for copy in copies:
         copy.wait()
 
 
 def pack(attn, full_grad):
-    out = shape((CHUNKS, 2 * attn.shape[0], attn.shape[1]), bf16)
+    (count, width), features = attn.shape, full_grad.shape[1]
+    lines = (count * width // BLK, count * features // CHUNKS // BLK)
     return pl.pallas_call(
         pack_kernel,
-        out_shape=out,
+        out_shape=(shape((CHUNKS, sum(lines), BLK), bf16), shape(full_grad.shape, bf16)),
         in_specs=[pl.BlockSpec(memory_space=pltpu.HBM)] * 2,
-        out_specs=pl.BlockSpec(memory_space=pltpu.HBM),
+        out_specs=(pl.BlockSpec(memory_space=pltpu.HBM),) * 2,
         scratch_shapes=[
             pltpu.VMEM(attn.shape, bf16),
             pltpu.VMEM(full_grad.shape, bf16),
-            pltpu.SemaphoreType.DMA((2 + 2 * CHUNKS,)),
+            pltpu.VMEM((lines[0], BLK), bf16),
+            pltpu.VMEM((CHUNKS, lines[1], BLK), bf16),
+            pltpu.SemaphoreType.DMA((3 + 2 * CHUNKS,)),
         ],
-        cost_estimate=pl.CostEstimate(flops=0, bytes_accessed=3 * out.size, transcendentals=0),
+        cost_estimate=pl.CostEstimate(flops=0, bytes_accessed=10**7, transcendentals=0),
     )(attn, full_grad)
 
 
@@ -132,13 +150,27 @@
 
 
 def grad_kernel(odd_ref, near_ref, out_ref):
-    near, count = near_ref.shape[0], near_ref.shape[1] // 2
-    left = jnp.concatenate([near_ref[p, count:, :] for p in range(near)], axis=0)
-    right = jnp.concatenate([near_ref[p, :count, :] for p in range(near)], axis=0)
-    term = lax.dot_general(left, right, (((0,), (0,)), ((), ())), preferred_element_type=f32)
-    far, size = out_ref.shape[0], out_ref.shape[1] * BLK // term.shape[1]
-    chunk = far * size
-    term = jnp.where(odd_ref[0] == 1, term[WINDOW - chunk :, :], term[:chunk, :])
+    far, size = out_ref.shape[0], out_ref.shape[1] * BLK // WINDOW
+    near, count, tiles = near_ref.shape[0], BLK, WINDOW // BLK
+    half = count // 2
+
+    def piece(p, k):
+        return near_ref[p, k * count : (k + 1) * count, :]
+
+    def times(left, right):
+        return lax.dot_general(left, right, (((0,), (0,)), ((), ())), preferred_element_type=f32)
+
+    attns = [jnp.concatenate([piece(p, k) for k in range(tiles)], axis=1) for p in range(near)]
+    whole = jnp.concatenate(
+        [jnp.concatenate([piece(p, tiles), piece(p, tiles + 1)], axis=1) for p in range(near)], axis=0
+    )
+    whole = times(whole, jnp.concatenate(attns, axis=0))
+    folds = jnp.concatenate([near_ref[p, (tiles + 2) * count :, :] for p in range(near)], axis=0)
+    top = times(folds, jnp.concatenate([a[:half] for a in attns], axis=0))
+    bottom = times(folds, jnp.concatenate([a[half:] for a in attns], axis=0))
+    rest = top[: BLK // 2] + bottom[BLK // 2 :]
+    even, odd = jnp.concatenate([whole, rest], axis=0), jnp.concatenate([rest, whole], axis=0)
+    term = jnp.where(odd_ref[0] == 1, odd, even)
     for z in range(far):
         block = term[z * size : (z + 1) * size, :]
         parts = [block[:, c : c + BLK] for c in range(0, term.shape[1], BLK)]
@@ -171,7 +203,7 @@
     odd = lax.rem(lax.axis_index("x"), 2)
 
     full_grad = lax.all_gather(d_out, TENSOR, axis=0, tiled=True)
-    packed = pack(attn, full_grad)
+    packed, full_grad = pack(attn, full_grad)
     packed, attn = lax.optimization_barrier((packed, attn))
     pieces = lax.all_to_all(packed, NEAR, 0, 0)
 

time: 89.2 us -> 88 us (0.987)
  waiting for transfers between devices: 16.9 us -> 15.5 us
    all_to_all x1, waiting for transfers between devices: 9.1 us -> 7.68 us  [body(): pieces = lax.all_to_all(packed, NEAR, 0, 0)]
where the time goes in v9:
time: 88 us; the launch traced here: 87.5 us
  blocking collectives  30.3 us (34%)
  starting transfers between devices  27.5 us (31%)
  waiting for transfers between devices  15.5 us (18%)
  Pallas kernels  10.6 us (12%)
  local copies, waits for them, and re-layouts  2.82 us (3%)
    all_gather x1, blocking collectives, body(): full_grad = lax.all_gather(d_out, TENSOR, axis=0, tiled=True)  30.3 us
    ppermute x3, starting transfers between devices, body(): lax.ppermute(sent[step - 1], 'yh', [(i, (i + step) % tall) for i in range...  12.4 us
    all_to_all x1, starting transfers between devices, body(): terms = lax.all_to_all(plane, FAR, 0, 0)  9.34 us
    pallas_call x6, Pallas kernels, call(): pl.pallas_call(kernel, out_shape=outs, in_specs=specs, out_specs=tuple((p...  8.2 us
    all_to_all x1, waiting for transfers between devices, body(): pieces = lax.all_to_all(packed, NEAR, 0, 0)  7.68 us
    ppermute x3, waiting for transfers between devices, body(): lax.ppermute(sent[step - 1], 'yh', [(i, (i + step) % tall) for i in range...  6.13 us
    all_to_all x1, starting transfers between devices, body(): pieces = lax.all_to_all(packed, NEAR, 0, 0)  3.72 us
    unnamed x10, local copies, waits for them, and re-layouts  2.82 us
  transfers between devices with their start and end apart: 6, of which 4 were waited for; matrix products, arithmetic and copies ran while one was open for 0% of the time, Pallas kernels for 7%

profile of v9, /device:TPU:1, one launch (start us, length us, event | category | flops | bytes accessed | tf_op | source)
XLA Modules:
  0.0 87.5 jit_solution(5832946031794847463)
XLA Ops:
  0.6 30.3 %all_gather.3.d_ref = bf16[128,2560]{1,0:T(8,128)(2,1)} all-gather(bf16[16,2560]{1,0:T(8,128)(2,1)} %param.5), channel_id=1, replica_groups=mesh['yl'=2,'x'=4,'z'=16,'yh'=4,'core'=2] {'yh','core'}, dimensions={0}, use_global_device_ids=true | all-gather | bytes 737280 | tf_op jit(solution)/shard_map/all_gather | solution.py:205
  31.0 2.4 %shard_map.58 = (bf16[8,704,128]{2,1,0:T(8,128)(2,1)}, bf16[128,2560]{1,0:T(8,128)(2,1)}) custom-call(bf16[128,384]{1,0:T(8,128)(2,1)} %attn_ref.2, bf16[128,2560]{1,0:T(8,128)(2,1)} %all_gather.3.d_ref), custom_call_target="tpu_custom_call" | custom-call | bytes 10000000 | tf_op jit(solution)/shard_map/pallas_call | solution.py:97
  33.4 0.0 copy-start
  33.4 0.0 copy-start.2
  33.4 3.7 %all-to-all-start = ((bf16[8,704,128]{2,1,0:T(8,128)(2,1)}), bf16[8,704,128]{2,1,0:T(8,128)(2,1)S(1)}, u32[]{:S(2)}, u32[]{:S(2)}) async-start(bf16[8,704,128]{2,1,0:T(8,128)(2,1)} %get-tuple-element.31), calls=%async_computation | async-start | bytes 2883584 | tf_op jit(solution)/shard_map/all_to_all | solution.py:208
  37.1 1.1 %copy-done.1 = bf16[128,2560]{1,0:T(8,128)(2,1)S(1)} copy-done((bf16[128,2560]{1,0:T(8,128)(2,1)S(1)}, bf16[128,2560]{1,0:T(8,128)(2,1)}, u32[]{:S(2)}) %copy-start.1) | copy-done | bytes 655384
  38.2 1.1 %shard_map.59 = bf16[128,384]{1,0:T(8,128)(2,1)} custom-call(bf16[128,2560]{1,0:T(8,128)(2,1)S(1)} %copy-done.1, bf16[2560,384]{1,0:T(8,128)(2,1)S(1)} %copy-done), custom_call_target="tpu_custom_call" | custom-call | flops 251658240 | bytes 2719744 | tf_op jit(solution)/shard_map/pallas_call | solution.py:25
  39.4 3.7 %shard_map.60 = (bf16[4,16,2560]{2,1,0:T(8,128)(2,1)S(1)}, bf16[4,16,2560]{2,1,0:T(8,128)(2,1)}) custom-call(s32[1]{0:T(128)} %bitcast.1.core_ref, bf16[128,384]{1,0:T(8,128)(2,1)S(1)} %copy-done.2, bf16[2560,384]{1,0:T(8,128)(2,1)S(1)} %copy-done), custom_call_target="tpu_custom_call" | custom-call | flops 503316480 | bytes 2719744 | tf_op jit(solution)/shard_map/pallas_call | solution.py:25
  43.0 0.8 copy-done.3
  43.8 2.1 %collective-permute-start = (bf16[4,16,2560]{2,1,0:T(8,128)(2,1)}, bf16[4,16,2560]{2,1,0:T(8,128)(2,1)S(1)}, u32[]{:S(2)}, u32[]{:S(2)}) collective-permute-start(bf16[4,16,2560]{2,1,0:T(8,128)(2,1)} %get-tuple-element.29), channel_id=1, source_target_pairs={{0,1},{1,0},{2,3},{3,2},{4,5},{5,4},{6,7},{7,6},{8,9},{9,8},{10,11... | collective-permute-start | bytes 983048 | tf_op jit(solution)/shard_map/ppermute | solution.py:218
  45.9 1.6 %collective-permute-done.arrived_ref = bf16[4,16,2560]{2,1,0:T(8,128)(2,1)S(1)} collective-permute-done((bf16[4,16,2560]{2,1,0:T(8,128)(2,1)}, bf16[4,16,2560]{2,1,0:T(8,128)(2,1)S(1)}, u32[]{:S(2)}, u32[]{:S(2)}) %collective-permute-start) | collective-permute-done | bytes 327712 | tf_op jit(solution)/shard_map/ppermute | solution.py:218
  47.5 1.0 %copy-done.4 = bf16[4,16,2560]{2,1,0:T(8,128)(2,1)S(1)} copy-done((bf16[4,16,2560]{2,1,0:T(8,128)(2,1)S(1)}, bf16[4,16,2560]{2,1,0:T(8,128)(2,1)}, u32[]{:S(2)}) %copy-start.4) | copy-done | bytes 327704
  48.5 0.1 shard_map.61
  48.6 7.7 %all-to-all-done.near_ref = bf16[8,704,128]{2,1,0:T(8,128)(2,1)S(1)} async-done(((bf16[8,704,128]{2,1,0:T(8,128)(2,1)}), bf16[8,704,128]{2,1,0:T(8,128)(2,1)S(1)}, u32[]{:S(2)}, u32[]{:S(2)}) %all-to-all-start) | async-done | bytes 1441824 | tf_op jit(solution)/shard_map/all_to_all | solution.py:208
  56.3 1.3 %shard_map.62 = bf16[16,60,128]{2,1,0:T(8,128)(2,1)} custom-call(s32[1]{0:T(128)} %bitcast.2.odd_ref, bf16[8,704,128]{2,1,0:T(8,128)(2,1)S(1)} %all-to-all-done.near_ref), custom_call_target="tpu_custom_call" | custom-call | flops 301989888 | bytes 1687552 | tf_op jit(solution)/shard_map/pallas_call | solution.py:25
  57.6 9.3 %all-to-all-start.1 = ((bf16[16,60,128]{2,1,0:T(8,128)(2,1)}), bf16[16,60,128]{2,1,0:T(8,128)(2,1)S(1)}, u32[]{:S(2)}, u32[]{:S(2)}) async-start(bf16[16,60,128]{2,1,0:T(8,128)(2,1)} %shard_map.62), calls=%async_computation.1 | async-start | bytes 524288 | tf_op jit(solution)/shard_map/all_to_all | solution.py:231
  66.9 2.8 %collective-permute-start.1 = (bf16[16,2560]{1,0:T(8,128)(2,1)S(1)}, bf16[16,2560]{1,0:T(8,128)(2,1)S(1)}, u32[]{:S(2)}, u32[]{:S(2)}) collective-permute-start(bf16[16,2560]{1,0:T(8,128)(2,1)S(1)} %get-tuple-element.40), channel_id=1, source_target_pairs={{0,2},{2,4},{4,6},{6,0},{1,3},{3,5},{5,7},{7,1},{8,10},{10,12},{12... | collective-permute-start | bytes 245768 | tf_op jit(solution)/shard_map/ppermute | solution.py:235
  69.8 4.7 %collective-permute-start.2 = (bf16[16,2560]{1,0:T(8,128)(2,1)S(1)}, bf16[16,2560]{1,0:T(8,128)(2,1)S(1)}, u32[]{:S(2)}, u32[]{:S(2)}) collective-permute-start(bf16[16,2560]{1,0:T(8,128)(2,1)S(1)} %get-tuple-element.41), channel_id=1, source_target_pairs={{0,4},{2,6},{4,0},{6,2},{1,5},{3,7},{5,1},{7,3},{8,12},{10,14},{12... | collective-permute-start | bytes 245768 | tf_op jit(solution)/shard_map/ppermute | solution.py:235
  74.4 4.9 %collective-permute-start.3 = (bf16[16,2560]{1,0:T(8,128)(2,1)S(1)}, bf16[16,2560]{1,0:T(8,128)(2,1)S(1)}, u32[]{:S(2)}, u32[]{:S(2)}) collective-permute-start(bf16[16,2560]{1,0:T(8,128)(2,1)S(1)} %get-tuple-element.42), channel_id=1, source_target_pairs={{0,6},{2,0},{4,2},{6,4},{1,7},{3,1},{5,3},{7,5},{8,14},{10,8},{12,... | collective-permute-start | bytes 245768 | tf_op jit(solution)/shard_map/ppermute | solution.py:235
  79.4 0.0 collective-permute-done.1.a_ref
  79.4 0.9 %collective-permute-done.2.b_ref = bf16[16,2560]{1,0:T(8,128)(2,1)S(1)} collective-permute-done((bf16[16,2560]{1,0:T(8,128)(2,1)S(1)}, bf16[16,2560]{1,0:T(8,128)(2,1)S(1)}, u32[]{:S(2)}, u32[]{:S(2)}) %collective-permute-start.2) | collective-permute-done | bytes 81952 | tf_op jit(solution)/shard_map/ppermute | solution.py:235
  80.3 5.2 %collective-permute-done.3.c_ref = bf16[16,2560]{1,0:T(8,128)(2,1)S(1)} collective-permute-done((bf16[16,2560]{1,0:T(8,128)(2,1)S(1)}, bf16[16,2560]{1,0:T(8,128)(2,1)S(1)}, u32[]{:S(2)}, u32[]{:S(2)}) %collective-permute-start.3) | collective-permute-done | bytes 81952 | tf_op jit(solution)/shard_map/ppermute | solution.py:235
  85.5 1.3 %shard_map.63 = bf16[16,2560]{1,0:T(8,128)(2,1)} custom-call(f32[16,2560]{1,0:T(8,128)S(1)} %get-tuple-element.30.own_ref, bf16[16,2560]{1,0:T(8,128)(2,1)S(1)} %collective-permute-done.1.a_ref, bf16[16,2560]{1,0:T(8,128)(2,1)S(1)} %collective-permute-done.2.b_ref, bf16[16,2560]{1,0:T(8,128)(2,1)S(1)} %collective-permute-done.3.c_ref), custom_call_target="tpu_custom_call" | custom-call | bytes 491520 | tf_op jit(solution)/shard_map/pallas_call | solution.py:25
  86.8 0.7 shard_map.64
  (6 shorter events, 0.0 us)
Async XLA Ops:
  33.4 3.8 %copy-start = (bf16[2560,384]{1,0:T(8,128)(2,1)S(1)}, bf16[2560,384]{1,0:T(8,128)(2,1)}, u32[]{:S(2)}) copy-start(bf16[2560,384]{1,0:T(8,128)(2,1)} %weight_ref.3) | copy-start | bytes 5898244
  33.4 6.0 %copy-start.2 = (bf16[128,384]{1,0:T(8,128)(2,1)S(1)}, bf16[128,384]{1,0:T(8,128)(2,1)}, u32[]{:S(2)}) copy-start(bf16[128,384]{1,0:T(8,128)(2,1)} %attn_ref.2) | copy-start | bytes 294916
  33.4 22.9 %all-to-all-start = ((bf16[8,704,128]{2,1,0:T(8,128)(2,1)}), bf16[8,704,128]{2,1,0:T(8,128)(2,1)S(1)}, u32[]{:S(2)}, u32[]{:S(2)}) async-start(bf16[8,704,128]{2,1,0:T(8,128)(2,1)} %get-tuple-element.31), calls=%async_computation | async-start | bytes 2883584 | tf_op jit(solution)/shard_map/all_to_all | solution.py:208
  37.1 1.1 %copy-start.1 = (bf16[128,2560]{1,0:T(8,128)(2,1)S(1)}, bf16[128,2560]{1,0:T(8,128)(2,1)}, u32[]{:S(2)}) copy-start(bf16[128,2560]{1,0:T(8,128)(2,1)} %get-tuple-element.26.d_ref) | copy-start | bytes 1966084
  43.0 0.8 copy-start.3
  43.8 3.7 %collective-permute-start = (bf16[4,16,2560]{2,1,0:T(8,128)(2,1)}, bf16[4,16,2560]{2,1,0:T(8,128)(2,1)S(1)}, u32[]{:S(2)}, u32[]{:S(2)}) collective-permute-start(bf16[4,16,2560]{2,1,0:T(8,128)(2,1)} %get-tuple-element.29), channel_id=1, source_target_pairs={{0,1},{1,0},{2,3},{3,2},{4,5},{5,4},{6,7},{7,6},{8,9},{9,8},{10,11... | collective-permute-start | bytes 983048 | tf_op jit(solution)/shard_map/ppermute | solution.py:218
  47.5 1.0 %copy-start.4 = (bf16[4,16,2560]{2,1,0:T(8,128)(2,1)S(1)}, bf16[4,16,2560]{2,1,0:T(8,128)(2,1)}, u32[]{:S(2)}) copy-start(bf16[4,16,2560]{2,1,0:T(8,128)(2,1)} %copy-done.3) | copy-start | bytes 983044
  57.6 29.2 %all-to-all-start.1 = ((bf16[16,60,128]{2,1,0:T(8,128)(2,1)}), bf16[16,60,128]{2,1,0:T(8,128)(2,1)S(1)}, u32[]{:S(2)}, u32[]{:S(2)}) async-start(bf16[16,60,128]{2,1,0:T(8,128)(2,1)} %shard_map.62), calls=%async_computation.1 | async-start | bytes 524288 | tf_op jit(solution)/shard_map/all_to_all | solution.py:231
  66.9 12.4 %collective-permute-start.1 = (bf16[16,2560]{1,0:T(8,128)(2,1)S(1)}, bf16[16,2560]{1,0:T(8,128)(2,1)S(1)}, u32[]{:S(2)}, u32[]{:S(2)}) collective-permute-start(bf16[16,2560]{1,0:T(8,128)(2,1)S(1)} %get-tuple-element.40), channel_id=1, source_target_pairs={{0,2},{2,4},{4,6},{6,0},{1,3},{3,5},{5,7},{7,1},{8,10},{10,12},{12... | collective-permute-start | bytes 245768 | tf_op jit(solution)/shard_map/ppermute | solution.py:235
  69.8 10.5 %collective-permute-start.2 = (bf16[16,2560]{1,0:T(8,128)(2,1)S(1)}, bf16[16,2560]{1,0:T(8,128)(2,1)S(1)}, u32[]{:S(2)}, u32[]{:S(2)}) collective-permute-start(bf16[16,2560]{1,0:T(8,128)(2,1)S(1)} %get-tuple-element.41), channel_id=1, source_target_pairs={{0,4},{2,6},{4,0},{6,2},{1,5},{3,7},{5,1},{7,3},{8,12},{10,14},{12... | collective-permute-start | bytes 245768 | tf_op jit(solution)/shard_map/ppermute | solution.py:235
  74.4 11.1 %collective-permute-start.3 = (bf16[16,2560]{1,0:T(8,128)(2,1)S(1)}, bf16[16,2560]{1,0:T(8,128)(2,1)S(1)}, u32[]{:S(2)}, u32[]{:S(2)}) collective-permute-start(bf16[16,2560]{1,0:T(8,128)(2,1)S(1)} %get-tuple-element.42), channel_id=1, source_target_pairs={{0,6},{2,0},{4,2},{6,4},{1,7},{3,1},{5,3},{7,5},{8,14},{10,8},{12,... | collective-permute-start | bytes 245768 | tf_op jit(solution)/shard_map/ppermute | solution.py:235

commit v10 on v9

--- a/solution.py
+++ b/solution.py
@@ -219,7 +219,9 @@
     one = shape((rows, features), bf16)
     own, *sent = call(pair_kernel, (shape((rows, features), f32), one, one, one), (yh,), keep, arrived)
 
-    pieces, sent, d_attn = lax.optimization_barrier((pieces, sent, d_attn))
+    rings = [[(i, (i + step) % tall) for i in range(tall)] for step in range(tall)]
+    first = lax.ppermute(sent[0], "yh", rings[1])
+    pieces, first, later, d_attn = lax.optimization_barrier((pieces, first, sent[1:], d_attn))
     (plane,) = call(
         grad_kernel,
         (shape((far, features // near // far * width // BLK, BLK), bf16),),
@@ -227,12 +229,10 @@
         pieces,
         flops=2 * near * count * WINDOW * width,
     )
-    plane, sent = lax.optimization_barrier((plane, sent))
+    plane, later = lax.optimization_barrier((plane, later))
     terms = lax.all_to_all(plane, FAR, 0, 0)
 
-    blocks = []
-    for step in range(1, tall):
-        blocks.append(lax.ppermute(sent[step - 1], "yh", [(i, (i + step) % tall) for i in range(tall)]))
+    blocks = [first] + [lax.ppermute(later[step - 2], "yh", rings[step]) for step in range(2, tall)]
     (mixed,) = call(mixed_kernel, (one,), (), own, *blocks)
     (w_grad,) = call(total_kernel, (shape((features // near // far, width), f32),), (), terms)
     return (mixed, d_attn, w_grad)

time: 88 us -> 89.1 us (1.012)
  the two profiles are of different devices: /device:TPU:1 before, /device:TPU:6 now
where the time goes in v10:
time: 89.1 us; the launch traced here: 88.6 us
  starting transfers between devices  36.9 us (41%)
  blocking collectives  19.3 us (22%)
  waiting for transfers between devices  18.3 us (21%)
  Pallas kernels  10.6 us (12%)
  local copies, waits for them, and re-layouts  2.82 us (3%)
    all_gather x1, blocking collectives, body(): full_grad = lax.all_gather(d_out, TENSOR, axis=0, tiled=True)  19.3 us
    all_to_all x1, starting transfers between devices, body(): pieces = lax.all_to_all(packed, NEAR, 0, 0)  13.8 us
    all_to_all x1, starting transfers between devices, body(): terms = lax.all_to_all(plane, FAR, 0, 0)  10.8 us
    ppermute x2, starting transfers between devices, body(): lax.ppermute(later[step - 2], 'yh', rings[step])  8.43 us
    pallas_call x6, Pallas kernels, call(): pl.pallas_call(kernel, out_shape=outs, in_specs=specs, out_specs=tuple((p...  8.2 us
    ppermute x1, waiting for transfers between devices, body(): first = lax.ppermute(sent[0], 'yh', rings[1])  7.89 us
    all_to_all x1, waiting for transfers between devices, body(): terms = lax.all_to_all(plane, FAR, 0, 0)  5.04 us
    ppermute x2, waiting for transfers between devices, body(): lax.ppermute(later[step - 2], 'yh', rings[step])  3.62 us
  transfers between devices with their start and end apart: 6, of which 5 were waited for; matrix products, arithmetic and copies ran while one was open for 0% of the time, Pallas kernels for 7%

profile of v10, /device:TPU:6, one launch (start us, length us, event | category | flops | bytes accessed | tf_op | source)
XLA Modules:
  0.0 88.6 jit_solution(9287423298357433043)
XLA Ops:
  0.6 19.3 %all_gather.3.d_ref = bf16[128,2560]{1,0:T(8,128)(2,1)} all-gather(bf16[16,2560]{1,0:T(8,128)(2,1)} %param.5), channel_id=1, replica_groups=mesh['yl'=2,'x'=4,'z'=16,'yh'=4,'core'=2] {'yh','core'}, dimensions={0}, use_global_device_ids=true | all-gather | bytes 737280 | tf_op jit(solution)/shard_map/all_gather | solution.py:205
  19.9 2.4 %shard_map.58 = (bf16[8,704,128]{2,1,0:T(8,128)(2,1)}, bf16[128,2560]{1,0:T(8,128)(2,1)}) custom-call(bf16[128,384]{1,0:T(8,128)(2,1)} %attn_ref.2, bf16[128,2560]{1,0:T(8,128)(2,1)} %all_gather.3.d_ref), custom_call_target="tpu_custom_call" | custom-call | bytes 10000000 | tf_op jit(solution)/shard_map/pallas_call | solution.py:97
  22.3 0.0 copy-start
  22.3 0.0 copy-start.2
  22.3 13.8 %all-to-all-start = ((bf16[8,704,128]{2,1,0:T(8,128)(2,1)}), bf16[8,704,128]{2,1,0:T(8,128)(2,1)S(1)}, u32[]{:S(2)}, u32[]{:S(2)}) async-start(bf16[8,704,128]{2,1,0:T(8,128)(2,1)} %get-tuple-element.30), calls=%async_computation | async-start | bytes 2883584 | tf_op jit(solution)/shard_map/all_to_all | solution.py:208
  36.2 1.1 %copy-done.1 = bf16[128,2560]{1,0:T(8,128)(2,1)S(1)} copy-done((bf16[128,2560]{1,0:T(8,128)(2,1)S(1)}, bf16[128,2560]{1,0:T(8,128)(2,1)}, u32[]{:S(2)}) %copy-start.1) | copy-done | bytes 655384
  37.2 1.1 %shard_map.59 = bf16[128,384]{1,0:T(8,128)(2,1)} custom-call(bf16[128,2560]{1,0:T(8,128)(2,1)S(1)} %copy-done.1, bf16[2560,384]{1,0:T(8,128)(2,1)S(1)} %copy-done), custom_call_target="tpu_custom_call" | custom-call | flops 251658240 | bytes 2719744 | tf_op jit(solution)/shard_map/pallas_call | solution.py:25
  38.4 3.7 %shard_map.60 = (bf16[4,16,2560]{2,1,0:T(8,128)(2,1)S(1)}, bf16[4,16,2560]{2,1,0:T(8,128)(2,1)}) custom-call(s32[1]{0:T(128)} %bitcast.1.core_ref, bf16[128,384]{1,0:T(8,128)(2,1)S(1)} %copy-done.2, bf16[2560,384]{1,0:T(8,128)(2,1)S(1)} %copy-done), custom_call_target="tpu_custom_call" | custom-call | flops 503316480 | bytes 2719744 | tf_op jit(solution)/shard_map/pallas_call | solution.py:25
  42.1 0.8 copy-done.3
  42.8 2.0 %collective-permute-start = (bf16[4,16,2560]{2,1,0:T(8,128)(2,1)}, bf16[4,16,2560]{2,1,0:T(8,128)(2,1)S(1)}, u32[]{:S(2)}, u32[]{:S(2)}) collective-permute-start(bf16[4,16,2560]{2,1,0:T(8,128)(2,1)} %get-tuple-element.28), channel_id=1, source_target_pairs={{0,1},{1,0},{2,3},{3,2},{4,5},{5,4},{6,7},{7,6},{8,9},{9,8},{10,11... | collective-permute-start | bytes 983048 | tf_op jit(solution)/shard_map/ppermute | solution.py:218
  44.8 1.7 %collective-permute-done.arrived_ref = bf16[4,16,2560]{2,1,0:T(8,128)(2,1)S(1)} collective-permute-done((bf16[4,16,2560]{2,1,0:T(8,128)(2,1)}, bf16[4,16,2560]{2,1,0:T(8,128)(2,1)S(1)}, u32[]{:S(2)}, u32[]{:S(2)}) %collective-permute-start) | collective-permute-done | bytes 327712 | tf_op jit(solution)/shard_map/ppermute | solution.py:218
  46.6 1.0 %copy-done.4 = bf16[4,16,2560]{2,1,0:T(8,128)(2,1)S(1)} copy-done((bf16[4,16,2560]{2,1,0:T(8,128)(2,1)S(1)}, bf16[4,16,2560]{2,1,0:T(8,128)(2,1)}, u32[]{:S(2)}) %copy-start.4) | copy-done | bytes 327704
  47.5 0.1 shard_map.61
  47.6 1.9 %collective-permute-start.1 = (bf16[16,2560]{1,0:T(8,128)(2,1)S(1)}, bf16[16,2560]{1,0:T(8,128)(2,1)S(1)}, u32[]{:S(2)}, u32[]{:S(2)}) collective-permute-start(bf16[16,2560]{1,0:T(8,128)(2,1)S(1)} %get-tuple-element.31), channel_id=1, source_target_pairs={{0,2},{2,4},{4,6},{6,0},{1,3},{3,5},{5,7},{7,1},{8,10},{10,12},{12... | collective-permute-start | bytes 245768 | tf_op jit(solution)/shard_map/ppermute | solution.py:223
  49.5 7.9 %collective-permute-done.1.a_ref = bf16[16,2560]{1,0:T(8,128)(2,1)S(1)} collective-permute-done((bf16[16,2560]{1,0:T(8,128)(2,1)S(1)}, bf16[16,2560]{1,0:T(8,128)(2,1)S(1)}, u32[]{:S(2)}, u32[]{:S(2)}) %collective-permute-start.1) | collective-permute-done | bytes 81952 | tf_op jit(solution)/shard_map/ppermute | solution.py:223
  57.4 1.3 %shard_map.62 = bf16[16,60,128]{2,1,0:T(8,128)(2,1)} custom-call(s32[1]{0:T(128)} %bitcast.2.odd_ref, bf16[8,704,128]{2,1,0:T(8,128)(2,1)S(1)} %all-to-all-done.near_ref), custom_call_target="tpu_custom_call" | custom-call | flops 301989888 | bytes 1687552 | tf_op jit(solution)/shard_map/pallas_call | solution.py:25
  58.8 10.8 %all-to-all-start.1 = ((bf16[16,60,128]{2,1,0:T(8,128)(2,1)}), bf16[16,60,128]{2,1,0:T(8,128)(2,1)S(1)}, u32[]{:S(2)}, u32[]{:S(2)}) async-start(bf16[16,60,128]{2,1,0:T(8,128)(2,1)} %shard_map.62), calls=%async_computation.1 | async-start | bytes 524288 | tf_op jit(solution)/shard_map/all_to_all | solution.py:233
  69.5 4.8 %collective-permute-start.2 = (bf16[16,2560]{1,0:T(8,128)(2,1)S(1)}, bf16[16,2560]{1,0:T(8,128)(2,1)S(1)}, u32[]{:S(2)}, u32[]{:S(2)}) collective-permute-start(bf16[16,2560]{1,0:T(8,128)(2,1)S(1)} %get-tuple-element.39), channel_id=1, source_target_pairs={{0,4},{2,6},{4,0},{6,2},{1,5},{3,7},{5,1},{7,3},{8,12},{10,14},{12... | collective-permute-start | bytes 245768 | tf_op jit(solution)/shard_map/ppermute | solution.py:235
  74.4 3.6 %collective-permute-start.3 = (bf16[16,2560]{1,0:T(8,128)(2,1)S(1)}, bf16[16,2560]{1,0:T(8,128)(2,1)S(1)}, u32[]{:S(2)}, u32[]{:S(2)}) collective-permute-start(bf16[16,2560]{1,0:T(8,128)(2,1)S(1)} %get-tuple-element.40), channel_id=1, source_target_pairs={{0,6},{2,0},{4,2},{6,4},{1,7},{3,1},{5,3},{7,5},{8,14},{10,8},{12,... | collective-permute-start | bytes 245768 | tf_op jit(solution)/shard_map/ppermute | solution.py:235
  78.0 1.9 %collective-permute-done.2.b_ref = bf16[16,2560]{1,0:T(8,128)(2,1)S(1)} collective-permute-done((bf16[16,2560]{1,0:T(8,128)(2,1)S(1)}, bf16[16,2560]{1,0:T(8,128)(2,1)S(1)}, u32[]{:S(2)}, u32[]{:S(2)}) %collective-permute-start.2) | collective-permute-done | bytes 81952 | tf_op jit(solution)/shard_map/ppermute | solution.py:235
  79.9 1.7 %collective-permute-done.3.c_ref = bf16[16,2560]{1,0:T(8,128)(2,1)S(1)} collective-permute-done((bf16[16,2560]{1,0:T(8,128)(2,1)S(1)}, bf16[16,2560]{1,0:T(8,128)(2,1)S(1)}, u32[]{:S(2)}, u32[]{:S(2)}) %collective-permute-start.3) | collective-permute-done | bytes 81952 | tf_op jit(solution)/shard_map/ppermute | solution.py:235
  81.6 1.3 %shard_map.63 = bf16[16,2560]{1,0:T(8,128)(2,1)} custom-call(f32[16,2560]{1,0:T(8,128)S(1)} %get-tuple-element.29.own_ref, bf16[16,2560]{1,0:T(8,128)(2,1)S(1)} %collective-permute-done.1.a_ref, bf16[16,2560]{1,0:T(8,128)(2,1)S(1)} %collective-permute-done.2.b_ref, bf16[16,2560]{1,0:T(8,128)(2,1)S(1)} %collective-permute-done.3.c_ref), custom_call_target="tpu_custom_call" | custom-call | bytes 491520 | tf_op jit(solution)/shard_map/pallas_call | solution.py:25
  82.9 5.0 %all-to-all-done.1.pieces_ref = bf16[16,60,128]{2,1,0:T(8,128)(2,1)S(1)} async-done(((bf16[16,60,128]{2,1,0:T(8,128)(2,1)}), bf16[16,60,128]{2,1,0:T(8,128)(2,1)S(1)}, u32[]{:S(2)}, u32[]{:S(2)}) %all-to-all-start.1) | async-done | bytes 245792 | tf_op jit(solution)/shard_map/all_to_all | solution.py:233
  87.9 0.7 shard_map.64
  (6 shorter events, 0.0 us)
Async XLA Ops:
  22.3 13.9 %copy-start = (bf16[2560,384]{1,0:T(8,128)(2,1)S(1)}, bf16[2560,384]{1,0:T(8,128)(2,1)}, u32[]{:S(2)}) copy-start(bf16[2560,384]{1,0:T(8,128)(2,1)} %weight_ref.3) | copy-start | bytes 5898244
  22.3 16.1 %copy-start.2 = (bf16[128,384]{1,0:T(8,128)(2,1)S(1)}, bf16[128,384]{1,0:T(8,128)(2,1)}, u32[]{:S(2)}) copy-start(bf16[128,384]{1,0:T(8,128)(2,1)} %attn_ref.2) | copy-start | bytes 294916
  22.3 35.1 %all-to-all-start = ((bf16[8,704,128]{2,1,0:T(8,128)(2,1)}), bf16[8,704,128]{2,1,0:T(8,128)(2,1)S(1)}, u32[]{:S(2)}, u32[]{:S(2)}) async-start(bf16[8,704,128]{2,1,0:T(8,128)(2,1)} %get-tuple-element.30), calls=%async_computation | async-start | bytes 2883584 | tf_op jit(solution)/shard_map/all_to_all | solution.py:208
  36.1 1.1 %copy-start.1 = (bf16[128,2560]{1,0:T(8,128)(2,1)S(1)}, bf16[128,2560]{1,0:T(8,128)(2,1)}, u32[]{:S(2)}) copy-start(bf16[128,2560]{1,0:T(8,128)(2,1)} %get-tuple-element.25.d_ref) | copy-start | bytes 1966084
  42.1 0.8 copy-start.3
  42.8 3.7 %collective-permute-start = (bf16[4,16,2560]{2,1,0:T(8,128)(2,1)}, bf16[4,16,2560]{2,1,0:T(8,128)(2,1)S(1)}, u32[]{:S(2)}, u32[]{:S(2)}) collective-permute-start(bf16[4,16,2560]{2,1,0:T(8,128)(2,1)} %get-tuple-element.28), channel_id=1, source_target_pairs={{0,1},{1,0},{2,3},{3,2},{4,5},{5,4},{6,7},{7,6},{8,9},{9,8},{10,11... | collective-permute-start | bytes 983048 | tf_op jit(solution)/shard_map/ppermute | solution.py:218
  46.6 1.0 %copy-start.4 = (bf16[4,16,2560]{2,1,0:T(8,128)(2,1)S(1)}, bf16[4,16,2560]{2,1,0:T(8,128)(2,1)}, u32[]{:S(2)}) copy-start(bf16[4,16,2560]{2,1,0:T(8,128)(2,1)} %copy-done.3) | copy-start | bytes 983044
  47.6 9.8 %collective-permute-start.1 = (bf16[16,2560]{1,0:T(8,128)(2,1)S(1)}, bf16[16,2560]{1,0:T(8,128)(2,1)S(1)}, u32[]{:S(2)}, u32[]{:S(2)}) collective-permute-start(bf16[16,2560]{1,0:T(8,128)(2,1)S(1)} %get-tuple-element.31), channel_id=1, source_target_pairs={{0,2},{2,4},{4,6},{6,0},{1,3},{3,5},{5,7},{7,1},{8,10},{10,12},{12... | collective-permute-start | bytes 245768 | tf_op jit(solution)/shard_map/ppermute | solution.py:223
  58.8 29.2 %all-to-all-start.1 = ((bf16[16,60,128]{2,1,0:T(8,128)(2,1)}), bf16[16,60,128]{2,1,0:T(8,128)(2,1)S(1)}, u32[]{:S(2)}, u32[]{:S(2)}) async-start(bf16[16,60,128]{2,1,0:T(8,128)(2,1)} %shard_map.62), calls=%async_computation.1 | async-start | bytes 524288 | tf_op jit(solution)/shard_map/all_to_all | solution.py:233
  69.5 10.3 %collective-permute-start.2 = (bf16[16,2560]{1,0:T(8,128)(2,1)S(1)}, bf16[16,2560]{1,0:T(8,128)(2,1)S(1)}, u32[]{:S(2)}, u32[]{:S(2)}) collective-permute-start(bf16[16,2560]{1,0:T(8,128)(2,1)S(1)} %get-tuple-element.39), channel_id=1, source_target_pairs={{0,4},{2,6},{4,0},{6,2},{1,5},{3,7},{5,1},{7,3},{8,12},{10,14},{12... | collective-permute-start | bytes 245768 | tf_op jit(solution)/shard_map/ppermute | solution.py:235
  74.4 7.2 %collective-permute-start.3 = (bf16[16,2560]{1,0:T(8,128)(2,1)S(1)}, bf16[16,2560]{1,0:T(8,128)(2,1)S(1)}, u32[]{:S(2)}, u32[]{:S(2)}) collective-permute-start(bf16[16,2560]{1,0:T(8,128)(2,1)S(1)} %get-tuple-element.40), channel_id=1, source_target_pairs={{0,6},{2,0},{4,2},{6,4},{1,7},{3,1},{5,3},{7,5},{8,14},{10,8},{12,... | collective-permute-start | bytes 245768 | tf_op jit(solution)/shard_map/ppermute | solution.py:235

commit v11 on v9

--- a/solution.py
+++ b/solution.py
@@ -231,7 +231,7 @@
     terms = lax.all_to_all(plane, FAR, 0, 0)
 
     blocks = []
-    for step in range(1, tall):
+    for step in (2, 3, 1):
         blocks.append(lax.ppermute(sent[step - 1], "yh", [(i, (i + step) % tall) for i in range(tall)]))
     (mixed,) = call(mixed_kernel, (one,), (), own, *blocks)
     (w_grad,) = call(total_kernel, (shape((features // near // far, width), f32),), (), terms)

time: 88 us -> 86.8 us (0.986)
  the two profiles are of different devices: /device:TPU:1 before, /device:TPU:8 now
where the time goes in v11:
time: 86.8 us; the launch traced here: 86.3 us
  starting transfers between devices  38.6 us (44%)
  blocking collectives  18.1 us (21%)
  waiting for transfers between devices  15.4 us (18%)
  Pallas kernels  10.6 us (12%)
  local copies, waits for them, and re-layouts  2.82 us (3%)
    all_gather x1, blocking collectives, body(): full_grad = lax.all_gather(d_out, TENSOR, axis=0, tiled=True)  18.1 us
    all_to_all x1, starting transfers between devices, body(): pieces = lax.all_to_all(packed, NEAR, 0, 0)  14.9 us
    ppermute x3, starting transfers between devices, body(): lax.ppermute(sent[step - 1], 'yh', [(i, (i + step) % tall) for i in range...  12.1 us
    all_to_all x1, starting transfers between devices, body(): terms = lax.all_to_all(plane, FAR, 0, 0)  9.63 us
    pallas_call x6, Pallas kernels, call(): pl.pallas_call(kernel, out_shape=outs, in_specs=specs, out_specs=tuple((p...  8.2 us
    all_to_all x1, waiting for transfers between devices, body(): pieces = lax.all_to_all(packed, NEAR, 0, 0)  7.81 us
    ppermute x3, waiting for transfers between devices, body(): lax.ppermute(sent[step - 1], 'yh', [(i, (i + step) % tall) for i in range...  5.86 us
    unnamed x10, local copies, waits for them, and re-layouts  2.82 us
  transfers between devices with their start and end apart: 6, of which 4 were waited for; matrix products, arithmetic and copies ran while one was open for 0% of the time, Pallas kernels for 7%

profile of v11, /device:TPU:8, one launch (start us, length us, event | category | flops | bytes accessed | tf_op | source)
XLA Modules:
  0.0 86.3 jit_solution(6197915490240583245)
XLA Ops:
  0.6 18.1 %all_gather.3.d_ref = bf16[128,2560]{1,0:T(8,128)(2,1)} all-gather(bf16[16,2560]{1,0:T(8,128)(2,1)} %param.5), channel_id=1, replica_groups=mesh['yl'=2,'x'=4,'z'=16,'yh'=4,'core'=2] {'yh','core'}, dimensions={0}, use_global_device_ids=true | all-gather | bytes 737280 | tf_op jit(solution)/shard_map/all_gather | solution.py:205
  18.8 2.4 %shard_map.58 = (bf16[8,704,128]{2,1,0:T(8,128)(2,1)}, bf16[128,2560]{1,0:T(8,128)(2,1)}) custom-call(bf16[128,384]{1,0:T(8,128)(2,1)} %attn_ref.2, bf16[128,2560]{1,0:T(8,128)(2,1)} %all_gather.3.d_ref), custom_call_target="tpu_custom_call" | custom-call | bytes 10000000 | tf_op jit(solution)/shard_map/pallas_call | solution.py:97
  21.2 0.0 copy-start
  21.2 0.0 copy-start.2
  21.2 14.9 %all-to-all-start = ((bf16[8,704,128]{2,1,0:T(8,128)(2,1)}), bf16[8,704,128]{2,1,0:T(8,128)(2,1)S(1)}, u32[]{:S(2)}, u32[]{:S(2)}) async-start(bf16[8,704,128]{2,1,0:T(8,128)(2,1)} %get-tuple-element.31), calls=%async_computation | async-start | bytes 2883584 | tf_op jit(solution)/shard_map/all_to_all | solution.py:208
  36.1 1.1 %copy-done.1 = bf16[128,2560]{1,0:T(8,128)(2,1)S(1)} copy-done((bf16[128,2560]{1,0:T(8,128)(2,1)S(1)}, bf16[128,2560]{1,0:T(8,128)(2,1)}, u32[]{:S(2)}) %copy-start.1) | copy-done | bytes 655384
  37.2 1.1 %shard_map.59 = bf16[128,384]{1,0:T(8,128)(2,1)} custom-call(bf16[128,2560]{1,0:T(8,128)(2,1)S(1)} %copy-done.1, bf16[2560,384]{1,0:T(8,128)(2,1)S(1)} %copy-done), custom_call_target="tpu_custom_call" | custom-call | flops 251658240 | bytes 2719744 | tf_op jit(solution)/shard_map/pallas_call | solution.py:25
  38.4 3.7 %shard_map.60 = (bf16[4,16,2560]{2,1,0:T(8,128)(2,1)S(1)}, bf16[4,16,2560]{2,1,0:T(8,128)(2,1)}) custom-call(s32[1]{0:T(128)} %bitcast.1.core_ref, bf16[128,384]{1,0:T(8,128)(2,1)S(1)} %copy-done.2, bf16[2560,384]{1,0:T(8,128)(2,1)S(1)} %copy-done), custom_call_target="tpu_custom_call" | custom-call | flops 503316480 | bytes 2719744 | tf_op jit(solution)/shard_map/pallas_call | solution.py:25
  42.1 0.8 copy-done.3
  42.8 2.0 %collective-permute-start = (bf16[4,16,2560]{2,1,0:T(8,128)(2,1)}, bf16[4,16,2560]{2,1,0:T(8,128)(2,1)S(1)}, u32[]{:S(2)}, u32[]{:S(2)}) collective-permute-start(bf16[4,16,2560]{2,1,0:T(8,128)(2,1)} %get-tuple-element.29), channel_id=1, source_target_pairs={{0,1},{1,0},{2,3},{3,2},{4,5},{5,4},{6,7},{7,6},{8,9},{9,8},{10,11... | collective-permute-start | bytes 983048 | tf_op jit(solution)/shard_map/ppermute | solution.py:218
  44.8 1.7 %collective-permute-done.arrived_ref = bf16[4,16,2560]{2,1,0:T(8,128)(2,1)S(1)} collective-permute-done((bf16[4,16,2560]{2,1,0:T(8,128)(2,1)}, bf16[4,16,2560]{2,1,0:T(8,128)(2,1)S(1)}, u32[]{:S(2)}, u32[]{:S(2)}) %collective-permute-start) | collective-permute-done | bytes 327712 | tf_op jit(solution)/shard_map/ppermute | solution.py:218
  46.5 1.0 %copy-done.4 = bf16[4,16,2560]{2,1,0:T(8,128)(2,1)S(1)} copy-done((bf16[4,16,2560]{2,1,0:T(8,128)(2,1)S(1)}, bf16[4,16,2560]{2,1,0:T(8,128)(2,1)}, u32[]{:S(2)}) %copy-start.4) | copy-done | bytes 327704
  47.5 0.1 shard_map.61
  47.6 7.8 %all-to-all-done.near_ref = bf16[8,704,128]{2,1,0:T(8,128)(2,1)S(1)} async-done(((bf16[8,704,128]{2,1,0:T(8,128)(2,1)}), bf16[8,704,128]{2,1,0:T(8,128)(2,1)S(1)}, u32[]{:S(2)}, u32[]{:S(2)}) %all-to-all-start) | async-done | bytes 1441824 | tf_op jit(solution)/shard_map/all_to_all | solution.py:208
  55.4 1.3 %shard_map.62 = bf16[16,60,128]{2,1,0:T(8,128)(2,1)} custom-call(s32[1]{0:T(128)} %bitcast.2.odd_ref, bf16[8,704,128]{2,1,0:T(8,128)(2,1)S(1)} %all-to-all-done.near_ref), custom_call_target="tpu_custom_call" | custom-call | flops 301989888 | bytes 1687552 | tf_op jit(solution)/shard_map/pallas_call | solution.py:25
  56.7 9.6 %all-to-all-start.1 = ((bf16[16,60,128]{2,1,0:T(8,128)(2,1)}), bf16[16,60,128]{2,1,0:T(8,128)(2,1)S(1)}, u32[]{:S(2)}, u32[]{:S(2)}) async-start(bf16[16,60,128]{2,1,0:T(8,128)(2,1)} %shard_map.62), calls=%async_computation.1 | async-start | bytes 524288 | tf_op jit(solution)/shard_map/all_to_all | solution.py:231
  66.4 5.3 %collective-permute-start.1 = (bf16[16,2560]{1,0:T(8,128)(2,1)S(1)}, bf16[16,2560]{1,0:T(8,128)(2,1)S(1)}, u32[]{:S(2)}, u32[]{:S(2)}) collective-permute-start(bf16[16,2560]{1,0:T(8,128)(2,1)S(1)} %get-tuple-element.40), channel_id=1, source_target_pairs={{0,4},{2,6},{4,0},{6,2},{1,5},{3,7},{5,1},{7,3},{8,12},{10,14},{12... | collective-permute-start | bytes 245768 | tf_op jit(solution)/shard_map/ppermute | solution.py:235
  71.7 3.3 %collective-permute-start.2 = (bf16[16,2560]{1,0:T(8,128)(2,1)S(1)}, bf16[16,2560]{1,0:T(8,128)(2,1)S(1)}, u32[]{:S(2)}, u32[]{:S(2)}) collective-permute-start(bf16[16,2560]{1,0:T(8,128)(2,1)S(1)} %get-tuple-element.41), channel_id=1, source_target_pairs={{0,6},{2,0},{4,2},{6,4},{1,7},{3,1},{5,3},{7,5},{8,14},{10,8},{12,... | collective-permute-start | bytes 245768 | tf_op jit(solution)/shard_map/ppermute | solution.py:235
  75.0 3.4 %collective-permute-start.3 = (bf16[16,2560]{1,0:T(8,128)(2,1)S(1)}, bf16[16,2560]{1,0:T(8,128)(2,1)S(1)}, u32[]{:S(2)}, u32[]{:S(2)}) collective-permute-start(bf16[16,2560]{1,0:T(8,128)(2,1)S(1)} %get-tuple-element.42), channel_id=1, source_target_pairs={{0,2},{2,4},{4,6},{6,0},{1,3},{3,5},{5,7},{7,1},{8,10},{10,12},{12... | collective-permute-start | bytes 245768 | tf_op jit(solution)/shard_map/ppermute | solution.py:235
  78.4 0.0 collective-permute-done.1.a_ref
  78.4 0.8 collective-permute-done.2.b_ref
  79.3 5.0 %collective-permute-done.3.c_ref = bf16[16,2560]{1,0:T(8,128)(2,1)S(1)} collective-permute-done((bf16[16,2560]{1,0:T(8,128)(2,1)S(1)}, bf16[16,2560]{1,0:T(8,128)(2,1)S(1)}, u32[]{:S(2)}, u32[]{:S(2)}) %collective-permute-start.3) | collective-permute-done | bytes 81952 | tf_op jit(solution)/shard_map/ppermute | solution.py:235
  84.3 1.3 %shard_map.63 = bf16[16,2560]{1,0:T(8,128)(2,1)} custom-call(f32[16,2560]{1,0:T(8,128)S(1)} %get-tuple-element.30.own_ref, bf16[16,2560]{1,0:T(8,128)(2,1)S(1)} %collective-permute-done.1.a_ref, bf16[16,2560]{1,0:T(8,128)(2,1)S(1)} %collective-permute-done.2.b_ref, bf16[16,2560]{1,0:T(8,128)(2,1)S(1)} %collective-permute-done.3.c_ref), custom_call_target="tpu_custom_call" | custom-call | bytes 491520 | tf_op jit(solution)/shard_map/pallas_call | solution.py:25
  85.6 0.7 shard_map.64
  (6 shorter events, 0.0 us)
Async XLA Ops:
  21.2 15.0 %copy-start = (bf16[2560,384]{1,0:T(8,128)(2,1)S(1)}, bf16[2560,384]{1,0:T(8,128)(2,1)}, u32[]{:S(2)}) copy-start(bf16[2560,384]{1,0:T(8,128)(2,1)} %weight_ref.3) | copy-start | bytes 5898244
  21.2 17.2 %copy-start.2 = (bf16[128,384]{1,0:T(8,128)(2,1)S(1)}, bf16[128,384]{1,0:T(8,128)(2,1)}, u32[]{:S(2)}) copy-start(bf16[128,384]{1,0:T(8,128)(2,1)} %attn_ref.2) | copy-start | bytes 294916
  21.2 34.2 %all-to-all-start = ((bf16[8,704,128]{2,1,0:T(8,128)(2,1)}), bf16[8,704,128]{2,1,0:T(8,128)(2,1)S(1)}, u32[]{:S(2)}, u32[]{:S(2)}) async-start(bf16[8,704,128]{2,1,0:T(8,128)(2,1)} %get-tuple-element.31), calls=%async_computation | async-start | bytes 2883584 | tf_op jit(solution)/shard_map/all_to_all | solution.py:208
  36.1 1.1 %copy-start.1 = (bf16[128,2560]{1,0:T(8,128)(2,1)S(1)}, bf16[128,2560]{1,0:T(8,128)(2,1)}, u32[]{:S(2)}) copy-start(bf16[128,2560]{1,0:T(8,128)(2,1)} %get-tuple-element.26.d_ref) | copy-start | bytes 1966084
  42.1 0.8 copy-start.3
  42.8 3.7 %collective-permute-start = (bf16[4,16,2560]{2,1,0:T(8,128)(2,1)}, bf16[4,16,2560]{2,1,0:T(8,128)(2,1)S(1)}, u32[]{:S(2)}, u32[]{:S(2)}) collective-permute-start(bf16[4,16,2560]{2,1,0:T(8,128)(2,1)} %get-tuple-element.29), channel_id=1, source_target_pairs={{0,1},{1,0},{2,3},{3,2},{4,5},{5,4},{6,7},{7,6},{8,9},{9,8},{10,11... | collective-permute-start | bytes 983048 | tf_op jit(solution)/shard_map/ppermute | solution.py:218
  46.5 1.0 %copy-start.4 = (bf16[4,16,2560]{2,1,0:T(8,128)(2,1)S(1)}, bf16[4,16,2560]{2,1,0:T(8,128)(2,1)}, u32[]{:S(2)}) copy-start(bf16[4,16,2560]{2,1,0:T(8,128)(2,1)} %copy-done.3) | copy-start | bytes 983044
  56.7 28.9 %all-to-all-start.1 = ((bf16[16,60,128]{2,1,0:T(8,128)(2,1)}), bf16[16,60,128]{2,1,0:T(8,128)(2,1)S(1)}, u32[]{:S(2)}, u32[]{:S(2)}) async-start(bf16[16,60,128]{2,1,0:T(8,128)(2,1)} %shard_map.62), calls=%async_computation.1 | async-start | bytes 524288 | tf_op jit(solution)/shard_map/all_to_all | solution.py:231
  66.4 12.1 %collective-permute-start.1 = (bf16[16,2560]{1,0:T(8,128)(2,1)S(1)}, bf16[16,2560]{1,0:T(8,128)(2,1)S(1)}, u32[]{:S(2)}, u32[]{:S(2)}) collective-permute-start(bf16[16,2560]{1,0:T(8,128)(2,1)S(1)} %get-tuple-element.40), channel_id=1, source_target_pairs={{0,4},{2,6},{4,0},{6,2},{1,5},{3,7},{5,1},{7,3},{8,12},{10,14},{12... | collective-permute-start | bytes 245768 | tf_op jit(solution)/shard_map/ppermute | solution.py:235
  71.7 7.6 %collective-permute-start.2 = (bf16[16,2560]{1,0:T(8,128)(2,1)S(1)}, bf16[16,2560]{1,0:T(8,128)(2,1)S(1)}, u32[]{:S(2)}, u32[]{:S(2)}) collective-permute-start(bf16[16,2560]{1,0:T(8,128)(2,1)S(1)} %get-tuple-element.41), channel_id=1, source_target_pairs={{0,6},{2,0},{4,2},{6,4},{1,7},{3,1},{5,3},{7,5},{8,14},{10,8},{12,... | collective-permute-start | bytes 245768 | tf_op jit(solution)/shard_map/ppermute | solution.py:235
  75.0 9.3 %collective-permute-start.3 = (bf16[16,2560]{1,0:T(8,128)(2,1)S(1)}, bf16[16,2560]{1,0:T(8,128)(2,1)S(1)}, u32[]{:S(2)}, u32[]{:S(2)}) collective-permute-start(bf16[16,2560]{1,0:T(8,128)(2,1)S(1)} %get-tuple-element.42), channel_id=1, source_target_pairs={{0,2},{2,4},{4,6},{6,0},{1,3},{3,5},{5,7},{7,1},{8,10},{10,12},{12... | collective-permute-start | bytes 245768 | tf_op jit(solution)/shard_map/ppermute | solution.py:235

commit v12 on v11

--- a/solution.py
+++ b/solution.py
@@ -141,12 +141,13 @@
 
 
 def mixed_kernel(own_ref, a_ref, b_ref, c_ref, out_ref):
-    table = signs_table()
-    for j in range(out_ref.shape[1] // BLK):
-        cols = slice(j * BLK, (j + 1) * BLK)
-        total = own_ref[:, cols] + a_ref[:, cols].astype(f32)
-        total += b_ref[:, cols].astype(f32) + c_ref[:, cols].astype(f32)
-        out_ref[:, cols] = rotate(total, table).astype(bf16)
+    rows, features = out_ref.shape
+    total = own_ref[...] + a_ref[...].astype(f32)
+    total += b_ref[...].astype(f32) + c_ref[...].astype(f32)
+    blocks = [total[:, c : c + BLK] for c in range(0, features, BLK)]
+    turned = rotate(jnp.concatenate(blocks, axis=0), signs_table()).astype(bf16)
+    for j in range(features // BLK):
+        out_ref[:, j * BLK : (j + 1) * BLK] = turned[j * rows : (j + 1) * rows, :]
 
 
 def grad_kernel(odd_ref, near_ref, out_ref):

time: 86.8 us -> 86.4 us (level)
  no operation moved by 1% of the time
where the time goes in v12:
time: 86.4 us; the launch traced here: 85.9 us
  starting transfers between devices  38.6 us (45%)
  blocking collectives  18.1 us (21%)
  waiting for transfers between devices  15.4 us (18%)
  Pallas kernels  10.2 us (12%)
  local copies, waits for them, and re-layouts  2.82 us (3%)
    all_gather x1, blocking collectives, body(): full_grad = lax.all_gather(d_out, TENSOR, axis=0, tiled=True)  18.1 us
    all_to_all x1, starting transfers between devices, body(): pieces = lax.all_to_all(packed, NEAR, 0, 0)  14.9 us
    ppermute x3, starting transfers between devices, body(): lax.ppermute(sent[step - 1], 'yh', [(i, (i + step) % tall) for i in range...  12 us
    all_to_all x1, starting transfers between devices, body(): terms = lax.all_to_all(plane, FAR, 0, 0)  9.63 us
    all_to_all x1, waiting for transfers between devices, body(): pieces = lax.all_to_all(packed, NEAR, 0, 0)  7.81 us
    pallas_call x6, Pallas kernels, call(): pl.pallas_call(kernel, out_shape=outs, in_specs=specs, out_specs=tuple((p...  7.8 us
    ppermute x3, waiting for transfers between devices, body(): lax.ppermute(sent[step - 1], 'yh', [(i, (i + step) % tall) for i in range...  5.86 us
    unnamed x10, local copies, waits for them, and re-layouts  2.82 us
  transfers between devices with their start and end apart: 6, of which 4 were waited for; matrix products, arithmetic and copies ran while one was open for 0% of the time, Pallas kernels for 7%

profile of v12, /device:TPU:8, one launch (start us, length us, event | category | flops | bytes accessed | tf_op | source)
XLA Modules:
  0.0 85.9 jit_solution(11372148526547193167)
XLA Ops:
  0.6 18.1 %all_gather.3.d_ref = bf16[128,2560]{1,0:T(8,128)(2,1)} all-gather(bf16[16,2560]{1,0:T(8,128)(2,1)} %param.5), channel_id=1, replica_groups=mesh['yl'=2,'x'=4,'z'=16,'yh'=4,'core'=2] {'yh','core'}, dimensions={0}, use_global_device_ids=true | all-gather | bytes 737280 | tf_op jit(solution)/shard_map/all_gather | solution.py:206
  18.8 2.4 %shard_map.58 = (bf16[8,704,128]{2,1,0:T(8,128)(2,1)}, bf16[128,2560]{1,0:T(8,128)(2,1)}) custom-call(bf16[128,384]{1,0:T(8,128)(2,1)} %attn_ref.2, bf16[128,2560]{1,0:T(8,128)(2,1)} %all_gather.3.d_ref), custom_call_target="tpu_custom_call" | custom-call | bytes 10000000 | tf_op jit(solution)/shard_map/pallas_call | solution.py:97
  21.2 0.0 copy-start
  21.2 0.0 copy-start.2
  21.2 14.9 %all-to-all-start = ((bf16[8,704,128]{2,1,0:T(8,128)(2,1)}), bf16[8,704,128]{2,1,0:T(8,128)(2,1)S(1)}, u32[]{:S(2)}, u32[]{:S(2)}) async-start(bf16[8,704,128]{2,1,0:T(8,128)(2,1)} %get-tuple-element.31), calls=%async_computation | async-start | bytes 2883584 | tf_op jit(solution)/shard_map/all_to_all | solution.py:209
  36.1 1.1 %copy-done.1 = bf16[128,2560]{1,0:T(8,128)(2,1)S(1)} copy-done((bf16[128,2560]{1,0:T(8,128)(2,1)S(1)}, bf16[128,2560]{1,0:T(8,128)(2,1)}, u32[]{:S(2)}) %copy-start.1) | copy-done | bytes 655384
  37.2 1.1 %shard_map.59 = bf16[128,384]{1,0:T(8,128)(2,1)} custom-call(bf16[128,2560]{1,0:T(8,128)(2,1)S(1)} %copy-done.1, bf16[2560,384]{1,0:T(8,128)(2,1)S(1)} %copy-done), custom_call_target="tpu_custom_call" | custom-call | flops 251658240 | bytes 2719744 | tf_op jit(solution)/shard_map/pallas_call | solution.py:25
  38.4 3.7 %shard_map.60 = (bf16[4,16,2560]{2,1,0:T(8,128)(2,1)S(1)}, bf16[4,16,2560]{2,1,0:T(8,128)(2,1)}) custom-call(s32[1]{0:T(128)} %bitcast.1.core_ref, bf16[128,384]{1,0:T(8,128)(2,1)S(1)} %copy-done.2, bf16[2560,384]{1,0:T(8,128)(2,1)S(1)} %copy-done), custom_call_target="tpu_custom_call" | custom-call | flops 503316480 | bytes 2719744 | tf_op jit(solution)/shard_map/pallas_call | solution.py:25
  42.1 0.8 copy-done.3
  42.8 2.0 %collective-permute-start = (bf16[4,16,2560]{2,1,0:T(8,128)(2,1)}, bf16[4,16,2560]{2,1,0:T(8,128)(2,1)S(1)}, u32[]{:S(2)}, u32[]{:S(2)}) collective-permute-start(bf16[4,16,2560]{2,1,0:T(8,128)(2,1)} %get-tuple-element.29), channel_id=1, source_target_pairs={{0,1},{1,0},{2,3},{3,2},{4,5},{5,4},{6,7},{7,6},{8,9},{9,8},{10,11... | collective-permute-start | bytes 983048 | tf_op jit(solution)/shard_map/ppermute | solution.py:219
  44.8 1.7 %collective-permute-done.arrived_ref = bf16[4,16,2560]{2,1,0:T(8,128)(2,1)S(1)} collective-permute-done((bf16[4,16,2560]{2,1,0:T(8,128)(2,1)}, bf16[4,16,2560]{2,1,0:T(8,128)(2,1)S(1)}, u32[]{:S(2)}, u32[]{:S(2)}) %collective-permute-start) | collective-permute-done | bytes 327712 | tf_op jit(solution)/shard_map/ppermute | solution.py:219
  46.5 1.0 %copy-done.4 = bf16[4,16,2560]{2,1,0:T(8,128)(2,1)S(1)} copy-done((bf16[4,16,2560]{2,1,0:T(8,128)(2,1)S(1)}, bf16[4,16,2560]{2,1,0:T(8,128)(2,1)}, u32[]{:S(2)}) %copy-start.4) | copy-done | bytes 327704
  47.5 0.1 shard_map.61
  47.6 7.8 %all-to-all-done.near_ref = bf16[8,704,128]{2,1,0:T(8,128)(2,1)S(1)} async-done(((bf16[8,704,128]{2,1,0:T(8,128)(2,1)}), bf16[8,704,128]{2,1,0:T(8,128)(2,1)S(1)}, u32[]{:S(2)}, u32[]{:S(2)}) %all-to-all-start) | async-done | bytes 1441824 | tf_op jit(solution)/shard_map/all_to_all | solution.py:209
  55.4 1.3 %shard_map.62 = bf16[16,60,128]{2,1,0:T(8,128)(2,1)} custom-call(s32[1]{0:T(128)} %bitcast.2.odd_ref, bf16[8,704,128]{2,1,0:T(8,128)(2,1)S(1)} %all-to-all-done.near_ref), custom_call_target="tpu_custom_call" | custom-call | flops 301989888 | bytes 1687552 | tf_op jit(solution)/shard_map/pallas_call | solution.py:25
  56.7 9.6 %all-to-all-start.1 = ((bf16[16,60,128]{2,1,0:T(8,128)(2,1)}), bf16[16,60,128]{2,1,0:T(8,128)(2,1)S(1)}, u32[]{:S(2)}, u32[]{:S(2)}) async-start(bf16[16,60,128]{2,1,0:T(8,128)(2,1)} %shard_map.62), calls=%async_computation.1 | async-start | bytes 524288 | tf_op jit(solution)/shard_map/all_to_all | solution.py:232
  66.4 5.3 %collective-permute-start.1 = (bf16[16,2560]{1,0:T(8,128)(2,1)S(1)}, bf16[16,2560]{1,0:T(8,128)(2,1)S(1)}, u32[]{:S(2)}, u32[]{:S(2)}) collective-permute-start(bf16[16,2560]{1,0:T(8,128)(2,1)S(1)} %get-tuple-element.40), channel_id=1, source_target_pairs={{0,4},{2,6},{4,0},{6,2},{1,5},{3,7},{5,1},{7,3},{8,12},{10,14},{12... | collective-permute-start | bytes 245768 | tf_op jit(solution)/shard_map/ppermute | solution.py:236
  71.7 3.3 %collective-permute-start.2 = (bf16[16,2560]{1,0:T(8,128)(2,1)S(1)}, bf16[16,2560]{1,0:T(8,128)(2,1)S(1)}, u32[]{:S(2)}, u32[]{:S(2)}) collective-permute-start(bf16[16,2560]{1,0:T(8,128)(2,1)S(1)} %get-tuple-element.41), channel_id=1, source_target_pairs={{0,6},{2,0},{4,2},{6,4},{1,7},{3,1},{5,3},{7,5},{8,14},{10,8},{12,... | collective-permute-start | bytes 245768 | tf_op jit(solution)/shard_map/ppermute | solution.py:236
  75.0 3.4 %collective-permute-start.3 = (bf16[16,2560]{1,0:T(8,128)(2,1)S(1)}, bf16[16,2560]{1,0:T(8,128)(2,1)S(1)}, u32[]{:S(2)}, u32[]{:S(2)}) collective-permute-start(bf16[16,2560]{1,0:T(8,128)(2,1)S(1)} %get-tuple-element.42), channel_id=1, source_target_pairs={{0,2},{2,4},{4,6},{6,0},{1,3},{3,5},{5,7},{7,1},{8,10},{10,12},{12... | collective-permute-start | bytes 245768 | tf_op jit(solution)/shard_map/ppermute | solution.py:236
  78.4 0.0 collective-permute-done.1.a_ref
  78.4 0.8 collective-permute-done.2.b_ref
  79.3 5.0 %collective-permute-done.3.c_ref = bf16[16,2560]{1,0:T(8,128)(2,1)S(1)} collective-permute-done((bf16[16,2560]{1,0:T(8,128)(2,1)S(1)}, bf16[16,2560]{1,0:T(8,128)(2,1)S(1)}, u32[]{:S(2)}, u32[]{:S(2)}) %collective-permute-start.3) | collective-permute-done | bytes 81952 | tf_op jit(solution)/shard_map/ppermute | solution.py:236
  84.3 0.9 %shard_map.63 = bf16[16,2560]{1,0:T(8,128)(2,1)} custom-call(f32[16,2560]{1,0:T(8,128)S(1)} %get-tuple-element.30.own_ref, bf16[16,2560]{1,0:T(8,128)(2,1)S(1)} %collective-permute-done.1.a_ref, bf16[16,2560]{1,0:T(8,128)(2,1)S(1)} %collective-permute-done.2.b_ref, bf16[16,2560]{1,0:T(8,128)(2,1)S(1)} %collective-permute-done.3.c_ref), custom_call_target="tpu_custom_call" | custom-call | bytes 491520 | tf_op jit(solution)/shard_map/pallas_call | solution.py:25
  85.2 0.7 shard_map.64
  (6 shorter events, 0.0 us)
Async XLA Ops:
  21.2 15.0 %copy-start = (bf16[2560,384]{1,0:T(8,128)(2,1)S(1)}, bf16[2560,384]{1,0:T(8,128)(2,1)}, u32[]{:S(2)}) copy-start(bf16[2560,384]{1,0:T(8,128)(2,1)} %weight_ref.3) | copy-start | bytes 5898244
  21.2 17.2 %copy-start.2 = (bf16[128,384]{1,0:T(8,128)(2,1)S(1)}, bf16[128,384]{1,0:T(8,128)(2,1)}, u32[]{:S(2)}) copy-start(bf16[128,384]{1,0:T(8,128)(2,1)} %attn_ref.2) | copy-start | bytes 294916
  21.2 34.2 %all-to-all-start = ((bf16[8,704,128]{2,1,0:T(8,128)(2,1)}), bf16[8,704,128]{2,1,0:T(8,128)(2,1)S(1)}, u32[]{:S(2)}, u32[]{:S(2)}) async-start(bf16[8,704,128]{2,1,0:T(8,128)(2,1)} %get-tuple-element.31), calls=%async_computation | async-start | bytes 2883584 | tf_op jit(solution)/shard_map/all_to_all | solution.py:209
  36.1 1.1 %copy-start.1 = (bf16[128,2560]{1,0:T(8,128)(2,1)S(1)}, bf16[128,2560]{1,0:T(8,128)(2,1)}, u32[]{:S(2)}) copy-start(bf16[128,2560]{1,0:T(8,128)(2,1)} %get-tuple-element.26.d_ref) | copy-start | bytes 1966084
  42.1 0.8 copy-start.3
  42.8 3.7 %collective-permute-start = (bf16[4,16,2560]{2,1,0:T(8,128)(2,1)}, bf16[4,16,2560]{2,1,0:T(8,128)(2,1)S(1)}, u32[]{:S(2)}, u32[]{:S(2)}) collective-permute-start(bf16[4,16,2560]{2,1,0:T(8,128)(2,1)} %get-tuple-element.29), channel_id=1, source_target_pairs={{0,1},{1,0},{2,3},{3,2},{4,5},{5,4},{6,7},{7,6},{8,9},{9,8},{10,11... | collective-permute-start | bytes 983048 | tf_op jit(solution)/shard_map/ppermute | solution.py:219
  46.5 1.0 %copy-start.4 = (bf16[4,16,2560]{2,1,0:T(8,128)(2,1)S(1)}, bf16[4,16,2560]{2,1,0:T(8,128)(2,1)}, u32[]{:S(2)}) copy-start(bf16[4,16,2560]{2,1,0:T(8,128)(2,1)} %copy-done.3) | copy-start | bytes 983044
  56.7 28.5 %all-to-all-start.1 = ((bf16[16,60,128]{2,1,0:T(8,128)(2,1)}), bf16[16,60,128]{2,1,0:T(8,128)(2,1)S(1)}, u32[]{:S(2)}, u32[]{:S(2)}) async-start(bf16[16,60,128]{2,1,0:T(8,128)(2,1)} %shard_map.62), calls=%async_computation.1 | async-start | bytes 524288 | tf_op jit(solution)/shard_map/all_to_all | solution.py:232
  66.4 12.1 %collective-permute-start.1 = (bf16[16,2560]{1,0:T(8,128)(2,1)S(1)}, bf16[16,2560]{1,0:T(8,128)(2,1)S(1)}, u32[]{:S(2)}, u32[]{:S(2)}) collective-permute-start(bf16[16,2560]{1,0:T(8,128)(2,1)S(1)} %get-tuple-element.40), channel_id=1, source_target_pairs={{0,4},{2,6},{4,0},{6,2},{1,5},{3,7},{5,1},{7,3},{8,12},{10,14},{12... | collective-permute-start | bytes 245768 | tf_op jit(solution)/shard_map/ppermute | solution.py:236
  71.7 7.6 %collective-permute-start.2 = (bf16[16,2560]{1,0:T(8,128)(2,1)S(1)}, bf16[16,2560]{1,0:T(8,128)(2,1)S(1)}, u32[]{:S(2)}, u32[]{:S(2)}) collective-permute-start(bf16[16,2560]{1,0:T(8,128)(2,1)S(1)} %get-tuple-element.41), channel_id=1, source_target_pairs={{0,6},{2,0},{4,2},{6,4},{1,7},{3,1},{5,3},{7,5},{8,14},{10,8},{12,... | collective-permute-start | bytes 245768 | tf_op jit(solution)/shard_map/ppermute | solution.py:236
  75.0 9.3 %collective-permute-start.3 = (bf16[16,2560]{1,0:T(8,128)(2,1)S(1)}, bf16[16,2560]{1,0:T(8,128)(2,1)S(1)}, u32[]{:S(2)}, u32[]{:S(2)}) collective-permute-start(bf16[16,2560]{1,0:T(8,128)(2,1)S(1)} %get-tuple-element.42), channel_id=1, source_target_pairs={{0,2},{2,4},{4,6},{6,0},{1,3},{3,5},{5,7},{7,1},{8,10},{10,12},{12... | collective-permute-start | bytes 245768 | tf_op jit(solution)/shard_map/ppermute | solution.py:236
